TPU v7x, 32 devices: a whole 2x2x4 slice. The times are simulated.
32 devices in a mesh: rows: 4 (over z), cols: 8 (over y, x, core).
Axes of the slice: x: 2, y: 2, z: 4, core: 2. Of those that a mesh axis runs over, the one named last changes fastest.
Arguments:
- model_dir: float32 [65536, 128], P('cols'), may hold values from -6 to 6
- sens_blocks: bfloat16 [4, 3072, 128, 128], P('rows', 'cols'), may hold values from -0.09375 to 0.09375
- blk_row: int32 [4, 3072], P('rows', 'cols'), may hold values from 0 to 31, as said below
- blk_col: int32 [4, 3072], P('rows', 'cols'), may hold values from 0 to 63, as said below
- blk_count: int32 [4, 8], P('rows', 'cols'), may hold values from 48 to 384, as said below
- send_order: int32 [8, 64], P('cols'), may hold values from 0 to 63, each once within a row
- neighbors: int32 [4, 65536], P(None, 'cols'), may hold values from 0 to 65535, as said below
- face_weight: float32 [4, 65536], P(None, 'cols'), may hold values from 0.05 to 0.5
Outputs:
- data_image: float32 [16384, 128], P('rows')
- normal_product: float32 [65536, 128], P('cols')
Inputs may be any that keep to these rules, and one draw needn't show every extreme that they name: Within one device's 384 slots the pairs (blk_row, blk_col) are all different. `blk_col`: paired with blk_row as stated there. The live slots of a device are its first blk_count slots; some device has all 384 live. `send_order`: each row is a permutation. `neighbors`: every neighbour lies within 64 of the cell's own number.
All inputs are finite; a program needn't handle non-finite values.
Results may differ from a plain program's by a relative error of at most 0.0029.
Values may be sent and summed in bfloat16 or wider, within the bound.
No kernel may reach another device: no remote copies, remote signals or barrier semaphores. Data moves between devices by JAX's collectives and lax.ppermute only.
A program may use at most 192 MiB of HBM per device.

v0:
```python
import math

import jax
import jax.numpy as jnp
import numpy as np
from jax import lax
from jax.experimental import pallas as pl
from jax.experimental.pallas import tpu as pltpu
from jax.sharding import PartitionSpec as P

BLK = 128
RB_DEV = 32
RIM = 64
STEP = 16
MIB = 1 << 20
SMALL = 16 * MIB
LARGE = 56 * MIB
ANY_SPEC = pl.BlockSpec(memory_space=pl.ANY)
VMEM_SPEC = pl.BlockSpec(memory_space=pltpu.VMEM)
SMEM_SPEC = pl.BlockSpec(memory_space=pltpu.SMEM)


def haar_matrix(order_n):
    matrix = np.ones((1, 1))
    while matrix.shape[0] < order_n:
        length = matrix.shape[0]
        upper = np.kron(matrix, np.array([[1.0, 1.0]]))
        lower = np.kron(np.eye(length), np.array([[1.0, -1.0]]))
        matrix = np.concatenate([upper, lower], axis=0) / math.sqrt(2.0)
    return matrix


def fetch(source, target, sems, pieces):
    each = source.shape[0] // pieces
    parts = [pl.ds(i * each, each) for i in range(pieces)]
    return [
        pltpu.make_async_copy(source.at[part], target.at[part], sems.at[i])
        for i, part in enumerate(parts)
    ]


def gather_pieces(sources, held_ref, me, sems):
    each = held_ref.shape[0] // len(sources)
    return [
        pltpu.make_async_copy(
            ref.at[pl.ds(first, each)],
            held_ref.at[pl.ds((me ^ offset) * each, each)],
            sems.at[offset],
        )
        for offset, (ref, first) in enumerate(sources)
    ]


def piece_stores(source, offset, even_refs, odd_ref, sems):
    each = source.shape[0]
    stride = odd_ref.shape[0] // (sems.shape[0] // 2)
    if offset % 2:
        target = odd_ref.at[pl.ds((offset // 2) * stride, each)]
    else:
        target = even_refs[offset // 2].at[pl.ds(0, each)]
    return pltpu.make_async_copy(source, target, sems.at[offset])


def start_all(copies):
    for copy in copies:
        copy.start()


def wait_all(copies):
    for copy in copies:
        copy.wait()


def analyze_body(me_ref, order_ref, model_ref, *refs):
    even_refs, (odd_ref, block_ref, coeff_ref, got, put) = refs[:-5], refs[-5:]
    width = model_ref.shape[2]
    per_peer = even_refs[0].shape[0]
    peers = put.shape[0]
    me = me_ref[0]
    loads = fetch(model_ref, block_ref, got, got.shape[0])
    start_all(loads)
    row = lax.broadcasted_iota(jnp.int32, (BLK, BLK), 0)
    col = lax.broadcasted_iota(jnp.int32, (BLK, BLK), 1)
    level = jnp.ones_like(row)
    scale = jnp.full((BLK, width), BLK**-0.5, jnp.float32)
    wide_row = lax.broadcasted_iota(jnp.int32, (BLK, width), 0)
    size = 2
    while size < BLK:
        level = jnp.where(row >= size, size, level)
        scale = jnp.where(wide_row >= size, (size / BLK) ** 0.5, scale)
        size *= 2
    span = BLK // level
    inside = col - (row - level) * span
    sign = jnp.where(inside * 2 < span, 1.0, -1.0)
    sign = jnp.where((inside >= 0) & (inside < span), sign, 0.0)
    sign = jnp.where(row == 0, 1.0, sign).astype(jnp.bfloat16)
    both_signs = jnp.concatenate([sign, sign], axis=1)
    wait_all(loads)
    stores = []
    ends = []
    for rows in (block_ref[model_ref.shape[0] - 1, BLK - RIM :], block_ref[0, :RIM]):
        high = rows.astype(jnp.bfloat16)
        low = (rows - high.astype(jnp.float32)).astype(jnp.bfloat16)
        ends.append(jnp.concatenate([high, low], axis=0))
    for offset in [*range(1, peers, 2), *range(peers - 2, -1, -2)]:
        peer = (me ^ offset) * per_peer
        for q in range(per_peer):
            x = block_ref[order_ref[0, peer + q]]
            high = x.astype(jnp.bfloat16)
            low = (x - high.astype(jnp.float32)).astype(jnp.bfloat16)
            raw = jnp.dot(
                both_signs, jnp.concatenate([high, low], axis=0),
                preferred_element_type=jnp.float32,
            )
            coeff_ref[offset, q] = (raw * scale).astype(jnp.bfloat16)
        length = per_peer
        if offset % 2:
            coeff_ref[offset, per_peer] = jnp.where(me ^ offset == me + 1, ends[0], ends[1])
            length += 1
        source = coeff_ref.at[offset, pl.ds(0, length)]
        stores.append(piece_stores(source, offset, even_refs, odd_ref, put))
        stores[-1].start()
    wait_all(stores)


def piece_shapes(piece, peers, dtype, more=0):
    half = peers // 2
    return [jax.ShapeDtypeStruct(piece, dtype)] * half + [
        jax.ShapeDtypeStruct((half * (piece[0] + more), *piece[1:]), dtype)
    ]


def analyze(me, order, model_blocks, peers):
    blocks, _, width = model_blocks.shape
    piece = (blocks // peers, BLK, width)
    return pl.pallas_call(
        analyze_body,
        out_shape=piece_shapes(piece, peers, jnp.bfloat16, 1),
        in_specs=[SMEM_SPEC, SMEM_SPEC, ANY_SPEC],
        out_specs=[ANY_SPEC] * (peers // 2 + 1),
        scratch_shapes=[
            pltpu.VMEM((blocks, BLK, width), jnp.float32),
            pltpu.VMEM((peers, piece[0] + 1, *piece[1:]), jnp.bfloat16),
            pltpu.SemaphoreType.DMA((16,)),
            pltpu.SemaphoreType.DMA((peers,)),
        ],
        compiler_params=pltpu.CompilerParams(vmem_limit_bytes=LARGE),
        cost_estimate=pl.CostEstimate(
            flops=4 * blocks * BLK * BLK * width, bytes_accessed=6 * blocks * BLK * width,
            transcendentals=0,
        ),
        name="analyze",
    )(me, order, model_blocks)


def slot_loop(count, sens_ref, block_ref, sems, others, acc_ref, work):
    steps = sems.shape[0]
    each = sens_ref.shape[0] // steps

    def block_copy(step):
        part = pl.ds(step * each, each)
        return pltpu.make_async_copy(sens_ref.at[part], block_ref.at[part], sems.at[step])

    start_all(others)
    needed = (count + each - 1) // each

    @pl.loop(0, needed)
    def _(step):
        block_copy(step).start()

    acc_ref[...] = jnp.zeros_like(acc_ref)
    wait_all(others)

    @pl.loop(0, needed)
    def _(step):
        block_copy(step).wait()
        for k in range(each):
            slot = step * each + k
            work(slot, block_ref[slot], slot < count)


def forward_body(me_ref, rows_ref, cols_ref, count_ref, sens_ref, *refs):
    peers = len(refs) - 9
    wave_refs, (even_ref, odd_ref) = refs[:peers], refs[peers + 1 : peers + 3]
    block_ref, held_ref, acc_ref, sems, got, put = refs[peers + 3 :]
    row_blocks = acc_ref.shape[0] - 1
    each = row_blocks // peers
    me = me_ref[0]
    def work(slot, block, live):
        row = jnp.where(live, rows_ref[0, slot], row_blocks)
        acc_ref[row] += jnp.dot(
            block, held_ref[cols_ref[0, slot]], preferred_element_type=jnp.float32
        )

    waves = gather_pieces([(ref, 0) for ref in wave_refs], held_ref, me, got)
    slot_loop(count_ref[0, 0], sens_ref, block_ref, sems, waves, acc_ref, work)
    stores = []
    for offset in [*range(1, peers, 2), *range(0, peers, 2)]:
        target = odd_ref if offset % 2 else even_ref
        stores.append(
            pltpu.make_async_copy(
                acc_ref.at[pl.ds((me ^ offset) * each, each)],
                target.at[pl.ds((offset // 2) * each, each)],
                put.at[offset],
            )
        )
    start_all(stores)
    wait_all(stores)


def forward(me, rows, cols, count, sens, waves, after):
    slots = sens.shape[0]
    peers = len(waves)
    blocks, width = after[1], sens.shape[2]
    half = (RB_DEV // 2, BLK, width)
    return pl.pallas_call(
        forward_body,
        out_shape=[jax.ShapeDtypeStruct(half, jnp.float32)] * 2,
        in_specs=[SMEM_SPEC] * 4 + [ANY_SPEC] * (1 + peers + 1),
        out_specs=[ANY_SPEC] * 2,
        scratch_shapes=[
            pltpu.VMEM(sens.shape, sens.dtype),
            pltpu.VMEM((blocks, BLK, width), jnp.bfloat16),
            pltpu.VMEM((RB_DEV + 1, BLK, width), jnp.float32),
            pltpu.SemaphoreType.DMA((slots // STEP,)),
            pltpu.SemaphoreType.DMA((peers,)),
            pltpu.SemaphoreType.DMA((peers,)),
        ],
        compiler_params=pltpu.CompilerParams(vmem_limit_bytes=LARGE),
        cost_estimate=pl.CostEstimate(
            flops=2 * slots * BLK * BLK * width, bytes_accessed=2 * slots * BLK * BLK,
            transcendentals=0,
        ),
        name="forward",
    )(me, rows, cols, count, sens, *waves, after[0])


def adjoint_body(me_ref, rows_ref, cols_ref, count_ref, sens_ref, even_in_ref, odd_in_ref,
                 after_ref, *refs):
    out_refs, image_ref = refs[:-9], refs[-9]
    block_ref, held_ref, acc_ref, half_ref, sems, got, put, whole = refs[-8:]
    peers = put.shape[0]
    col_blocks = acc_ref.shape[0] - 1
    each = col_blocks // peers
    me = me_ref[0]
    def work(slot, block, live):
        col = jnp.where(live, cols_ref[0, slot], col_blocks)
        acc_ref[col] += lax.dot_general(
            block, held_ref[rows_ref[0, slot]], (((0,), (0,)), ((), ())),
            preferred_element_type=jnp.float32,
        )

    each_in = held_ref.shape[0] // peers
    sources = [
        (odd_in_ref if o % 2 else even_in_ref, o // 2 * each_in) for o in range(peers)
    ]
    images = gather_pieces(sources, held_ref, me, got)
    slot_loop(count_ref[0, 0], sens_ref, block_ref, sems, images, acc_ref, work)
    stores = []
    for offset in reversed(range(peers)):
        part = acc_ref[pl.ds((me ^ offset) * each, each)]
        half_ref[offset] = part.astype(half_ref.dtype)
        target = out_refs[offset // 2].at[pl.ds(offset % 2 * each, each)]
        stores.append(pltpu.make_async_copy(half_ref.at[offset], target, put.at[offset]))
        stores[-1].start()
    stores.extend(fetch(held_ref, image_ref, whole, whole.shape[0]))
    start_all(stores[peers:])
    wait_all(stores)


def adjoint(me, rows, cols, count, sens, even, odd, after, blocks, peers):
    slots = sens.shape[0]
    width = even.shape[2]
    piece = (blocks // peers, BLK, width)
    image = (RB_DEV, BLK, width)
    outs = pl.pallas_call(
        adjoint_body,
        out_shape=[jax.ShapeDtypeStruct((2 * piece[0], *piece[1:]), jnp.bfloat16)] * (peers // 2)
        + [jax.ShapeDtypeStruct(image, jnp.bfloat16)],
        in_specs=[SMEM_SPEC] * 4 + [ANY_SPEC] * 4,
        out_specs=[ANY_SPEC] * (peers // 2 + 1),
        scratch_shapes=[
            pltpu.VMEM(sens.shape, sens.dtype),
            pltpu.VMEM(image, jnp.bfloat16),
            pltpu.VMEM((blocks + 1, BLK, width), jnp.float32),
            pltpu.VMEM((peers, *piece), jnp.bfloat16),
            pltpu.SemaphoreType.DMA((slots // STEP,)),
            pltpu.SemaphoreType.DMA((peers,)),
            pltpu.SemaphoreType.DMA((peers,)),
            pltpu.SemaphoreType.DMA((4,)),
        ],
        compiler_params=pltpu.CompilerParams(vmem_limit_bytes=LARGE),
        cost_estimate=pl.CostEstimate(
            flops=2 * slots * BLK * BLK * width, bytes_accessed=2 * slots * BLK * BLK,
            transcendentals=0,
        ),
        name="adjoint",
    )(me, rows, cols, count, sens, even, odd, after)
    return outs[:-1], outs[-1]


def tile_value(near, face, window):
    span = lax.broadcasted_iota(jnp.int32, (2 * BLK, BLK), 0)
    center = lax.broadcasted_iota(jnp.int32, (2 * BLK, BLK), 1) + RIM
    mix = jnp.where(span == center, jnp.sum(face, axis=0, keepdims=True), 0.0)
    for k in range(4):
        mix = mix - jnp.where(span == near[k : k + 1], face[k : k + 1], 0.0)
    mix_high = mix.astype(jnp.bfloat16)
    mix_low = (mix - mix_high.astype(jnp.float32)).astype(jnp.bfloat16)
    near_high = window.astype(jnp.bfloat16)
    near_low = (window - near_high.astype(jnp.float32)).astype(jnp.bfloat16)
    return lax.dot_general(
        jnp.concatenate([mix_high, mix_high, mix_low], axis=0),
        jnp.concatenate([near_high, near_low, near_high], axis=0),
        (((0,), (0,)), ((), ())), preferred_element_type=jnp.float32,
    )


def smooth_body(offset_ref, model_ref, near_ref, weight_ref, after_ref,
                out_ref, ext_ref, value_ref, got, put):
    cells, width = model_ref.shape
    steps = put.shape[0]
    tiles = cells // BLK // steps
    each = cells // got.shape[0]
    loads = [
        pltpu.make_async_copy(
            model_ref.at[pl.ds(i * each, each)], ext_ref.at[pl.ds(RIM + i * each, each)], got.at[i]
        )
        for i in range(got.shape[0])
    ]
    start_all(loads)
    ext_ref[:RIM] = jnp.zeros((RIM, width), jnp.float32)
    ext_ref[RIM + cells :] = jnp.zeros((RIM, width), jnp.float32)
    wait_all(loads)

    def store(step):
        part = pl.ds(step * tiles * BLK, tiles * BLK)
        return pltpu.make_async_copy(value_ref.at[part], out_ref.at[part], put.at[step])

    @pl.loop(0, steps)
    def _(step):
        for t in range(tiles):
            start = pl.multiple_of((step * tiles + t) * BLK, BLK)
            near = near_ref[:, pl.ds(start, BLK)] - (offset_ref[0] + start)
            face = weight_ref[:, pl.ds(start, BLK)]
            window = ext_ref[pl.ds(start, 2 * BLK), :]
            value_ref[pl.ds(start, BLK), :] = tile_value(near, face, window)
        store(step).start()

    for step in range(steps):
        store(step).wait()


def smoothing(offset, model, neighbors, face_weight, after):
    cells, width = model.shape
    return pl.pallas_call(
        smooth_body,
        out_shape=jax.ShapeDtypeStruct((cells, width), jnp.float32),
        in_specs=[SMEM_SPEC, ANY_SPEC, VMEM_SPEC, VMEM_SPEC, ANY_SPEC],
        out_specs=ANY_SPEC,
        scratch_shapes=[
            pltpu.VMEM((cells + 2 * RIM, width), jnp.float32),
            pltpu.VMEM((cells, width), jnp.float32),
            pltpu.SemaphoreType.DMA((16,)),
            pltpu.SemaphoreType.DMA((8,)),
        ],
        compiler_params=pltpu.CompilerParams(vmem_limit_bytes=LARGE),
        cost_estimate=pl.CostEstimate(
            flops=24 * cells * BLK * width, bytes_accessed=16 * cells * width, transcendentals=0
        ),
        name="smoothing",
    )(offset, model, neighbors, face_weight, after)


def edges_body(me_ref, offset_ref, model_ref, near_ref, weight_ref, base_ref, after_ref, *refs):
    odd_refs, refs = refs[:-6], refs[-6:]
    out_ref, window_ref, value_ref, ends_ref, got, put = refs
    cells = model_ref.shape[0]
    each = odd_refs[-1].shape[0] - 1
    inner = 2 * BLK - RIM
    starts = (0, cells - BLK)
    me = me_ref[0]
    loads = [
        pltpu.make_async_copy(
            model_ref.at[pl.ds(0, inner)], window_ref.at[0, pl.ds(RIM, inner)], got.at[0]
        ),
        pltpu.make_async_copy(
            model_ref.at[pl.ds(cells - inner, inner)], window_ref.at[1, pl.ds(0, inner)], got.at[1]
        ),
    ]
    for i, odd_ref in enumerate(odd_refs):
        loads.append(
            pltpu.make_async_copy(odd_ref.at[each], ends_ref.at[i], got.at[2 + i])
        )
    start_all(loads)
    wait_all(loads)
    zero = jnp.zeros((RIM, model_ref.shape[1]), jnp.float32)
    low, high = zero, zero
    for i in range(len(odd_refs)):
        rows = ends_ref[i, :RIM].astype(jnp.float32) + ends_ref[i, RIM:].astype(jnp.float32)
        peer = me ^ (2 * i + 1)
        low = jnp.where(peer == me - 1, rows, low)
        high = jnp.where(peer == me + 1, rows, high)
    window_ref[0, :RIM] = low
    window_ref[1, inner:] = high
    stores = []
    for i, start in enumerate(starts):
        near = near_ref[:, start : start + BLK] - (offset_ref[0] + start)
        value_ref[i] = tile_value(near, weight_ref[:, start : start + BLK], window_ref[i])
        stores.append(
            pltpu.make_async_copy(value_ref.at[i], out_ref.at[pl.ds(start, BLK)], put.at[i])
        )
    start_all(stores)
    wait_all(stores)


def edges(me, offset, model, neighbors, face_weight, base, after, odd_pieces):
    width = model.shape[1]
    count = len(odd_pieces)
    return pl.pallas_call(
        edges_body,
        out_shape=jax.ShapeDtypeStruct(base.shape, base.dtype),
        in_specs=[SMEM_SPEC, SMEM_SPEC, ANY_SPEC, VMEM_SPEC, VMEM_SPEC]
        + [ANY_SPEC] * (2 + count),
        out_specs=ANY_SPEC,
        input_output_aliases={5: 0},
        scratch_shapes=[
            pltpu.VMEM((2, 2 * BLK, width), jnp.float32),
            pltpu.VMEM((2, BLK, width), jnp.float32),
            pltpu.VMEM((count, BLK, width), jnp.bfloat16),
            pltpu.SemaphoreType.DMA((2 + count,)),
            pltpu.SemaphoreType.DMA((2,)),
        ],
        compiler_params=pltpu.CompilerParams(vmem_limit_bytes=LARGE),
        cost_estimate=pl.CostEstimate(
            flops=24 * 2 * BLK * BLK * width, bytes_accessed=32 * BLK * width, transcendentals=0
        ),
        name="edges",
    )(me, offset, model, neighbors, face_weight, base, after, *odd_pieces)


def finish_body(me_ref, order_ref, basis_ref, even_ref, odd_ref, base_ref,
                out_ref, token_ref, block_ref, value_ref, got, put, *, offset):
    per_peer = odd_ref.shape[0]
    cols = 2 * per_peer
    fetches, stores = [], []
    for i in range(cols):
        peer = me_ref[0] ^ (offset + i // per_peer)
        cell = order_ref[0, peer * per_peer + i % per_peer]
        fetches.append(pltpu.make_async_copy(base_ref.at[cell], block_ref.at[i], got.at[i]))
        stores.append(pltpu.make_async_copy(block_ref.at[i], out_ref.at[cell], put.at[i]))
    start_all(fetches)
    for i in range(cols):
        wave = even_ref[i] if i < per_peer else odd_ref[i - per_peer]
        both = jnp.concatenate([wave, wave], axis=0)
        value_ref[i] = jnp.dot(basis_ref[...], both, preferred_element_type=jnp.float32)
    wait_all(fetches)
    block_ref[...] += value_ref[...]
    start_all(stores)
    token_ref[...] = jnp.zeros_like(token_ref)
    wait_all(stores)


def finish(me, order, even, odd, base, offset):
    width = odd.shape[2]
    cols = 2 * odd.shape[0]
    basis = haar_matrix(BLK).T.astype(np.float32)
    high = basis.astype(jnp.bfloat16)
    low = (basis - high.astype(np.float32)).astype(jnp.bfloat16)
    basis2 = jnp.asarray(np.concatenate([high, low], axis=1))
    return pl.pallas_call(
        lambda *refs: finish_body(*refs, offset=offset),
        out_shape=[
            jax.ShapeDtypeStruct(base.shape, base.dtype),
            jax.ShapeDtypeStruct((8, BLK), jnp.float32),
        ],
        in_specs=[SMEM_SPEC] * 2 + [VMEM_SPEC] * 3 + [ANY_SPEC],
        out_specs=[ANY_SPEC, VMEM_SPEC],
        input_output_aliases={5: 0},
        scratch_shapes=[
            pltpu.VMEM((cols, BLK, width), jnp.float32),
            pltpu.VMEM((cols, BLK, width), jnp.float32),
            pltpu.SemaphoreType.DMA((cols,)),
            pltpu.SemaphoreType.DMA((cols,)),
        ],
        compiler_params=pltpu.CompilerParams(vmem_limit_bytes=SMALL),
        cost_estimate=pl.CostEstimate(
            flops=4 * cols * BLK * BLK * width, bytes_accessed=10 * cols * BLK * width,
            transcendentals=0,
        ),
        name="finish",
    )(me, order, basis2, even, odd, base)


def merge_body(got_ref, mine_ref, after_ref, out_ref):
    total = got_ref[...].astype(jnp.float32) + mine_ref[...].astype(jnp.float32)
    out_ref[...] = total.astype(out_ref.dtype)


def merge(got, mine, after):
    return pl.pallas_call(
        merge_body,
        out_shape=jax.ShapeDtypeStruct(mine.shape, mine.dtype),
        in_specs=[VMEM_SPEC, VMEM_SPEC, ANY_SPEC],
        out_specs=VMEM_SPEC,
        compiler_params=pltpu.CompilerParams(vmem_limit_bytes=SMALL),
        cost_estimate=pl.CostEstimate(
            flops=mine.size, bytes_accessed=6 * mine.size, transcendentals=0
        ),
        name="merge",
    )(got, mine, after)


def pick_body(take_ref, got_ref, mine_ref, after_ref, token_ref, *out_refs):
    each = out_refs[0].shape[0]
    for i, out_ref in enumerate(out_refs):
        part = pl.ds(i * each, each)
        out_ref[...] = jnp.where(take_ref[0] > 0, got_ref[part], mine_ref[part])


def pick(take, got, mine, after, token, parts):
    shape = (mine.shape[0] // parts, *mine.shape[1:])
    return pl.pallas_call(
        pick_body,
        out_shape=[jax.ShapeDtypeStruct(shape, mine.dtype)] * parts,
        in_specs=[SMEM_SPEC, VMEM_SPEC, VMEM_SPEC, ANY_SPEC, ANY_SPEC],
        out_specs=[VMEM_SPEC] * parts,
        compiler_params=pltpu.CompilerParams(vmem_limit_bytes=SMALL),
        cost_estimate=pl.CostEstimate(
            flops=mine.size, bytes_accessed=6 * mine.size, transcendentals=0
        ),
        name="pick",
    )(take, got, mine, after, token)


def line_sums(parts, axis, deliver):
    count = lax.axis_size(axis)
    half = count // 2
    me = lax.axis_index(axis)
    stages = []
    for hop in range(half - 1):
        stages.append(([(hop, hop + 1), (count - 1 - hop, count - 2 - hop)], False))
    stages.append(([(half - 1, half), (half, half - 1)], False))
    for hop in range(half - 1):
        left, right = half - 1 - hop, half + hop
        stages.append(([(left, left - 1), (right, right + 1)], True))
    state = list(parts)
    got = [lax.ppermute(part, axis, stages[0][0]) for part in parts]
    after = parts[0]
    for time in range(len(parts) + len(stages) - 1):
        for s, (pairs, outwards) in enumerate(stages):
            k = time - s
            if not 0 <= k < len(parts):
                continue
            last = s + 1 == len(stages)
            if outwards:
                take = (me == pairs[0][1]) | (me == pairs[1][1])
                take = take.astype(jnp.int32).reshape(1)
                if last:
                    after = deliver(k, take, got[k], state[k], after)
                else:
                    state[k] = jnp.where(take[0] > 0, got[k], state[k])
            else:
                state[k] = after = merge(got[k], state[k], after)
                if last:
                    take = jnp.zeros((1,), jnp.int32)
                    after = deliver(k, take, state[k], state[k], after)
            if not last:
                got[k] = lax.ppermute(state[k], axis, stages[s + 1][0])


def swap(piece, axis, offset):
    return lax.ppermute(piece, axis, [(c, c ^ offset) for c in range(lax.axis_size(axis))])


def local(model_dir, sens_blocks, blk_row, blk_col, blk_count, send_order, neighbors, face_weight):
    cell_count, width = model_dir.shape
    blocks = cell_count // BLK
    peers = lax.axis_size("cols")
    half = peers // 2
    per_peer = blocks // peers
    col = lax.axis_index("cols").astype(jnp.int32)
    me = col.reshape(1)
    offset = (col * cell_count - RIM).reshape(1)
    sens = sens_blocks[0]
    evens = range(1, half)

    *own, odd = analyze(me, send_order, model_dir.reshape(blocks, BLK, width), peers)
    partner = swap(odd, "cols", 1)
    direct = {j: swap(own[j], "cols", 2 * j) for j in reversed(evens)}
    passed = {
        j: swap(partner[j * (per_peer + 1) : (j + 1) * (per_peer + 1)], "cols", 2 * j)
        for j in reversed(evens)
    }
    waves = [own[0], partner]
    for j in evens:
        waves += [direct[j], passed[j]]
    smooth = smoothing(offset, model_dir, neighbors, face_weight, partner)

    even_rows, odd_rows = forward(
        me, blk_row, blk_col, blk_count, sens, waves, (smooth, blocks)
    )
    pair = (even_rows + swap(odd_rows, "cols", 1)).reshape(half, -1, BLK, width)
    to_send = pair.astype(jnp.bfloat16)
    shares = [swap(to_send[j], "cols", 2 * j) for j in evens]
    total = pair[0] + sum(share.astype(jnp.float32) for share in shares)
    image_share = total.astype(jnp.bfloat16)
    even_image = jnp.concatenate(
        [image_share] + [swap(image_share, "cols", 2 * j) for j in evens], axis=0
    )
    odd_image = swap(even_image, "cols", 1)
    smooth = edges(
        me, offset, model_dir, neighbors, face_weight, smooth, to_send, waves[1::2]
    )

    partial_cols, image = adjoint(
        me, blk_row, blk_col, blk_count, sens, even_image, odd_image, smooth, blocks, peers
    )
    data_image = image.reshape(RB_DEV * BLK, width).astype(jnp.float32)
    normal = smooth.reshape(blocks, BLK, width)
    order = sorted(range(half), key=lambda j: (-bin(j).count("1"), j))
    waiting, tokens = [], []

    def end_one():
        nonlocal normal
        even, odd_piece, j = waiting.pop(0)
        normal, token = finish(me, send_order, even, odd_piece, normal, 2 * j)
        tokens.append(token)

    def deliver(k, take, got, mine, after):
        if k >= 2:
            end_one()
        token = tokens[-1] if tokens else after
        j = order[k]
        if j:
            [total] = pick(take, got, mine, after, token, 1)
            even = swap(total, "cols", 2 * j)
            other = even[per_peer:]
        else:
            even, other = pick(take, got, mine, after, token, 2)
            total = even
        waiting.append((even, swap(other, "cols", 1), j))
        return total

    line_sums([partial_cols[j] for j in order], "rows", deliver)
    while waiting:
        end_one()
    return (data_image, normal.reshape(cell_count, width))


def solution(mesh):
    placed = (
        P("cols", None),
        P("rows", "cols", None, None),
        P("rows", "cols"),
        P("rows", "cols"),
        P("rows", "cols"),
        P("cols", None),
        P(None, "cols"),
        P(None, "cols"),
    )
    return jax.shard_map(
        local,
        mesh=mesh,
        in_specs=placed,
        out_specs=(P("rows", None), P("cols", None)),
        check_vma=False,
    )
```

profile of v0, /device:TPU:11, one launch (start us, length us, event | category | flops | bytes accessed | tf_op | source)
XLA Modules:
  0.0 178.7 jit_solution(11014280914667127310)
XLA Ops:
  0.6 5.0 %analyze.1 = (bf16[8,128,128]{2,1,0:T(8,128)(2,1)}, bf16[8,128,128]{2,1,0:T(8,128)(2,1)}, bf16[8,128,128]{2,1,0:T(8,128)(2,1)}, bf16[8,128,128]{2,1,0:T(8,128)(2,1)}, bf16[36,128,128]{2,1,0:T(8,128)(2,1)}) custom-call(s32[1]{0:T(128)} %bitcast.me_ref.refs_0_, s32[1,64]{1,0:T(1,128)} %refs_1_.7, f32[64,128,128]{2,1,0:T(8,128)} %bitcast.15), custom_call_target="tpu_custom_call" | custom-call | flops 536870912 | bytes 6291456 | tf_op jit(solution)/shard_map/analyze/pallas_call | solution.py:136
  5.6 0.7 collective-permute-start
  6.4 0.3 collective-permute-start.1
  6.6 1.2 collective-permute-start.3
  7.9 1.2 collective-permute-start.5
  9.8 1.3 collective-permute-start.6
  11.0 0.2 collective-permute-start.4
  11.3 3.2 %collective-permute-done.1.refs_2_ = bf16[8,128,128]{2,1,0:T(8,128)(2,1)S(1)} collective-permute-done((bf16[8,128,128]{2,1,0:T(8,128)(2,1)}, bf16[8,128,128]{2,1,0:T(8,128)(2,1)S(1)}, u32[]{:S(2)}, u32[]{:S(2)}) %collective-permute-start.1) | collective-permute-done | bytes 262176 | tf_op jit(solution)/shard_map/ppermute | solution.py:573
  14.5 0.3 collective-permute-start.2
  14.7 13.3 %smoothing.1.refs_8_.base_ref = f32[8192,128]{1,0:T(8,128)} custom-call(s32[1]{0:T(128)} %bitcast.3.offset_ref, f32[8192,128]{1,0:T(8,128)} %model_ref.3, s32[4,8192]{1,0:T(4,128)} %near_ref.3, f32[4,8192]{1,0:T(4,128)} %weight_ref.3, bf16[36,128,128]{2,1,0:T(8,128)(2,1)} %copy-done.6), custom_call_target="tpu_custom_call" | custom-call | flops 3221225472 | bytes 16777216 | tf_op jit(solution)/shard_map/smoothing/pallas_call | solution.py:356
  28.1 4.5 %collective-permute-done.4.refs_5_.refs_2_ = bf16[9,128,128]{2,1,0:T(8,128)(2,1)S(1)} collective-permute-done((bf16[9,128,128]{2,1,0:T(8,128)(2,1)S(1)}, bf16[9,128,128]{2,1,0:T(8,128)(2,1)S(1)}, u32[]{:S(2)}, u32[]{:S(2)}) %collective-permute-start.4) | collective-permute-done | bytes 294944 | tf_op jit(solution)/shard_map/ppermute | solution.py:573
  32.8 0.6 copy-done.10
  33.5 7.5 %forward.1 = (f32[16,128,128]{2,1,0:T(8,128)}, f32[16,128,128]{2,1,0:T(8,128)}) custom-call(s32[1]{0:T(128)} %bitcast.me_ref.refs_0_, s32[1,384]{1,0:T(1,128)} %rows_ref.3, s32[1,384]{1,0:T(1,128)} %cols_ref.3, s32[1,1]{1,0:T(1,128)S(6)} %copy.24.count_ref, bf16[384,128,128]{2,1,0:T(8,128)(2,1)} %bitcast.13, bf16[8,128,128]{2,1,0:T(8,128)(2,1)} %get-tuple-element.22.refs_0_, ...), custom_call_target="tpu_custom_call" | custom-call | flops 1610612736 | bytes 12582912 | tf_op jit(solution)/shard_map/forward/pallas_call | solution.py:216
  41.1 2.9 %collective-permute-done.7 = f32[16,128,128]{2,1,0:T(8,128)S(1)} collective-permute-done((f32[16,128,128]{2,1,0:T(8,128)}, f32[16,128,128]{2,1,0:T(8,128)S(1)}, u32[]{:S(2)}, u32[]{:S(2)}) %collective-permute-start.7) | collective-permute-done | bytes 1048608 | tf_op jit(solution)/shard_map/ppermute | solution.py:573
  44.0 1.4 fusion.1
  45.4 3.1 %collective-permute-start.8 = (bf16[4,128,128]{2,1,0:T(8,128)(2,1)S(1)}, bf16[4,128,128]{2,1,0:T(8,128)(2,1)S(1)}, u32[]{:S(2)}, u32[]{:S(2)}) collective-permute-start(bf16[4,128,128]{2,1,0:T(8,128)(2,1)S(1)} %get-tuple-element.47), channel_id=1, source_target_pairs={{0,2},{1,3},{2,0},{3,1},{4,6},{5,7},{6,4},{7,5},{8,10},{9,11},{10,... | collective-permute-start | bytes 393224 | tf_op jit(solution)/shard_map/ppermute | solution.py:573
  48.5 1.3 collective-permute-start.9
  49.8 2.5 %collective-permute-done.8 = bf16[4,128,128]{2,1,0:T(8,128)(2,1)S(1)} collective-permute-done((bf16[4,128,128]{2,1,0:T(8,128)(2,1)S(1)}, bf16[4,128,128]{2,1,0:T(8,128)(2,1)S(1)}, u32[]{:S(2)}, u32[]{:S(2)}) %collective-permute-start.8) | collective-permute-done | bytes 131104 | tf_op jit(solution)/shard_map/ppermute | solution.py:573
  52.3 2.6 %collective-permute-done.10 = bf16[4,128,128]{2,1,0:T(8,128)(2,1)S(1)} collective-permute-done((bf16[4,128,128]{2,1,0:T(8,128)(2,1)S(1)}, bf16[4,128,128]{2,1,0:T(8,128)(2,1)S(1)}, u32[]{:S(2)}, u32[]{:S(2)}) %collective-permute-start.10) | collective-permute-done | bytes 131104 | tf_op jit(solution)/shard_map/ppermute | solution.py:573
  54.9 1.0 collective-permute-done.9
  55.9 2.5 %collective-permute-start.13 = (bf16[4,128,128]{2,1,0:T(8,128)(2,1)S(1)}, bf16[4,128,128]{2,1,0:T(8,128)(2,1)S(1)}, u32[]{:S(2)}, u32[]{:S(2)}) collective-permute-start(bf16[4,128,128]{2,1,0:T(8,128)(2,1)S(1)} %fusion), channel_id=1, source_target_pairs={{0,6},{1,7},{2,4},{3,5},{4,2},{5,3},{6,0},{7,1},{8,14},{9,15},{10,... | collective-permute-start | bytes 393224 | tf_op jit(solution)/shard_map/ppermute | solution.py:573
  58.7 2.0 %collective-permute-done.13 = bf16[4,128,128]{2,1,0:T(8,128)(2,1)S(1)} collective-permute-done((bf16[4,128,128]{2,1,0:T(8,128)(2,1)S(1)}, bf16[4,128,128]{2,1,0:T(8,128)(2,1)S(1)}, u32[]{:S(2)}, u32[]{:S(2)}) %collective-permute-start.13) | collective-permute-done | bytes 131104 | tf_op jit(solution)/shard_map/ppermute | solution.py:573
  60.7 3.6 %collective-permute-done.12 = bf16[4,128,128]{2,1,0:T(8,128)(2,1)S(1)} collective-permute-done((bf16[4,128,128]{2,1,0:T(8,128)(2,1)S(1)}, bf16[4,128,128]{2,1,0:T(8,128)(2,1)S(1)}, u32[]{:S(2)}, u32[]{:S(2)}) %collective-permute-start.12) | collective-permute-done | bytes 131104 | tf_op jit(solution)/shard_map/ppermute | solution.py:573
  64.4 1.6 collective-permute-start.14
  66.0 3.1 %edges.1.after_ref = f32[8192,128]{1,0:T(8,128)} custom-call(s32[1]{0:T(128)} %bitcast.me_ref.refs_0_, s32[1]{0:T(128)} %bitcast.3.offset_ref, f32[8192,128]{1,0:T(8,128)} %model_ref.3, s32[4,8192]{1,0:T(4,128)} %near_ref.3, f32[4,8192]{1,0:T(4,128)} %weight_ref.3, f32[8192,128]{1,0:T(8,128)} %smoothing.1.refs_8_.base_ref, ...), custom_call_target="tpu_custom_call", output_to_operand_aliasing={{}: (5, {})} | custom-call | flops 100663296 | bytes 524288 | tf_op jit(solution)/shard_map/edges/pallas_call | solution.py:420
  69.1 0.8 copy-done.13
  69.9 8.0 %adjoint.1 = (bf16[16,128,128]{2,1,0:T(8,128)(2,1)}, bf16[16,128,128]{2,1,0:T(8,128)(2,1)}, bf16[16,128,128]{2,1,0:T(8,128)(2,1)}, bf16[16,128,128]{2,1,0:T(8,128)(2,1)}, bf16[32,128,128]{2,1,0:T(8,128)(2,1)}) custom-call(s32[1]{0:T(128)} %bitcast.me_ref.refs_0_, s32[1,384]{1,0:T(1,128)} %rows_ref.3, s32[1,384]{1,0:T(1,128)} %cols_ref.3, ...), custom_call_target="tpu_custom_call" | custom-call | flops 1610612736 | bytes 12582912 | tf_op jit(solution)/shard_map/adjoint/pallas_call | solution.py:276
  78.0 1.3 collective-permute-start.16
  79.3 1.3 collective-permute-start.18
  80.6 18.5 %collective-permute-done.16.got_ref = bf16[16,128,128]{2,1,0:T(8,128)(2,1)S(1)} collective-permute-done((bf16[16,128,128]{2,1,0:T(8,128)(2,1)}, bf16[16,128,128]{2,1,0:T(8,128)(2,1)S(1)}, u32[]{:S(2)}, u32[]{:S(2)}) %collective-permute-start.16) | collective-permute-done | bytes 524320 | tf_op jit(solution)/shard_map/ppermute | solution.py:548
  99.1 1.0 copy-done
  100.3 2.1 %collective-permute-start.17 = (bf16[16,128,128]{2,1,0:T(8,128)(2,1)S(1)}, bf16[16,128,128]{2,1,0:T(8,128)(2,1)S(1)}, u32[]{:S(2)}, u32[]{:S(2)}) collective-permute-start(bf16[16,128,128]{2,1,0:T(8,128)(2,1)S(1)} %merge.8.after_ref.mine_ref), channel_id=1, source_target_pairs={{8,16},{16,8},{9,17},{17,9},{10,18},{18,10},{11,19},{19,11},{12,20... | collective-permute-start | bytes 1572872 | tf_op jit(solution)/shard_map/ppermute | solution.py:569
  102.3 1.3 collective-permute-start.21
  103.6 3.1 %collective-permute-done.18.got_ref = bf16[16,128,128]{2,1,0:T(8,128)(2,1)S(1)} collective-permute-done((bf16[16,128,128]{2,1,0:T(8,128)(2,1)}, bf16[16,128,128]{2,1,0:T(8,128)(2,1)S(1)}, u32[]{:S(2)}, u32[]{:S(2)}) %collective-permute-start.18) | collective-permute-done | bytes 524320 | tf_op jit(solution)/shard_map/ppermute | solution.py:548
  106.8 1.0 copy-done.4
  107.9 3.2 %collective-permute-start.20 = (bf16[16,128,128]{2,1,0:T(8,128)(2,1)S(1)}, bf16[16,128,128]{2,1,0:T(8,128)(2,1)}, u32[]{:S(2)}, u32[]{:S(2)}) collective-permute-start(bf16[16,128,128]{2,1,0:T(8,128)(2,1)S(1)} %merge.9.after_ref.mine_ref), channel_id=1, source_target_pairs={{8,16},{16,8},{9,17},{17,9},{10,18},{18,10},{11,19},{19,11},{12,20... | collective-permute-start | bytes 1572872 | tf_op jit(solution)/shard_map/ppermute | solution.py:569
  111.1 5.0 %collective-permute-done.17.got_ref = bf16[16,128,128]{2,1,0:T(8,128)(2,1)S(1)} collective-permute-done((bf16[16,128,128]{2,1,0:T(8,128)(2,1)S(1)}, bf16[16,128,128]{2,1,0:T(8,128)(2,1)S(1)}, u32[]{:S(2)}, u32[]{:S(2)}) %collective-permute-start.17) | collective-permute-done | bytes 524320 | tf_op jit(solution)/shard_map/ppermute | solution.py:569
  116.3 2.1 %collective-permute-start.19 = (bf16[16,128,128]{2,1,0:T(8,128)(2,1)S(1)}, bf16[16,128,128]{2,1,0:T(8,128)(2,1)}, u32[]{:S(2)}, u32[]{:S(2)}) collective-permute-start(bf16[16,128,128]{2,1,0:T(8,128)(2,1)S(1)} %merge.10.after_ref.mine_ref), channel_id=1, source_target_pairs={{8,0},{16,24},{9,1},{17,25},{10,2},{18,26},{11,3},{19,27},{12,4},{... | collective-permute-start | bytes 1572872 | tf_op jit(solution)/shard_map/ppermute | solution.py:569
  118.4 1.3 collective-permute-start.15
  119.8 2.2 %collective-permute-start.24 = (bf16[16,128,128]{2,1,0:T(8,128)(2,1)S(1)}, bf16[16,128,128]{2,1,0:T(8,128)(2,1)S(1)}, u32[]{:S(2)}, u32[]{:S(2)}) collective-permute-start(bf16[16,128,128]{2,1,0:T(8,128)(2,1)S(1)} %merge.11.after_ref.mine_ref), channel_id=1, source_target_pairs={{8,16},{16,8},{9,17},{17,9},{10,18},{18,10},{11,19},{19,11},{12,20... | collective-permute-start | bytes 1572872 | tf_op jit(solution)/shard_map/ppermute | solution.py:569
  122.0 5.2 %collective-permute-done.20.got_ref = bf16[16,128,128]{2,1,0:T(8,128)(2,1)} collective-permute-done((bf16[16,128,128]{2,1,0:T(8,128)(2,1)S(1)}, bf16[16,128,128]{2,1,0:T(8,128)(2,1)}, u32[]{:S(2)}, u32[]{:S(2)}) %collective-permute-start.20) | collective-permute-done | bytes 524320 | tf_op jit(solution)/shard_map/ppermute | solution.py:569
  127.3 1.2 merge.12.after_ref.token_ref.mine_ref
  128.4 1.3 collective-permute-start.23
  129.8 1.2 pick.4.after_ref
  131.0 2.7 %collective-permute-done.15.got_ref = bf16[16,128,128]{2,1,0:T(8,128)(2,1)S(1)} collective-permute-done((bf16[16,128,128]{2,1,0:T(8,128)(2,1)S(1)}, bf16[16,128,128]{2,1,0:T(8,128)(2,1)S(1)}, u32[]{:S(2)}, u32[]{:S(2)}) %collective-permute-start.15) | collective-permute-done | bytes 524320 | tf_op jit(solution)/shard_map/ppermute | solution.py:548
  133.9 2.1 %collective-permute-start.22 = (bf16[16,128,128]{2,1,0:T(8,128)(2,1)S(1)}, bf16[16,128,128]{2,1,0:T(8,128)(2,1)S(1)}, u32[]{:S(2)}, u32[]{:S(2)}) collective-permute-start(bf16[16,128,128]{2,1,0:T(8,128)(2,1)S(1)} %merge.13.after_ref.mine_ref), channel_id=1, source_target_pairs={{8,16},{16,8},{9,17},{17,9},{10,18},{18,10},{11,19},{19,11},{12,20... | collective-permute-start | bytes 1572872 | tf_op jit(solution)/shard_map/ppermute | solution.py:569
  136.0 1.8 %collective-permute-done.24.got_ref = bf16[16,128,128]{2,1,0:T(8,128)(2,1)S(1)} collective-permute-done((bf16[16,128,128]{2,1,0:T(8,128)(2,1)S(1)}, bf16[16,128,128]{2,1,0:T(8,128)(2,1)S(1)}, u32[]{:S(2)}, u32[]{:S(2)}) %collective-permute-start.24) | collective-permute-done | bytes 524320 | tf_op jit(solution)/shard_map/ppermute | solution.py:569
  137.9 1.3 collective-permute-start.26
  139.3 2.1 %collective-permute-done.23.got_ref = bf16[16,128,128]{2,1,0:T(8,128)(2,1)S(1)} collective-permute-done((bf16[16,128,128]{2,1,0:T(8,128)(2,1)S(1)}, bf16[16,128,128]{2,1,0:T(8,128)(2,1)S(1)}, u32[]{:S(2)}, u32[]{:S(2)}) %collective-permute-start.23) | collective-permute-done | bytes 524320 | tf_op jit(solution)/shard_map/ppermute | solution.py:569
  141.6 4.0 %collective-permute-done.27.refs_3_ = bf16[16,128,128]{2,1,0:T(8,128)(2,1)S(1)} collective-permute-done((bf16[16,128,128]{2,1,0:T(8,128)(2,1)S(1)}, bf16[16,128,128]{2,1,0:T(8,128)(2,1)S(1)}, u32[]{:S(2)}, u32[]{:S(2)}) %collective-permute-start.27) | collective-permute-done | bytes 524320 | tf_op jit(solution)/shard_map/ppermute | solution.py:573
  145.7 3.8 %collective-permute-done.22.got_ref = bf16[16,128,128]{2,1,0:T(8,128)(2,1)S(1)} collective-permute-done((bf16[16,128,128]{2,1,0:T(8,128)(2,1)S(1)}, bf16[16,128,128]{2,1,0:T(8,128)(2,1)S(1)}, u32[]{:S(2)}, u32[]{:S(2)}) %collective-permute-start.22) | collective-permute-done | bytes 524320 | tf_op jit(solution)/shard_map/ppermute | solution.py:569
  149.6 1.5 collective-permute-start.25
  151.1 3.3 %finish.4 = (f32[64,128,128]{2,1,0:T(8,128)}, f32[8,128]{1,0:T(8,128)S(1)}) custom-call(s32[1]{0:T(128)} %bitcast.me_ref.refs_0_, s32[1,64]{1,0:T(1,128)S(1)} %copy-done.5, bf16[128,256]{1,0:T(8,128)(2,1)S(1)} %copy-done.1, bf16[16,128,128]{2,1,0:T(8,128)(2,1)S(1)} %collective-permute-done.27.refs_3_, ...), custom_call_target="tpu_custom_call", output_to_operand_aliasing={{0}: (5, {})} | custom-call | flops 134217728 | bytes 2621440 | tf_op jit(solution)/shard_map/finish/pallas_call | solution.py:471
  154.7 0.2 collective-permute-done.29.refs_3_
  155.0 0.6 collective-permute-start.30
  155.6 1.2 collective-permute-done.30.refs_4_
  156.8 3.3 %finish.5 = (f32[64,128,128]{2,1,0:T(8,128)}, f32[8,128]{1,0:T(8,128)S(1)}) custom-call(s32[1]{0:T(128)} %bitcast.me_ref.refs_0_, s32[1,64]{1,0:T(1,128)S(1)} %copy-done.5, bf16[128,256]{1,0:T(8,128)(2,1)S(1)} %copy-done.1, bf16[16,128,128]{2,1,0:T(8,128)(2,1)S(1)} %collective-permute-done.29.refs_3_, ...), custom_call_target="tpu_custom_call", output_to_operand_aliasing={{0}: (5, {})} | custom-call | flops 134217728 | bytes 2621440 | tf_op jit(solution)/shard_map/finish/pallas_call | solution.py:471
  160.2 2.8 %collective-permute-done.25.got_ref = bf16[16,128,128]{2,1,0:T(8,128)(2,1)S(1)} collective-permute-done((bf16[16,128,128]{2,1,0:T(8,128)(2,1)S(1)}, bf16[16,128,128]{2,1,0:T(8,128)(2,1)S(1)}, u32[]{:S(2)}, u32[]{:S(2)}) %collective-permute-start.25) | collective-permute-done | bytes 524320 | tf_op jit(solution)/shard_map/ppermute | solution.py:569
  163.1 0.8 collective-permute-start.31
  163.9 3.5 %collective-permute-done.32.refs_3_ = bf16[16,128,128]{2,1,0:T(8,128)(2,1)S(1)} collective-permute-done((bf16[16,128,128]{2,1,0:T(8,128)(2,1)S(1)}, bf16[16,128,128]{2,1,0:T(8,128)(2,1)S(1)}, u32[]{:S(2)}, u32[]{:S(2)}) %collective-permute-start.32) | collective-permute-done | bytes 524320 | tf_op jit(solution)/shard_map/ppermute | solution.py:573
  167.4 1.8 collective-permute-start.33
  169.2 1.5 bitcast_convert_fusion
  170.7 3.9 %finish.6 = (f32[64,128,128]{2,1,0:T(8,128)}, f32[8,128]{1,0:T(8,128)}) custom-call(s32[1]{0:T(128)} %bitcast.me_ref.refs_0_, s32[1,64]{1,0:T(1,128)S(1)} %copy-done.5, bf16[128,256]{1,0:T(8,128)(2,1)S(1)} %copy-done.1, bf16[16,128,128]{2,1,0:T(8,128)(2,1)S(1)} %collective-permute-done.32.refs_3_, ...), custom_call_target="tpu_custom_call", output_to_operand_aliasing={{0}: (5, {})} | custom-call | flops 134217728 | bytes 2621440 | tf_op jit(solution)/shard_map/finish/pallas_call | solution.py:471
  174.6 3.9 %finish.7 = (f32[64,128,128]{2,1,0:T(8,128)}, f32[8,128]{1,0:T(8,128)}) custom-call(s32[1]{0:T(128)} %bitcast.me_ref.refs_0_, s32[1,64]{1,0:T(1,128)S(1)} %copy-done.5, bf16[128,256]{1,0:T(8,128)(2,1)S(1)} %copy-done.1, bf16[8,128,128]{2,1,0:T(8,128)(2,1)S(1)} %get-tuple-element.37.refs_3_, ...), custom_call_target="tpu_custom_call", output_to_operand_aliasing={{0}: (5, {})} | custom-call | flops 134217728 | bytes 2621440 | tf_op jit(solution)/shard_map/finish/pallas_call | solution.py:471
  (68 shorter events, 2.6 us)
Async XLA Ops:
  5.6 4.1 %collective-permute-start = (bf16[36,128,128]{2,1,0:T(8,128)(2,1)}, bf16[36,128,128]{2,1,0:T(8,128)(2,1)S(1)}, u32[]{:S(2)}, u32[]{:S(2)}) collective-permute-start(bf16[36,128,128]{2,1,0:T(8,128)(2,1)} %get-tuple-element.23), channel_id=1, source_target_pairs={{0,1},{1,0},{2,3},{3,2},{4,5},{5,4},{6,7},{7,6},{8,9},{9,8},{10,11... | collective-permute-start | bytes 3538952 | tf_op jit(solution)/shard_map/ppermute | solution.py:573
  6.4 8.1 %collective-permute-start.1 = (bf16[8,128,128]{2,1,0:T(8,128)(2,1)}, bf16[8,128,128]{2,1,0:T(8,128)(2,1)S(1)}, u32[]{:S(2)}, u32[]{:S(2)}) collective-permute-start(bf16[8,128,128]{2,1,0:T(8,128)(2,1)} %get-tuple-element.24), channel_id=1, source_target_pairs={{0,2},{1,3},{2,0},{3,1},{4,6},{5,7},{6,4},{7,5},{8,10},{9,11},{10,... | collective-permute-start | bytes 786440 | tf_op jit(solution)/shard_map/ppermute | solution.py:573
  6.6 21.4 %collective-permute-start.3 = (bf16[8,128,128]{2,1,0:T(8,128)(2,1)}, bf16[8,128,128]{2,1,0:T(8,128)(2,1)S(1)}, u32[]{:S(2)}, u32[]{:S(2)}) collective-permute-start(bf16[8,128,128]{2,1,0:T(8,128)(2,1)} %get-tuple-element.25), channel_id=1, source_target_pairs={{0,4},{1,5},{2,6},{3,7},{4,0},{5,1},{6,2},{7,3},{8,12},{9,13},{10,... | collective-permute-start | bytes 786440 | tf_op jit(solution)/shard_map/ppermute | solution.py:573
  7.9 20.2 %collective-permute-start.5 = (bf16[8,128,128]{2,1,0:T(8,128)(2,1)}, bf16[8,128,128]{2,1,0:T(8,128)(2,1)S(1)}, u32[]{:S(2)}, u32[]{:S(2)}) collective-permute-start(bf16[8,128,128]{2,1,0:T(8,128)(2,1)} %get-tuple-element.26), channel_id=1, source_target_pairs={{0,6},{1,7},{2,4},{3,5},{4,2},{5,3},{6,0},{7,1},{8,14},{9,15},{10,... | collective-permute-start | bytes 786440 | tf_op jit(solution)/shard_map/ppermute | solution.py:573
  9.7 5.0 %copy-start.6 = (bf16[36,128,128]{2,1,0:T(8,128)(2,1)}, bf16[36,128,128]{2,1,0:T(8,128)(2,1)S(1)}, u32[]{:S(2)}) copy-start(bf16[36,128,128]{2,1,0:T(8,128)(2,1)S(1)} %collective-permute-done.after_ref.refs_1_.refs_0_) | copy-start | bytes 3538948
  9.8 18.3 %collective-permute-start.6 = (bf16[9,128,128]{2,1,0:T(8,128)(2,1)S(1)}, bf16[9,128,128]{2,1,0:T(8,128)(2,1)S(1)}, u32[]{:S(2)}, u32[]{:S(2)}) collective-permute-start(bf16[9,128,128]{2,1,0:T(8,128)(2,1)S(1)} %get-tuple-element.44), channel_id=1, source_target_pairs={{0,6},{1,7},{2,4},{3,5},{4,2},{5,3},{6,0},{7,1},{8,14},{9,15},{10,... | collective-permute-start | bytes 884744 | tf_op jit(solution)/shard_map/ppermute | solution.py:573
  11.0 21.6 %collective-permute-start.4 = (bf16[9,128,128]{2,1,0:T(8,128)(2,1)S(1)}, bf16[9,128,128]{2,1,0:T(8,128)(2,1)S(1)}, u32[]{:S(2)}, u32[]{:S(2)}) collective-permute-start(bf16[9,128,128]{2,1,0:T(8,128)(2,1)S(1)} %get-tuple-element.45), channel_id=1, source_target_pairs={{0,4},{1,5},{2,6},{3,7},{4,0},{5,1},{6,2},{7,3},{8,12},{9,13},{10,... | collective-permute-start | bytes 884744 | tf_op jit(solution)/shard_map/ppermute | solution.py:573
  14.5 13.6 %copy-start.14 = (bf16[8,128,128]{2,1,0:T(8,128)(2,1)}, bf16[8,128,128]{2,1,0:T(8,128)(2,1)S(1)}, u32[]{:S(2)}) copy-start(bf16[8,128,128]{2,1,0:T(8,128)(2,1)S(1)} %collective-permute-done.1.refs_2_) | copy-start | bytes 786436
  14.5 18.3 %collective-permute-start.2 = (bf16[9,128,128]{2,1,0:T(8,128)(2,1)S(1)}, bf16[9,128,128]{2,1,0:T(8,128)(2,1)S(1)}, u32[]{:S(2)}, u32[]{:S(2)}) collective-permute-start(bf16[9,128,128]{2,1,0:T(8,128)(2,1)S(1)} %get-tuple-element.46), channel_id=1, source_target_pairs={{0,2},{1,3},{2,0},{3,1},{4,6},{5,7},{6,4},{7,5},{8,10},{9,11},{10,... | collective-permute-start | bytes 884744 | tf_op jit(solution)/shard_map/ppermute | solution.py:573
  28.1 4.7 %copy-start.15 = (bf16[8,128,128]{2,1,0:T(8,128)(2,1)}, bf16[8,128,128]{2,1,0:T(8,128)(2,1)S(1)}, u32[]{:S(2)}) copy-start(bf16[8,128,128]{2,1,0:T(8,128)(2,1)S(1)} %collective-permute-done.3.refs_4_) | copy-start | bytes 786436
  28.1 4.7 %copy-start.16 = (bf16[8,128,128]{2,1,0:T(8,128)(2,1)}, bf16[8,128,128]{2,1,0:T(8,128)(2,1)S(1)}, u32[]{:S(2)}) copy-start(bf16[8,128,128]{2,1,0:T(8,128)(2,1)S(1)} %collective-permute-done.5.refs_6_) | copy-start | bytes 786436
  28.1 4.7 %copy-start.9 = (bf16[9,128,128]{2,1,0:T(8,128)(2,1)}, bf16[9,128,128]{2,1,0:T(8,128)(2,1)S(1)}, u32[]{:S(2)}) copy-start(bf16[9,128,128]{2,1,0:T(8,128)(2,1)S(1)} %collective-permute-done.6.refs_7_.refs_3_) | copy-start | bytes 884740
  32.6 0.7 copy-start.10
  32.8 0.7 copy-start.11
  41.0 2.9 %collective-permute-start.7 = (f32[16,128,128]{2,1,0:T(8,128)}, f32[16,128,128]{2,1,0:T(8,128)S(1)}, u32[]{:S(2)}, u32[]{:S(2)}) collective-permute-start(f32[16,128,128]{2,1,0:T(8,128)} %get-tuple-element.28), channel_id=1, source_target_pairs={{0,1},{1,0},{2,3},{3,2},{4,5},{5,4},{6,7},{7,6},{8,9},{9,8},{10,11... | collective-permute-start | bytes 3145736 | tf_op jit(solution)/shard_map/ppermute | solution.py:573
  45.4 20.6 %copy-start.7 = (bf16[16,128,128]{2,1,0:T(8,128)(2,1)}, bf16[16,128,128]{2,1,0:T(8,128)(2,1)S(1)}, u32[]{:S(2)}) copy-start(bf16[16,128,128]{2,1,0:T(8,128)(2,1)S(1)} %get-tuple-element.42) | copy-start | bytes 1572868
  45.4 6.8 %collective-permute-start.8 = (bf16[4,128,128]{2,1,0:T(8,128)(2,1)S(1)}, bf16[4,128,128]{2,1,0:T(8,128)(2,1)S(1)}, u32[]{:S(2)}, u32[]{:S(2)}) collective-permute-start(bf16[4,128,128]{2,1,0:T(8,128)(2,1)S(1)} %get-tuple-element.47), channel_id=1, source_target_pairs={{0,2},{1,3},{2,0},{3,1},{4,6},{5,7},{6,4},{7,5},{8,10},{9,11},{10,... | collective-permute-start | bytes 393224 | tf_op jit(solution)/shard_map/ppermute | solution.py:573
  48.5 6.3 %collective-permute-start.10 = (bf16[4,128,128]{2,1,0:T(8,128)(2,1)S(1)}, bf16[4,128,128]{2,1,0:T(8,128)(2,1)S(1)}, u32[]{:S(2)}, u32[]{:S(2)}) collective-permute-start(bf16[4,128,128]{2,1,0:T(8,128)(2,1)S(1)} %get-tuple-element.48), channel_id=1, source_target_pairs={{0,6},{1,7},{2,4},{3,5},{4,2},{5,3},{6,0},{7,1},{8,14},{9,15},{10,... | collective-permute-start | bytes 393224 | tf_op jit(solution)/shard_map/ppermute | solution.py:573
  48.5 7.3 %collective-permute-start.9 = (bf16[4,128,128]{2,1,0:T(8,128)(2,1)S(1)}, bf16[4,128,128]{2,1,0:T(8,128)(2,1)S(1)}, u32[]{:S(2)}, u32[]{:S(2)}) collective-permute-start(bf16[4,128,128]{2,1,0:T(8,128)(2,1)S(1)} %get-tuple-element.49), channel_id=1, source_target_pairs={{0,4},{1,5},{2,6},{3,7},{4,0},{5,1},{6,2},{7,3},{8,12},{9,13},{10,... | collective-permute-start | bytes 393224 | tf_op jit(solution)/shard_map/ppermute | solution.py:573
  55.9 4.8 %collective-permute-start.13 = (bf16[4,128,128]{2,1,0:T(8,128)(2,1)S(1)}, bf16[4,128,128]{2,1,0:T(8,128)(2,1)S(1)}, u32[]{:S(2)}, u32[]{:S(2)}) collective-permute-start(bf16[4,128,128]{2,1,0:T(8,128)(2,1)S(1)} %fusion), channel_id=1, source_target_pairs={{0,6},{1,7},{2,4},{3,5},{4,2},{5,3},{6,0},{7,1},{8,14},{9,15},{10,... | collective-permute-start | bytes 393224 | tf_op jit(solution)/shard_map/ppermute | solution.py:573
  58.4 6.0 %collective-permute-start.12 = (bf16[4,128,128]{2,1,0:T(8,128)(2,1)S(1)}, bf16[4,128,128]{2,1,0:T(8,128)(2,1)S(1)}, u32[]{:S(2)}, u32[]{:S(2)}) collective-permute-start(bf16[4,128,128]{2,1,0:T(8,128)(2,1)S(1)} %fusion), channel_id=1, source_target_pairs={{0,4},{1,5},{2,6},{3,7},{4,0},{5,1},{6,2},{7,3},{8,12},{9,13},{10,... | collective-permute-start | bytes 393224 | tf_op jit(solution)/shard_map/ppermute | solution.py:573
  58.6 5.8 %collective-permute-start.11 = (bf16[4,128,128]{2,1,0:T(8,128)(2,1)S(1)}, bf16[4,128,128]{2,1,0:T(8,128)(2,1)S(1)}, u32[]{:S(2)}, u32[]{:S(2)}) collective-permute-start(bf16[4,128,128]{2,1,0:T(8,128)(2,1)S(1)} %fusion), channel_id=1, source_target_pairs={{0,2},{1,3},{2,0},{3,1},{4,6},{5,7},{6,4},{7,5},{8,10},{9,11},{10,... | collective-permute-start | bytes 393224 | tf_op jit(solution)/shard_map/ppermute | solution.py:573
  64.4 4.7 %copy-start.8 = (bf16[16,128,128]{2,1,0:T(8,128)(2,1)}, bf16[16,128,128]{2,1,0:T(8,128)(2,1)S(1)}, u32[]{:S(2)}) copy-start(bf16[16,128,128]{2,1,0:T(8,128)(2,1)S(1)} %pad_maximum_fusion.even_in_ref) | copy-start | bytes 1572868
  64.4 4.7 %collective-permute-start.14 = (bf16[16,128,128]{2,1,0:T(8,128)(2,1)S(1)}, bf16[16,128,128]{2,1,0:T(8,128)(2,1)S(1)}, u32[]{:S(2)}, u32[]{:S(2)}) collective-permute-start(bf16[16,128,128]{2,1,0:T(8,128)(2,1)S(1)} %pad_maximum_fusion.even_in_ref), channel_id=1, source_target_pairs={{0,1},{1,0},{2,3},{3,2},{4,5},{5,4},{6,7},{7,6},{8,9},{9,8},{10,11... | collective-permute-start | bytes 1572872 | tf_op jit(solution)/shard_map/ppermute | solution.py:573
  69.1 0.8 copy-start.13
  78.0 21.1 %collective-permute-start.16 = (bf16[16,128,128]{2,1,0:T(8,128)(2,1)}, bf16[16,128,128]{2,1,0:T(8,128)(2,1)S(1)}, u32[]{:S(2)}, u32[]{:S(2)}) collective-permute-start(bf16[16,128,128]{2,1,0:T(8,128)(2,1)} %get-tuple-element.31.mine_ref.after_ref), channel_id=1, source_target_pairs={{0,8},{24,16},{1,9},{25,17},{2,10},{26,18},{3,11},{27,19},{4,12},{... | collective-permute-start | bytes 1572872 | tf_op jit(solution)/shard_map/ppermute | solution.py:548
  79.3 27.5 %collective-permute-start.18 = (bf16[16,128,128]{2,1,0:T(8,128)(2,1)}, bf16[16,128,128]{2,1,0:T(8,128)(2,1)S(1)}, u32[]{:S(2)}, u32[]{:S(2)}) collective-permute-start(bf16[16,128,128]{2,1,0:T(8,128)(2,1)} %get-tuple-element.32.mine_ref), channel_id=1, source_target_pairs={{0,8},{24,16},{1,9},{25,17},{2,10},{26,18},{3,11},{27,19},{4,12},{... | collective-permute-start | bytes 1572872 | tf_op jit(solution)/shard_map/ppermute | solution.py:548
  99.1 1.0 copy-start
  100.1 18.3 %copy-start.2 = (bf16[16,128,128]{2,1,0:T(8,128)(2,1)S(1)}, bf16[16,128,128]{2,1,0:T(8,128)(2,1)}, u32[]{:S(2)}) copy-start(bf16[16,128,128]{2,1,0:T(8,128)(2,1)} %get-tuple-element.30.mine_ref) | copy-start | bytes 1572868
  100.1 19.6 %copy-start.3 = (bf16[16,128,128]{2,1,0:T(8,128)(2,1)S(1)}, bf16[16,128,128]{2,1,0:T(8,128)(2,1)}, u32[]{:S(2)}) copy-start(bf16[16,128,128]{2,1,0:T(8,128)(2,1)} %get-tuple-element.33.mine_ref) | copy-start | bytes 1572868
  100.3 15.9 %collective-permute-start.17 = (bf16[16,128,128]{2,1,0:T(8,128)(2,1)S(1)}, bf16[16,128,128]{2,1,0:T(8,128)(2,1)S(1)}, u32[]{:S(2)}, u32[]{:S(2)}) collective-permute-start(bf16[16,128,128]{2,1,0:T(8,128)(2,1)S(1)} %merge.8.after_ref.mine_ref), channel_id=1, source_target_pairs={{8,16},{16,8},{9,17},{17,9},{10,18},{18,10},{11,19},{19,11},{12,20... | collective-permute-start | bytes 1572872 | tf_op jit(solution)/shard_map/ppermute | solution.py:569
  102.3 17.4 %collective-permute-start.21 = (bf16[16,128,128]{2,1,0:T(8,128)(2,1)}, bf16[16,128,128]{2,1,0:T(8,128)(2,1)S(1)}, u32[]{:S(2)}, u32[]{:S(2)}) collective-permute-start(bf16[16,128,128]{2,1,0:T(8,128)(2,1)} %get-tuple-element.33.mine_ref), channel_id=1, source_target_pairs={{0,8},{24,16},{1,9},{25,17},{2,10},{26,18},{3,11},{27,19},{4,12},{... | collective-permute-start | bytes 1572872 | tf_op jit(solution)/shard_map/ppermute | solution.py:548
  106.8 1.0 copy-start.4
  107.9 19.3 %collective-permute-start.20 = (bf16[16,128,128]{2,1,0:T(8,128)(2,1)S(1)}, bf16[16,128,128]{2,1,0:T(8,128)(2,1)}, u32[]{:S(2)}, u32[]{:S(2)}) collective-permute-start(bf16[16,128,128]{2,1,0:T(8,128)(2,1)S(1)} %merge.9.after_ref.mine_ref), channel_id=1, source_target_pairs={{8,16},{16,8},{9,17},{17,9},{10,18},{18,10},{11,19},{19,11},{12,20... | collective-permute-start | bytes 1572872 | tf_op jit(solution)/shard_map/ppermute | solution.py:569
  116.3 13.5 %collective-permute-start.19 = (bf16[16,128,128]{2,1,0:T(8,128)(2,1)S(1)}, bf16[16,128,128]{2,1,0:T(8,128)(2,1)}, u32[]{:S(2)}, u32[]{:S(2)}) collective-permute-start(bf16[16,128,128]{2,1,0:T(8,128)(2,1)S(1)} %merge.10.after_ref.mine_ref), channel_id=1, source_target_pairs={{8,0},{16,24},{9,1},{17,25},{10,2},{18,26},{11,3},{19,27},{12,4},{... | collective-permute-start | bytes 1572872 | tf_op jit(solution)/shard_map/ppermute | solution.py:569
  118.4 15.4 %collective-permute-start.15 = (bf16[16,128,128]{2,1,0:T(8,128)(2,1)S(1)}, bf16[16,128,128]{2,1,0:T(8,128)(2,1)S(1)}, u32[]{:S(2)}, u32[]{:S(2)}) collective-permute-start(bf16[16,128,128]{2,1,0:T(8,128)(2,1)S(1)} %copy-done.2), channel_id=1, source_target_pairs={{0,8},{24,16},{1,9},{25,17},{2,10},{26,18},{3,11},{27,19},{4,12},{... | collective-permute-start | bytes 1572872 | tf_op jit(solution)/shard_map/ppermute | solution.py:548
  119.8 18.0 %collective-permute-start.24 = (bf16[16,128,128]{2,1,0:T(8,128)(2,1)S(1)}, bf16[16,128,128]{2,1,0:T(8,128)(2,1)S(1)}, u32[]{:S(2)}, u32[]{:S(2)}) collective-permute-start(bf16[16,128,128]{2,1,0:T(8,128)(2,1)S(1)} %merge.11.after_ref.mine_ref), channel_id=1, source_target_pairs={{8,16},{16,8},{9,17},{17,9},{10,18},{18,10},{11,19},{19,11},{12,20... | collective-permute-start | bytes 1572872 | tf_op jit(solution)/shard_map/ppermute | solution.py:569
  128.4 13.0 %collective-permute-start.23 = (bf16[16,128,128]{2,1,0:T(8,128)(2,1)S(1)}, bf16[16,128,128]{2,1,0:T(8,128)(2,1)S(1)}, u32[]{:S(2)}, u32[]{:S(2)}) collective-permute-start(bf16[16,128,128]{2,1,0:T(8,128)(2,1)S(1)} %merge.12.after_ref.token_ref.mine_ref), channel_id=1, source_target_pairs={{8,0},{16,24},{9,1},{17,25},{10,2},{18,26},{11,3},{19,27},{12,4},{... | collective-permute-start | bytes 1572872 | tf_op jit(solution)/shard_map/ppermute | solution.py:569
  131.0 14.6 %collective-permute-start.27 = (bf16[16,128,128]{2,1,0:T(8,128)(2,1)S(1)}, bf16[16,128,128]{2,1,0:T(8,128)(2,1)S(1)}, u32[]{:S(2)}, u32[]{:S(2)}) collective-permute-start(bf16[16,128,128]{2,1,0:T(8,128)(2,1)S(1)} %pick.4.after_ref), channel_id=1, source_target_pairs={{0,6},{1,7},{2,4},{3,5},{4,2},{5,3},{6,0},{7,1},{8,14},{9,15},{10,... | collective-permute-start | bytes 1572872 | tf_op jit(solution)/shard_map/ppermute | solution.py:573
  133.9 17.2 %copy-start.1 = (bf16[128,256]{1,0:T(8,128)(2,1)S(1)}, bf16[128,256]{1,0:T(8,128)(2,1)}, u32[]{:S(2)}) copy-start(bf16[128,256]{1,0:T(8,128)(2,1)} %constant.19.clone.refs_2_) | copy-start | bytes 196612
  133.9 17.2 %copy-start.5 = (s32[1,64]{1,0:T(1,128)S(1)}, s32[1,64]{1,0:T(1,128)}, u32[]{:S(2)}) copy-start(s32[1,64]{1,0:T(1,128)} %refs_1_.7) | copy-start | bytes 772
  133.9 15.6 %collective-permute-start.22 = (bf16[16,128,128]{2,1,0:T(8,128)(2,1)S(1)}, bf16[16,128,128]{2,1,0:T(8,128)(2,1)S(1)}, u32[]{:S(2)}, u32[]{:S(2)}) collective-permute-start(bf16[16,128,128]{2,1,0:T(8,128)(2,1)S(1)} %merge.13.after_ref.mine_ref), channel_id=1, source_target_pairs={{8,16},{16,8},{9,17},{17,9},{10,18},{18,10},{11,19},{19,11},{12,20... | collective-permute-start | bytes 1572872 | tf_op jit(solution)/shard_map/ppermute | solution.py:569
  137.9 16.6 %collective-permute-start.26 = (bf16[16,128,128]{2,1,0:T(8,128)(2,1)S(1)}, bf16[16,128,128]{2,1,0:T(8,128)(2,1)S(1)}, u32[]{:S(2)}, u32[]{:S(2)}) collective-permute-start(bf16[16,128,128]{2,1,0:T(8,128)(2,1)S(1)} %merge.14.after_ref.token_ref.mine_ref), channel_id=1, source_target_pairs={{8,0},{16,24},{9,1},{17,25},{10,2},{18,26},{11,3},{19,27},{12,4},{... | collective-permute-start | bytes 1572872 | tf_op jit(solution)/shard_map/ppermute | solution.py:569
  141.5 13.4 %collective-permute-start.29 = (bf16[16,128,128]{2,1,0:T(8,128)(2,1)S(1)}, bf16[16,128,128]{2,1,0:T(8,128)(2,1)S(1)}, u32[]{:S(2)}, u32[]{:S(2)}) collective-permute-start(bf16[16,128,128]{2,1,0:T(8,128)(2,1)S(1)} %pick.5.after_ref), channel_id=1, source_target_pairs={{0,2},{1,3},{2,0},{3,1},{4,6},{5,7},{6,4},{7,5},{8,10},{9,11},{10,... | collective-permute-start | bytes 1572872 | tf_op jit(solution)/shard_map/ppermute | solution.py:573
  145.6 5.5 %collective-permute-start.28 = (bf16[8,128,128]{2,1,0:T(8,128)(2,1)S(1)}, bf16[8,128,128]{2,1,0:T(8,128)(2,1)S(1)}, u32[]{:S(2)}, u32[]{:S(2)}) collective-permute-start(bf16[8,128,128]{2,1,0:T(8,128)(2,1)S(1)} %slice.51), channel_id=1, source_target_pairs={{0,1},{1,0},{2,3},{3,2},{4,5},{5,4},{6,7},{7,6},{8,9},{9,8},{10,11... | collective-permute-start | bytes 786440 | tf_op jit(solution)/shard_map/ppermute | solution.py:573
  149.6 13.3 %collective-permute-start.25 = (bf16[16,128,128]{2,1,0:T(8,128)(2,1)S(1)}, bf16[16,128,128]{2,1,0:T(8,128)(2,1)S(1)}, u32[]{:S(2)}, u32[]{:S(2)}) collective-permute-start(bf16[16,128,128]{2,1,0:T(8,128)(2,1)S(1)} %merge.15.after_ref.mine_ref), channel_id=1, source_target_pairs={{8,0},{16,24},{9,1},{17,25},{10,2},{18,26},{11,3},{19,27},{12,4},{... | collective-permute-start | bytes 1572872 | tf_op jit(solution)/shard_map/ppermute | solution.py:569
  154.7 14.5 %copy-start.12 = (bf16[32,128,128]{2,1,0:T(8,128)(2,1)S(1)}, bf16[32,128,128]{2,1,0:T(8,128)(2,1)}, u32[]{:S(2)}) copy-start(bf16[32,128,128]{2,1,0:T(8,128)(2,1)} %get-tuple-element.29) | copy-start | bytes 3145732
  154.7 12.7 %collective-permute-start.32 = (bf16[16,128,128]{2,1,0:T(8,128)(2,1)S(1)}, bf16[16,128,128]{2,1,0:T(8,128)(2,1)S(1)}, u32[]{:S(2)}, u32[]{:S(2)}) collective-permute-start(bf16[16,128,128]{2,1,0:T(8,128)(2,1)S(1)} %pick.6.after_ref), channel_id=1, source_target_pairs={{0,4},{1,5},{2,6},{3,7},{4,0},{5,1},{6,2},{7,3},{8,12},{9,13},{10,... | collective-permute-start | bytes 1572872 | tf_op jit(solution)/shard_map/ppermute | solution.py:573
  155.0 1.8 %collective-permute-start.30 = (bf16[8,128,128]{2,1,0:T(8,128)(2,1)S(1)}, bf16[8,128,128]{2,1,0:T(8,128)(2,1)S(1)}, u32[]{:S(2)}, u32[]{:S(2)}) collective-permute-start(bf16[8,128,128]{2,1,0:T(8,128)(2,1)S(1)} %slice.52), channel_id=1, source_target_pairs={{0,1},{1,0},{2,3},{3,2},{4,5},{5,4},{6,7},{7,6},{8,9},{9,8},{10,11... | collective-permute-start | bytes 786440 | tf_op jit(solution)/shard_map/ppermute | solution.py:573
  163.1 11.5 %collective-permute-start.31 = (bf16[8,128,128]{2,1,0:T(8,128)(2,1)S(1)}, bf16[8,128,128]{2,1,0:T(8,128)(2,1)S(1)}, u32[]{:S(2)}, u32[]{:S(2)}) collective-permute-start(bf16[8,128,128]{2,1,0:T(8,128)(2,1)S(1)} %get-tuple-element.38), channel_id=1, source_target_pairs={{0,1},{1,0},{2,3},{3,2},{4,5},{5,4},{6,7},{7,6},{8,9},{9,8},{10,11... | collective-permute-start | bytes 786440 | tf_op jit(solution)/shard_map/ppermute | solution.py:573
  167.4 3.3 %collective-permute-start.33 = (bf16[8,128,128]{2,1,0:T(8,128)(2,1)S(1)}, bf16[8,128,128]{2,1,0:T(8,128)(2,1)S(1)}, u32[]{:S(2)}, u32[]{:S(2)}) collective-permute-start(bf16[8,128,128]{2,1,0:T(8,128)(2,1)S(1)} %slice.53), channel_id=1, source_target_pairs={{0,1},{1,0},{2,3},{3,2},{4,5},{5,4},{6,7},{7,6},{8,9},{9,8},{10,11... | collective-permute-start | bytes 786440 | tf_op jit(solution)/shard_map/ppermute | solution.py:573
where the time goes:
time: 179 us
  waiting for transfers between devices  76.4 us (43%)
  Pallas kernels  55 us (31%)
  starting transfers between devices  38.4 us (21%)
  local copies, waits for them, and re-layouts  3.81 us (2%)
  other arithmetic  3.06 us (2%)
  between operations  1.96 us (1%)
    ppermute x22, waiting for transfers between devices, swap(): lax.ppermute(piece, axis, [(c, c ^ offset) for c in range(lax.axis_size(a...  31.2 us
    ppermute x4, waiting for transfers between devices, line_sums(): got = [lax.ppermute(part, axis, stages[0][0]) for part in parts]  24.4 us
    ppermute x8, waiting for transfers between devices, line_sums(): got[k] = lax.ppermute(state[k], axis, stages[s + 1][0])  20.9 us
    ppermute x22, starting transfers between devices, swap(): lax.ppermute(piece, axis, [(c, c ^ offset) for c in range(lax.axis_size(a...  17.5 us
    ppermute x8, starting transfers between devices, line_sums(): got[k] = lax.ppermute(state[k], axis, stages[s + 1][0])  15.7 us
    pallas_call x4, Pallas kernels, finish(): pl.pallas_call(lambda *refs: finish_body(*refs, offset=offset), out_shape...  14.5 us
    pallas_call x1, Pallas kernels, smoothing(): pl.pallas_call(smooth_body, out_shape=jax.ShapeDtypeStruct((cells, width)...  13.3 us
    pallas_call x1, Pallas kernels, adjoint(): pl.pallas_call(adjoint_body, out_shape=[jax.ShapeDtypeStruct((2 * piece[0...  8.02 us
  transfers between devices with their start and end apart: 34, of which 22 were waited for; matrix products, arithmetic and copies ran while one was open for 1% of the time, Pallas kernels for 17%

commit v1 on v0

--- a/solution.py
+++ b/solution.py
@@ -47,8 +47,17 @@
             held_ref.at[pl.ds((me ^ offset) * each, each)],
             sems.at[offset],
         )
-        for offset, (ref, first) in enumerate(sources)
+        for ref, first, offset in sources
     ]
+
+
+def far_first(peers):
+    return sorted(range(1, peers // 2), key=lambda j: (-bin(j).count("1"), j))
+
+
+def wave_offsets(peers):
+    far = far_first(peers)
+    return [0, 1, *[2 * j for j in far], *[2 * j + 1 for j in far]]
 
 
 def piece_stores(source, offset, even_refs, odd_ref, sems):
@@ -153,7 +162,7 @@
     )(me, order, model_blocks)
 
 
-def slot_loop(count, sens_ref, block_ref, sems, others, acc_ref, work):
+def slot_loop(count, sens_ref, block_ref, sems, others, acc_ref, work, then=()):
     steps = sems.shape[0]
     each = sens_ref.shape[0] // steps
 
@@ -170,6 +179,7 @@
 
     acc_ref[...] = jnp.zeros_like(acc_ref)
     wait_all(others)
+    start_all(then)
 
     @pl.loop(0, needed)
     def _(step):
@@ -192,7 +202,8 @@
             block, held_ref[cols_ref[0, slot]], preferred_element_type=jnp.float32
         )
 
-    waves = gather_pieces([(ref, 0) for ref in wave_refs], held_ref, me, got)
+    sources = [(ref, 0, offset) for ref, offset in zip(wave_refs, wave_offsets(peers))]
+    waves = gather_pieces(sources, held_ref, me, got)
     slot_loop(count_ref[0, 0], sens_ref, block_ref, sems, waves, acc_ref, work)
     stores = []
     for offset in [*range(1, peers, 2), *range(0, peers, 2)]:
@@ -252,19 +263,19 @@
 
     each_in = held_ref.shape[0] // peers
     sources = [
-        (odd_in_ref if o % 2 else even_in_ref, o // 2 * each_in) for o in range(peers)
+        (ref, i * each_in, 2 * j + odd)
+        for i, j in enumerate([0, *far_first(peers)])
+        for odd, ref in enumerate((even_in_ref, odd_in_ref))
     ]
     images = gather_pieces(sources, held_ref, me, got)
-    slot_loop(count_ref[0, 0], sens_ref, block_ref, sems, images, acc_ref, work)
-    stores = []
+    stores = fetch(held_ref, image_ref, whole, whole.shape[0])
+    slot_loop(count_ref[0, 0], sens_ref, block_ref, sems, images, acc_ref, work, stores)
     for offset in reversed(range(peers)):
         part = acc_ref[pl.ds((me ^ offset) * each, each)]
         half_ref[offset] = part.astype(half_ref.dtype)
         target = out_refs[offset // 2].at[pl.ds(offset % 2 * each, each)]
         stores.append(pltpu.make_async_copy(half_ref.at[offset], target, put.at[offset]))
         stores[-1].start()
-    stores.extend(fetch(held_ref, image_ref, whole, whole.shape[0]))
-    start_all(stores[peers:])
     wait_all(stores)
 
 
@@ -583,18 +594,16 @@
     me = col.reshape(1)
     offset = (col * cell_count - RIM).reshape(1)
     sens = sens_blocks[0]
-    evens = range(1, half)
+    far = far_first(peers)
 
     *own, odd = analyze(me, send_order, model_dir.reshape(blocks, BLK, width), peers)
     partner = swap(odd, "cols", 1)
-    direct = {j: swap(own[j], "cols", 2 * j) for j in reversed(evens)}
+    direct = {j: swap(own[j], "cols", 2 * j) for j in far}
     passed = {
         j: swap(partner[j * (per_peer + 1) : (j + 1) * (per_peer + 1)], "cols", 2 * j)
-        for j in reversed(evens)
+        for j in far
     }
-    waves = [own[0], partner]
-    for j in evens:
-        waves += [direct[j], passed[j]]
+    waves = [own[0], partner, *[direct[j] for j in far], *[passed[j] for j in far]]
     smooth = smoothing(offset, model_dir, neighbors, face_weight, partner)
 
     even_rows, odd_rows = forward(
@@ -602,15 +611,15 @@
     )
     pair = (even_rows + swap(odd_rows, "cols", 1)).reshape(half, -1, BLK, width)
     to_send = pair.astype(jnp.bfloat16)
-    shares = [swap(to_send[j], "cols", 2 * j) for j in evens]
+    shares = [swap(to_send[j], "cols", 2 * j) for j in far]
     total = pair[0] + sum(share.astype(jnp.float32) for share in shares)
     image_share = total.astype(jnp.bfloat16)
     even_image = jnp.concatenate(
-        [image_share] + [swap(image_share, "cols", 2 * j) for j in evens], axis=0
+        [image_share] + [swap(image_share, "cols", 2 * j) for j in far], axis=0
     )
     odd_image = swap(even_image, "cols", 1)
     smooth = edges(
-        me, offset, model_dir, neighbors, face_weight, smooth, to_send, waves[1::2]
+        me, offset, model_dir, neighbors, face_weight, smooth, to_send, [partner, *[passed[j] for j in range(1, half)]]
     )
 
     partial_cols, image = adjoint(
@@ -618,18 +627,18 @@
     )
     data_image = image.reshape(RB_DEV * BLK, width).astype(jnp.float32)
     normal = smooth.reshape(blocks, BLK, width)
-    order = sorted(range(half), key=lambda j: (-bin(j).count("1"), j))
+    order = [*far, 0]
     waiting, tokens = [], []
 
-    def end_one():
+    def end_one(place):
         nonlocal normal
-        even, odd_piece, j = waiting.pop(0)
+        even, odd_piece, j = waiting.pop(place)
         normal, token = finish(me, send_order, even, odd_piece, normal, 2 * j)
         tokens.append(token)
 
     def deliver(k, take, got, mine, after):
         if k >= 2:
-            end_one()
+            end_one(0)
         token = tokens[-1] if tokens else after
         j = order[k]
         if j:
@@ -644,7 +653,7 @@
 
     line_sums([partial_cols[j] for j in order], "rows", deliver)
     while waiting:
-        end_one()
+        end_one(-1)
     return (data_image, normal.reshape(cell_count, width))
 
 

time: 179 us -> 181 us (1.011)
  the two profiles are of different devices: /device:TPU:11 before, /device:TPU:0 now
where the time goes in v1:
time: 181 us; the launch traced here: 180 us
  Pallas kernels  62 us (34%)
  starting transfers between devices  61 us (34%)
  waiting for transfers between devices  48.1 us (27%)
  local copies, waits for them, and re-layouts  3.87 us (2%)
  other arithmetic  3.06 us (2%)
  between operations  2.03 us (1%)
    ppermute x22, starting transfers between devices, swap(): lax.ppermute(piece, axis, [(c, c ^ offset) for c in range(lax.axis_size(a...  38 us
    ppermute x22, waiting for transfers between devices, swap(): lax.ppermute(piece, axis, [(c, c ^ offset) for c in range(lax.axis_size(a...  25.5 us
    ppermute x4, waiting for transfers between devices, line_sums(): got = [lax.ppermute(part, axis, stages[0][0]) for part in parts]  16.6 us
    pallas_call x4, Pallas kernels, finish(): pl.pallas_call(lambda *refs: finish_body(*refs, offset=offset), out_shape...  14.5 us
    ppermute x4, starting transfers between devices, line_sums(): got = [lax.ppermute(part, axis, stages[0][0]) for part in parts]  13.8 us
    pallas_call x1, Pallas kernels, smoothing(): pl.pallas_call(smooth_body, out_shape=jax.ShapeDtypeStruct((cells, width)...  13.3 us
    pallas_call x1, Pallas kernels, adjoint(): pl.pallas_call(adjoint_body, out_shape=[jax.ShapeDtypeStruct((2 * piece[0...  11.5 us
    pallas_call x1, Pallas kernels, forward(): pl.pallas_call(forward_body, out_shape=[jax.ShapeDtypeStruct(half, jnp.fl...  11 us
  transfers between devices with their start and end apart: 34, of which 16 were waited for; matrix products, arithmetic and copies ran while one was open for 1% of the time, Pallas kernels for 17%

profile of v1, /device:TPU:0, one launch (start us, length us, event | category | flops | bytes accessed | tf_op | source)
XLA Modules:
  0.0 180.1 jit_solution(10231574299448941102)
XLA Ops:
  0.6 5.0 %analyze.1 = (bf16[8,128,128]{2,1,0:T(8,128)(2,1)}, bf16[8,128,128]{2,1,0:T(8,128)(2,1)}, bf16[8,128,128]{2,1,0:T(8,128)(2,1)}, bf16[8,128,128]{2,1,0:T(8,128)(2,1)}, bf16[36,128,128]{2,1,0:T(8,128)(2,1)}) custom-call(s32[1]{0:T(128)} %bitcast.me_ref.refs_0_, s32[1,64]{1,0:T(1,128)} %refs_1_.7, f32[64,128,128]{2,1,0:T(8,128)} %bitcast.15), custom_call_target="tpu_custom_call" | custom-call | flops 536870912 | bytes 6291456 | tf_op jit(solution)/shard_map/analyze/pallas_call | solution.py:145
  5.6 0.5 collective-permute-start
  6.1 3.5 %collective-permute-start.1 = (bf16[8,128,128]{2,1,0:T(8,128)(2,1)}, bf16[8,128,128]{2,1,0:T(8,128)(2,1)S(1)}, u32[]{:S(2)}, u32[]{:S(2)}) collective-permute-start(bf16[8,128,128]{2,1,0:T(8,128)(2,1)} %get-tuple-element.24), channel_id=1, source_target_pairs={{0,6},{1,7},{2,4},{3,5},{4,2},{5,3},{6,0},{7,1},{8,14},{9,15},{10,... | collective-permute-start | bytes 786440 | tf_op jit(solution)/shard_map/ppermute | solution.py:584
  9.7 0.5 collective-permute-start.2
  10.2 0.1 collective-permute-start.3
  11.1 2.9 %collective-permute-start.4 = (bf16[9,128,128]{2,1,0:T(8,128)(2,1)S(1)}, bf16[9,128,128]{2,1,0:T(8,128)(2,1)S(1)}, u32[]{:S(2)}, u32[]{:S(2)}) collective-permute-start(bf16[9,128,128]{2,1,0:T(8,128)(2,1)S(1)} %get-tuple-element.46), channel_id=1, source_target_pairs={{0,6},{1,7},{2,4},{3,5},{4,2},{5,3},{6,0},{7,1},{8,14},{9,15},{10,... | collective-permute-start | bytes 884744 | tf_op jit(solution)/shard_map/ppermute | solution.py:584
  14.0 0.5 collective-permute-start.5
  14.5 2.6 %collective-permute-done.1.refs_2_ = bf16[8,128,128]{2,1,0:T(8,128)(2,1)S(1)} collective-permute-done((bf16[8,128,128]{2,1,0:T(8,128)(2,1)}, bf16[8,128,128]{2,1,0:T(8,128)(2,1)S(1)}, u32[]{:S(2)}, u32[]{:S(2)}) %collective-permute-start.1) | collective-permute-done | bytes 262176 | tf_op jit(solution)/shard_map/ppermute | solution.py:584
  17.1 1.9 %collective-permute-start.6 = (bf16[9,128,128]{2,1,0:T(8,128)(2,1)S(1)}, bf16[9,128,128]{2,1,0:T(8,128)(2,1)S(1)}, u32[]{:S(2)}, u32[]{:S(2)}) collective-permute-start(bf16[9,128,128]{2,1,0:T(8,128)(2,1)S(1)} %get-tuple-element.44), channel_id=1, source_target_pairs={{0,4},{1,5},{2,6},{3,7},{4,0},{5,1},{6,2},{7,3},{8,12},{9,13},{10,... | collective-permute-start | bytes 884744 | tf_op jit(solution)/shard_map/ppermute | solution.py:584
  19.0 13.3 %smoothing.1.refs_8_.base_ref = f32[8192,128]{1,0:T(8,128)} custom-call(s32[1]{0:T(128)} %bitcast.3.offset_ref, f32[8192,128]{1,0:T(8,128)} %model_ref.3, s32[4,8192]{1,0:T(4,128)} %near_ref.3, f32[4,8192]{1,0:T(4,128)} %weight_ref.3, bf16[36,128,128]{2,1,0:T(8,128)(2,1)} %copy-done.6), custom_call_target="tpu_custom_call" | custom-call | flops 3221225472 | bytes 16777216 | tf_op jit(solution)/shard_map/smoothing/pallas_call | solution.py:367
  32.4 3.0 %collective-permute-done.5.refs_6_.refs_1_ = bf16[9,128,128]{2,1,0:T(8,128)(2,1)S(1)} collective-permute-done((bf16[9,128,128]{2,1,0:T(8,128)(2,1)S(1)}, bf16[9,128,128]{2,1,0:T(8,128)(2,1)S(1)}, u32[]{:S(2)}, u32[]{:S(2)}) %collective-permute-start.5) | collective-permute-done | bytes 294944 | tf_op jit(solution)/shard_map/ppermute | solution.py:584
  35.4 0.7 copy-done.10
  36.2 11.0 %forward.1 = (f32[16,128,128]{2,1,0:T(8,128)}, f32[16,128,128]{2,1,0:T(8,128)}) custom-call(s32[1]{0:T(128)} %bitcast.me_ref.refs_0_, s32[1,384]{1,0:T(1,128)} %rows_ref.3, s32[1,384]{1,0:T(1,128)} %cols_ref.3, s32[1,1]{1,0:T(1,128)S(6)} %copy.24.count_ref, bf16[384,128,128]{2,1,0:T(8,128)(2,1)} %bitcast.13, bf16[8,128,128]{2,1,0:T(8,128)(2,1)} %get-tuple-element.22.refs_0_, ...), custom_call_target="tpu_custom_call" | custom-call | flops 1610612736 | bytes 12582912 | tf_op jit(solution)/shard_map/forward/pallas_call | solution.py:227
  47.3 2.9 %collective-permute-done.7 = f32[16,128,128]{2,1,0:T(8,128)S(1)} collective-permute-done((f32[16,128,128]{2,1,0:T(8,128)}, f32[16,128,128]{2,1,0:T(8,128)S(1)}, u32[]{:S(2)}, u32[]{:S(2)}) %collective-permute-start.7) | collective-permute-done | bytes 1048608 | tf_op jit(solution)/shard_map/ppermute | solution.py:584
  50.1 1.4 fusion.1
  51.7 3.4 %collective-permute-start.9 = (bf16[4,128,128]{2,1,0:T(8,128)(2,1)S(1)}, bf16[4,128,128]{2,1,0:T(8,128)(2,1)S(1)}, u32[]{:S(2)}, u32[]{:S(2)}) collective-permute-start(bf16[4,128,128]{2,1,0:T(8,128)(2,1)S(1)} %get-tuple-element.49), channel_id=1, source_target_pairs={{0,2},{1,3},{2,0},{3,1},{4,6},{5,7},{6,4},{7,5},{8,10},{9,11},{10,... | collective-permute-start | bytes 393224 | tf_op jit(solution)/shard_map/ppermute | solution.py:584
  55.1 4.9 %collective-permute-done.10 = bf16[4,128,128]{2,1,0:T(8,128)(2,1)S(1)} collective-permute-done((bf16[4,128,128]{2,1,0:T(8,128)(2,1)S(1)}, bf16[4,128,128]{2,1,0:T(8,128)(2,1)S(1)}, u32[]{:S(2)}, u32[]{:S(2)}) %collective-permute-start.10) | collective-permute-done | bytes 131104 | tf_op jit(solution)/shard_map/ppermute | solution.py:584
  60.0 1.2 collective-permute-done.9
  61.3 0.3 collective-permute-start.11
  61.6 1.6 collective-permute-start.12
  63.2 1.7 collective-permute-start.13
  64.8 3.4 %collective-permute-done.11 = bf16[4,128,128]{2,1,0:T(8,128)(2,1)S(1)} collective-permute-done((bf16[4,128,128]{2,1,0:T(8,128)(2,1)S(1)}, bf16[4,128,128]{2,1,0:T(8,128)(2,1)S(1)}, u32[]{:S(2)}, u32[]{:S(2)}) %collective-permute-start.11) | collective-permute-done | bytes 131104 | tf_op jit(solution)/shard_map/ppermute | solution.py:584
  68.2 0.5 collective-permute-done.12
  68.7 0.8 collective-permute-done.13
  69.7 3.2 %edges.1.after_ref = f32[8192,128]{1,0:T(8,128)} custom-call(s32[1]{0:T(128)} %bitcast.me_ref.refs_0_, s32[1]{0:T(128)} %bitcast.3.offset_ref, f32[8192,128]{1,0:T(8,128)} %model_ref.3, s32[4,8192]{1,0:T(4,128)} %near_ref.3, f32[4,8192]{1,0:T(4,128)} %weight_ref.3, f32[8192,128]{1,0:T(8,128)} %smoothing.1.refs_8_.base_ref, ...), custom_call_target="tpu_custom_call", output_to_operand_aliasing={{}: (5, {})} | custom-call | flops 100663296 | bytes 524288 | tf_op jit(solution)/shard_map/edges/pallas_call | solution.py:431
  72.9 0.8 copy-done.13
  73.7 11.5 %adjoint.1 = (bf16[16,128,128]{2,1,0:T(8,128)(2,1)}, bf16[16,128,128]{2,1,0:T(8,128)(2,1)}, bf16[16,128,128]{2,1,0:T(8,128)(2,1)}, bf16[16,128,128]{2,1,0:T(8,128)(2,1)}, bf16[32,128,128]{2,1,0:T(8,128)(2,1)}) custom-call(s32[1]{0:T(128)} %bitcast.me_ref.refs_0_, s32[1,384]{1,0:T(1,128)} %rows_ref.3, s32[1,384]{1,0:T(1,128)} %cols_ref.3, ...), custom_call_target="tpu_custom_call" | custom-call | flops 1610612736 | bytes 12582912 | tf_op jit(solution)/shard_map/adjoint/pallas_call | solution.py:287
  85.2 1.3 collective-permute-start.16
  86.5 1.3 collective-permute-start.18
  87.9 11.3 %collective-permute-done.16.got_ref = bf16[16,128,128]{2,1,0:T(8,128)(2,1)S(1)} collective-permute-done((bf16[16,128,128]{2,1,0:T(8,128)(2,1)}, bf16[16,128,128]{2,1,0:T(8,128)(2,1)S(1)}, u32[]{:S(2)}, u32[]{:S(2)}) %collective-permute-start.16) | collective-permute-done | bytes 524320 | tf_op jit(solution)/shard_map/ppermute | solution.py:559
  99.2 1.0 copy-done
  100.3 0.8 collective-permute-start.17
  101.2 5.5 %collective-permute-start.15 = (bf16[16,128,128]{2,1,0:T(8,128)(2,1)}, bf16[16,128,128]{2,1,0:T(8,128)(2,1)S(1)}, u32[]{:S(2)}, u32[]{:S(2)}) collective-permute-start(bf16[16,128,128]{2,1,0:T(8,128)(2,1)} %get-tuple-element.30.mine_ref), channel_id=1, source_target_pairs={{0,8},{24,16},{1,9},{25,17},{2,10},{26,18},{3,11},{27,19},{4,12},{... | collective-permute-start | bytes 1572872 | tf_op jit(solution)/shard_map/ppermute | solution.py:559
  106.7 3.7 %collective-permute-done.18.got_ref = bf16[16,128,128]{2,1,0:T(8,128)(2,1)S(1)} collective-permute-done((bf16[16,128,128]{2,1,0:T(8,128)(2,1)}, bf16[16,128,128]{2,1,0:T(8,128)(2,1)S(1)}, u32[]{:S(2)}, u32[]{:S(2)}) %collective-permute-start.18) | collective-permute-done | bytes 524320 | tf_op jit(solution)/shard_map/ppermute | solution.py:559
  110.4 1.0 copy-done.4
  111.6 1.5 collective-permute-start.22
  113.2 1.3 collective-permute-start.21
  114.5 5.6 %collective-permute-start.20 = (bf16[16,128,128]{2,1,0:T(8,128)(2,1)S(1)}, bf16[16,128,128]{2,1,0:T(8,128)(2,1)S(1)}, u32[]{:S(2)}, u32[]{:S(2)}) collective-permute-start(bf16[16,128,128]{2,1,0:T(8,128)(2,1)S(1)} %copy-done.2), channel_id=1, source_target_pairs={{0,8},{24,16},{1,9},{25,17},{2,10},{26,18},{3,11},{27,19},{4,12},{... | collective-permute-start | bytes 1572872 | tf_op jit(solution)/shard_map/ppermute | solution.py:559
  120.1 1.6 collective-permute-done.15.got_ref
  121.8 0.7 collective-permute-start.19
  122.5 1.2 merge.12.after_ref.token_ref.mine_ref
  123.7 1.3 collective-permute-start.25
  125.0 0.3 collective-permute-done.21.got_ref
  125.3 1.2 pick.4.after_ref
  126.4 12.0 %collective-permute-start.26 = (bf16[16,128,128]{2,1,0:T(8,128)(2,1)S(1)}, bf16[16,128,128]{2,1,0:T(8,128)(2,1)S(1)}, u32[]{:S(2)}, u32[]{:S(2)}) collective-permute-start(bf16[16,128,128]{2,1,0:T(8,128)(2,1)S(1)} %pick.4.after_ref), channel_id=1, source_target_pairs={{0,6},{1,7},{2,4},{3,5},{4,2},{5,3},{6,0},{7,1},{8,14},{9,15},{10,... | collective-permute-start | bytes 1572872 | tf_op jit(solution)/shard_map/ppermute | solution.py:584
  138.6 0.8 collective-permute-start.24
  139.4 0.1 merge.14.after_ref.token_ref.mine_ref
  139.5 1.3 collective-permute-start.23
  140.8 0.1 pick.5.after_ref
  141.0 7.9 %collective-permute-start.31 = (bf16[16,128,128]{2,1,0:T(8,128)(2,1)S(1)}, bf16[16,128,128]{2,1,0:T(8,128)(2,1)S(1)}, u32[]{:S(2)}, u32[]{:S(2)}) collective-permute-start(bf16[16,128,128]{2,1,0:T(8,128)(2,1)S(1)} %pick.5.after_ref), channel_id=1, source_target_pairs={{0,2},{1,3},{2,0},{3,1},{4,6},{5,7},{6,4},{7,5},{8,10},{9,11},{10,... | collective-permute-start | bytes 1572872 | tf_op jit(solution)/shard_map/ppermute | solution.py:584
  148.9 1.9 %collective-permute-done.26.refs_3_ = bf16[16,128,128]{2,1,0:T(8,128)(2,1)S(1)} collective-permute-done((bf16[16,128,128]{2,1,0:T(8,128)(2,1)S(1)}, bf16[16,128,128]{2,1,0:T(8,128)(2,1)S(1)}, u32[]{:S(2)}, u32[]{:S(2)}) %collective-permute-start.26) | collective-permute-done | bytes 524320 | tf_op jit(solution)/shard_map/ppermute | solution.py:584
  151.1 1.5 collective-permute-start.30
  152.6 3.3 %finish.4 = (f32[64,128,128]{2,1,0:T(8,128)}, f32[8,128]{1,0:T(8,128)S(1)}) custom-call(s32[1]{0:T(128)} %bitcast.me_ref.refs_0_, s32[1,64]{1,0:T(1,128)S(1)} %copy-done.5, bf16[128,256]{1,0:T(8,128)(2,1)S(1)} %copy-done.1, bf16[16,128,128]{2,1,0:T(8,128)(2,1)S(1)} %collective-permute-done.26.refs_3_, ...), custom_call_target="tpu_custom_call", output_to_operand_aliasing={{0}: (5, {})} | custom-call | flops 134217728 | bytes 2621440 | tf_op jit(solution)/shard_map/finish/pallas_call | solution.py:482
  155.9 0.1 pick.6.after_ref
  156.1 0.4 collective-permute-start.28
  156.6 0.3 collective-permute-start.32
  156.8 1.3 collective-permute-done.32.refs_4_
  158.2 3.3 %finish.5 = (f32[64,128,128]{2,1,0:T(8,128)}, f32[8,128]{1,0:T(8,128)S(1)}) custom-call(s32[1]{0:T(128)} %bitcast.me_ref.refs_0_, s32[1,64]{1,0:T(1,128)S(1)} %copy-done.5, bf16[128,256]{1,0:T(8,128)(2,1)S(1)} %copy-done.1, bf16[16,128,128]{2,1,0:T(8,128)(2,1)S(1)} %collective-permute-done.31.refs_3_, ...), custom_call_target="tpu_custom_call", output_to_operand_aliasing={{0}: (5, {})} | custom-call | flops 134217728 | bytes 2621440 | tf_op jit(solution)/shard_map/finish/pallas_call | solution.py:482
  161.5 5.8 %collective-permute-done.30.got_ref = bf16[16,128,128]{2,1,0:T(8,128)(2,1)S(1)} collective-permute-done((bf16[16,128,128]{2,1,0:T(8,128)(2,1)S(1)}, bf16[16,128,128]{2,1,0:T(8,128)(2,1)S(1)}, u32[]{:S(2)}, u32[]{:S(2)}) %collective-permute-start.30) | collective-permute-done | bytes 524320 | tf_op jit(solution)/shard_map/ppermute | solution.py:580
  167.3 0.1 pick.7
  167.5 3.0 %collective-permute-done.28.refs_3_ = bf16[16,128,128]{2,1,0:T(8,128)(2,1)S(1)} collective-permute-done((bf16[16,128,128]{2,1,0:T(8,128)(2,1)S(1)}, bf16[16,128,128]{2,1,0:T(8,128)(2,1)S(1)}, u32[]{:S(2)}, u32[]{:S(2)}) %collective-permute-start.28) | collective-permute-done | bytes 524320 | tf_op jit(solution)/shard_map/ppermute | solution.py:584
  170.6 1.5 bitcast_convert_fusion
  172.1 3.9 %finish.6 = (f32[64,128,128]{2,1,0:T(8,128)}, f32[8,128]{1,0:T(8,128)}) custom-call(s32[1]{0:T(128)} %bitcast.me_ref.refs_0_, s32[1,64]{1,0:T(1,128)S(1)} %copy-done.5, bf16[128,256]{1,0:T(8,128)(2,1)S(1)} %copy-done.1, bf16[8,128,128]{2,1,0:T(8,128)(2,1)S(1)} %get-tuple-element.37.refs_3_, ...), custom_call_target="tpu_custom_call", output_to_operand_aliasing={{0}: (5, {})} | custom-call | flops 134217728 | bytes 2621440 | tf_op jit(solution)/shard_map/finish/pallas_call | solution.py:482
  176.0 3.9 %finish.7 = (f32[64,128,128]{2,1,0:T(8,128)}, f32[8,128]{1,0:T(8,128)}) custom-call(s32[1]{0:T(128)} %bitcast.me_ref.refs_0_, s32[1,64]{1,0:T(1,128)S(1)} %copy-done.5, bf16[128,256]{1,0:T(8,128)(2,1)S(1)} %copy-done.1, bf16[16,128,128]{2,1,0:T(8,128)(2,1)S(1)} %collective-permute-done.28.refs_3_, ...), custom_call_target="tpu_custom_call", output_to_operand_aliasing={{0}: (5, {})} | custom-call | flops 134217728 | bytes 2621440 | tf_op jit(solution)/shard_map/finish/pallas_call | solution.py:482
  (68 shorter events, 1.7 us)
Async XLA Ops:
  5.6 5.4 %collective-permute-start = (bf16[36,128,128]{2,1,0:T(8,128)(2,1)}, bf16[36,128,128]{2,1,0:T(8,128)(2,1)S(1)}, u32[]{:S(2)}, u32[]{:S(2)}) collective-permute-start(bf16[36,128,128]{2,1,0:T(8,128)(2,1)} %get-tuple-element.23), channel_id=1, source_target_pairs={{0,1},{1,0},{2,3},{3,2},{4,5},{5,4},{6,7},{7,6},{8,9},{9,8},{10,11... | collective-permute-start | bytes 3538952 | tf_op jit(solution)/shard_map/ppermute | solution.py:584
  6.1 10.9 %collective-permute-start.1 = (bf16[8,128,128]{2,1,0:T(8,128)(2,1)}, bf16[8,128,128]{2,1,0:T(8,128)(2,1)S(1)}, u32[]{:S(2)}, u32[]{:S(2)}) collective-permute-start(bf16[8,128,128]{2,1,0:T(8,128)(2,1)} %get-tuple-element.24), channel_id=1, source_target_pairs={{0,6},{1,7},{2,4},{3,5},{4,2},{5,3},{6,0},{7,1},{8,14},{9,15},{10,... | collective-permute-start | bytes 786440 | tf_op jit(solution)/shard_map/ppermute | solution.py:584
  9.7 22.7 %collective-permute-start.2 = (bf16[8,128,128]{2,1,0:T(8,128)(2,1)}, bf16[8,128,128]{2,1,0:T(8,128)(2,1)S(1)}, u32[]{:S(2)}, u32[]{:S(2)}) collective-permute-start(bf16[8,128,128]{2,1,0:T(8,128)(2,1)} %get-tuple-element.25), channel_id=1, source_target_pairs={{0,2},{1,3},{2,0},{3,1},{4,6},{5,7},{6,4},{7,5},{8,10},{9,11},{10,... | collective-permute-start | bytes 786440 | tf_op jit(solution)/shard_map/ppermute | solution.py:584
  10.2 22.1 %collective-permute-start.3 = (bf16[8,128,128]{2,1,0:T(8,128)(2,1)}, bf16[8,128,128]{2,1,0:T(8,128)(2,1)S(1)}, u32[]{:S(2)}, u32[]{:S(2)}) collective-permute-start(bf16[8,128,128]{2,1,0:T(8,128)(2,1)} %get-tuple-element.26), channel_id=1, source_target_pairs={{0,4},{1,5},{2,6},{3,7},{4,0},{5,1},{6,2},{7,3},{8,12},{9,13},{10,... | collective-permute-start | bytes 786440 | tf_op jit(solution)/shard_map/ppermute | solution.py:584
  11.0 8.0 %copy-start.6 = (bf16[36,128,128]{2,1,0:T(8,128)(2,1)}, bf16[36,128,128]{2,1,0:T(8,128)(2,1)S(1)}, u32[]{:S(2)}) copy-start(bf16[36,128,128]{2,1,0:T(8,128)(2,1)S(1)} %collective-permute-done.after_ref.refs_1_.refs_0_) | copy-start | bytes 3538948
  11.1 21.3 %collective-permute-start.4 = (bf16[9,128,128]{2,1,0:T(8,128)(2,1)S(1)}, bf16[9,128,128]{2,1,0:T(8,128)(2,1)S(1)}, u32[]{:S(2)}, u32[]{:S(2)}) collective-permute-start(bf16[9,128,128]{2,1,0:T(8,128)(2,1)S(1)} %get-tuple-element.46), channel_id=1, source_target_pairs={{0,6},{1,7},{2,4},{3,5},{4,2},{5,3},{6,0},{7,1},{8,14},{9,15},{10,... | collective-permute-start | bytes 884744 | tf_op jit(solution)/shard_map/ppermute | solution.py:584
  14.0 21.4 %collective-permute-start.5 = (bf16[9,128,128]{2,1,0:T(8,128)(2,1)S(1)}, bf16[9,128,128]{2,1,0:T(8,128)(2,1)S(1)}, u32[]{:S(2)}, u32[]{:S(2)}) collective-permute-start(bf16[9,128,128]{2,1,0:T(8,128)(2,1)S(1)} %get-tuple-element.45), channel_id=1, source_target_pairs={{0,2},{1,3},{2,0},{3,1},{4,6},{5,7},{6,4},{7,5},{8,10},{9,11},{10,... | collective-permute-start | bytes 884744 | tf_op jit(solution)/shard_map/ppermute | solution.py:584
  17.1 15.2 %copy-start.14 = (bf16[8,128,128]{2,1,0:T(8,128)(2,1)}, bf16[8,128,128]{2,1,0:T(8,128)(2,1)S(1)}, u32[]{:S(2)}) copy-start(bf16[8,128,128]{2,1,0:T(8,128)(2,1)S(1)} %collective-permute-done.1.refs_2_) | copy-start | bytes 786436
  17.1 18.3 %collective-permute-start.6 = (bf16[9,128,128]{2,1,0:T(8,128)(2,1)S(1)}, bf16[9,128,128]{2,1,0:T(8,128)(2,1)S(1)}, u32[]{:S(2)}, u32[]{:S(2)}) collective-permute-start(bf16[9,128,128]{2,1,0:T(8,128)(2,1)S(1)} %get-tuple-element.44), channel_id=1, source_target_pairs={{0,4},{1,5},{2,6},{3,7},{4,0},{5,1},{6,2},{7,3},{8,12},{9,13},{10,... | collective-permute-start | bytes 884744 | tf_op jit(solution)/shard_map/ppermute | solution.py:584
  32.3 3.1 %copy-start.15 = (bf16[8,128,128]{2,1,0:T(8,128)(2,1)}, bf16[8,128,128]{2,1,0:T(8,128)(2,1)S(1)}, u32[]{:S(2)}) copy-start(bf16[8,128,128]{2,1,0:T(8,128)(2,1)S(1)} %collective-permute-done.2.refs_3_) | copy-start | bytes 786436
  32.4 3.0 %copy-start.16 = (bf16[8,128,128]{2,1,0:T(8,128)(2,1)}, bf16[8,128,128]{2,1,0:T(8,128)(2,1)S(1)}, u32[]{:S(2)}) copy-start(bf16[8,128,128]{2,1,0:T(8,128)(2,1)S(1)} %collective-permute-done.3.refs_4_) | copy-start | bytes 786436
  32.4 3.0 %copy-start.9 = (bf16[9,128,128]{2,1,0:T(8,128)(2,1)}, bf16[9,128,128]{2,1,0:T(8,128)(2,1)S(1)}, u32[]{:S(2)}) copy-start(bf16[9,128,128]{2,1,0:T(8,128)(2,1)S(1)} %collective-permute-done.4.refs_5_.refs_3_) | copy-start | bytes 884740
  35.4 0.7 copy-start.10
  35.4 0.8 copy-start.11
  47.2 2.9 %collective-permute-start.7 = (f32[16,128,128]{2,1,0:T(8,128)}, f32[16,128,128]{2,1,0:T(8,128)S(1)}, u32[]{:S(2)}, u32[]{:S(2)}) collective-permute-start(f32[16,128,128]{2,1,0:T(8,128)} %get-tuple-element.28), channel_id=1, source_target_pairs={{0,1},{1,0},{2,3},{3,2},{4,5},{5,4},{6,7},{7,6},{8,9},{9,8},{10,11... | collective-permute-start | bytes 3145736 | tf_op jit(solution)/shard_map/ppermute | solution.py:584
  51.5 18.1 %copy-start.7 = (bf16[16,128,128]{2,1,0:T(8,128)(2,1)}, bf16[16,128,128]{2,1,0:T(8,128)(2,1)S(1)}, u32[]{:S(2)}) copy-start(bf16[16,128,128]{2,1,0:T(8,128)(2,1)S(1)} %get-tuple-element.42) | copy-start | bytes 1572868
  51.6 8.4 %collective-permute-start.10 = (bf16[4,128,128]{2,1,0:T(8,128)(2,1)S(1)}, bf16[4,128,128]{2,1,0:T(8,128)(2,1)S(1)}, u32[]{:S(2)}, u32[]{:S(2)}) collective-permute-start(bf16[4,128,128]{2,1,0:T(8,128)(2,1)S(1)} %get-tuple-element.48), channel_id=1, source_target_pairs={{0,4},{1,5},{2,6},{3,7},{4,0},{5,1},{6,2},{7,3},{8,12},{9,13},{10,... | collective-permute-start | bytes 393224 | tf_op jit(solution)/shard_map/ppermute | solution.py:584
  51.6 8.3 %collective-permute-start.8 = (bf16[4,128,128]{2,1,0:T(8,128)(2,1)S(1)}, bf16[4,128,128]{2,1,0:T(8,128)(2,1)S(1)}, u32[]{:S(2)}, u32[]{:S(2)}) collective-permute-start(bf16[4,128,128]{2,1,0:T(8,128)(2,1)S(1)} %get-tuple-element.47), channel_id=1, source_target_pairs={{0,6},{1,7},{2,4},{3,5},{4,2},{5,3},{6,0},{7,1},{8,14},{9,15},{10,... | collective-permute-start | bytes 393224 | tf_op jit(solution)/shard_map/ppermute | solution.py:584
  51.7 9.5 %collective-permute-start.9 = (bf16[4,128,128]{2,1,0:T(8,128)(2,1)S(1)}, bf16[4,128,128]{2,1,0:T(8,128)(2,1)S(1)}, u32[]{:S(2)}, u32[]{:S(2)}) collective-permute-start(bf16[4,128,128]{2,1,0:T(8,128)(2,1)S(1)} %get-tuple-element.49), channel_id=1, source_target_pairs={{0,2},{1,3},{2,0},{3,1},{4,6},{5,7},{6,4},{7,5},{8,10},{9,11},{10,... | collective-permute-start | bytes 393224 | tf_op jit(solution)/shard_map/ppermute | solution.py:584
  61.3 6.9 %collective-permute-start.11 = (bf16[4,128,128]{2,1,0:T(8,128)(2,1)S(1)}, bf16[4,128,128]{2,1,0:T(8,128)(2,1)S(1)}, u32[]{:S(2)}, u32[]{:S(2)}) collective-permute-start(bf16[4,128,128]{2,1,0:T(8,128)(2,1)S(1)} %fusion), channel_id=1, source_target_pairs={{0,6},{1,7},{2,4},{3,5},{4,2},{5,3},{6,0},{7,1},{8,14},{9,15},{10,... | collective-permute-start | bytes 393224 | tf_op jit(solution)/shard_map/ppermute | solution.py:584
  61.6 7.1 %collective-permute-start.12 = (bf16[4,128,128]{2,1,0:T(8,128)(2,1)S(1)}, bf16[4,128,128]{2,1,0:T(8,128)(2,1)S(1)}, u32[]{:S(2)}, u32[]{:S(2)}) collective-permute-start(bf16[4,128,128]{2,1,0:T(8,128)(2,1)S(1)} %fusion), channel_id=1, source_target_pairs={{0,2},{1,3},{2,0},{3,1},{4,6},{5,7},{6,4},{7,5},{8,10},{9,11},{10,... | collective-permute-start | bytes 393224 | tf_op jit(solution)/shard_map/ppermute | solution.py:584
  63.2 6.3 %collective-permute-start.13 = (bf16[4,128,128]{2,1,0:T(8,128)(2,1)S(1)}, bf16[4,128,128]{2,1,0:T(8,128)(2,1)S(1)}, u32[]{:S(2)}, u32[]{:S(2)}) collective-permute-start(bf16[4,128,128]{2,1,0:T(8,128)(2,1)S(1)} %fusion), channel_id=1, source_target_pairs={{0,4},{1,5},{2,6},{3,7},{4,0},{5,1},{6,2},{7,3},{8,12},{9,13},{10,... | collective-permute-start | bytes 393224 | tf_op jit(solution)/shard_map/ppermute | solution.py:584
  69.6 3.3 %copy-start.8 = (bf16[16,128,128]{2,1,0:T(8,128)(2,1)}, bf16[16,128,128]{2,1,0:T(8,128)(2,1)S(1)}, u32[]{:S(2)}) copy-start(bf16[16,128,128]{2,1,0:T(8,128)(2,1)S(1)} %pad_maximum_fusion.even_in_ref) | copy-start | bytes 1572868
  69.6 3.3 %collective-permute-start.14 = (bf16[16,128,128]{2,1,0:T(8,128)(2,1)S(1)}, bf16[16,128,128]{2,1,0:T(8,128)(2,1)S(1)}, u32[]{:S(2)}, u32[]{:S(2)}) collective-permute-start(bf16[16,128,128]{2,1,0:T(8,128)(2,1)S(1)} %pad_maximum_fusion.even_in_ref), channel_id=1, source_target_pairs={{0,1},{1,0},{2,3},{3,2},{4,5},{5,4},{6,7},{7,6},{8,9},{9,8},{10,11... | collective-permute-start | bytes 1572872 | tf_op jit(solution)/shard_map/ppermute | solution.py:584
  72.9 0.8 copy-start.13
  85.2 14.0 %collective-permute-start.16 = (bf16[16,128,128]{2,1,0:T(8,128)(2,1)}, bf16[16,128,128]{2,1,0:T(8,128)(2,1)S(1)}, u32[]{:S(2)}, u32[]{:S(2)}) collective-permute-start(bf16[16,128,128]{2,1,0:T(8,128)(2,1)} %get-tuple-element.31.mine_ref.after_ref), channel_id=1, source_target_pairs={{0,8},{24,16},{1,9},{25,17},{2,10},{26,18},{3,11},{27,19},{4,12},{... | collective-permute-start | bytes 1572872 | tf_op jit(solution)/shard_map/ppermute | solution.py:559
  86.5 23.9 %collective-permute-start.18 = (bf16[16,128,128]{2,1,0:T(8,128)(2,1)}, bf16[16,128,128]{2,1,0:T(8,128)(2,1)S(1)}, u32[]{:S(2)}, u32[]{:S(2)}) collective-permute-start(bf16[16,128,128]{2,1,0:T(8,128)(2,1)} %get-tuple-element.32.mine_ref), channel_id=1, source_target_pairs={{0,8},{24,16},{1,9},{25,17},{2,10},{26,18},{3,11},{27,19},{4,12},{... | collective-permute-start | bytes 1572872 | tf_op jit(solution)/shard_map/ppermute | solution.py:559
  99.2 1.0 copy-start
  100.2 14.3 %copy-start.2 = (bf16[16,128,128]{2,1,0:T(8,128)(2,1)S(1)}, bf16[16,128,128]{2,1,0:T(8,128)(2,1)}, u32[]{:S(2)}) copy-start(bf16[16,128,128]{2,1,0:T(8,128)(2,1)} %get-tuple-element.33.mine_ref) | copy-start | bytes 1572868
  100.2 21.4 %copy-start.3 = (bf16[16,128,128]{2,1,0:T(8,128)(2,1)S(1)}, bf16[16,128,128]{2,1,0:T(8,128)(2,1)}, u32[]{:S(2)}) copy-start(bf16[16,128,128]{2,1,0:T(8,128)(2,1)} %get-tuple-element.30.mine_ref) | copy-start | bytes 1572868
  100.3 12.7 %collective-permute-start.17 = (bf16[16,128,128]{2,1,0:T(8,128)(2,1)S(1)}, bf16[16,128,128]{2,1,0:T(8,128)(2,1)S(1)}, u32[]{:S(2)}, u32[]{:S(2)}) collective-permute-start(bf16[16,128,128]{2,1,0:T(8,128)(2,1)S(1)} %merge.8.after_ref.mine_ref), channel_id=1, source_target_pairs={{8,16},{16,8},{9,17},{17,9},{10,18},{18,10},{11,19},{19,11},{12,20... | collective-permute-start | bytes 1572872 | tf_op jit(solution)/shard_map/ppermute | solution.py:580
  101.2 20.5 %collective-permute-start.15 = (bf16[16,128,128]{2,1,0:T(8,128)(2,1)}, bf16[16,128,128]{2,1,0:T(8,128)(2,1)S(1)}, u32[]{:S(2)}, u32[]{:S(2)}) collective-permute-start(bf16[16,128,128]{2,1,0:T(8,128)(2,1)} %get-tuple-element.30.mine_ref), channel_id=1, source_target_pairs={{0,8},{24,16},{1,9},{25,17},{2,10},{26,18},{3,11},{27,19},{4,12},{... | collective-permute-start | bytes 1572872 | tf_op jit(solution)/shard_map/ppermute | solution.py:559
  110.4 1.0 copy-start.4
  111.6 10.9 %collective-permute-start.22 = (bf16[16,128,128]{2,1,0:T(8,128)(2,1)S(1)}, bf16[16,128,128]{2,1,0:T(8,128)(2,1)}, u32[]{:S(2)}, u32[]{:S(2)}) collective-permute-start(bf16[16,128,128]{2,1,0:T(8,128)(2,1)S(1)} %merge.9.after_ref.mine_ref), channel_id=1, source_target_pairs={{8,16},{16,8},{9,17},{17,9},{10,18},{18,10},{11,19},{19,11},{12,20... | collective-permute-start | bytes 1572872 | tf_op jit(solution)/shard_map/ppermute | solution.py:580
  113.2 12.1 %collective-permute-start.21 = (bf16[16,128,128]{2,1,0:T(8,128)(2,1)S(1)}, bf16[16,128,128]{2,1,0:T(8,128)(2,1)}, u32[]{:S(2)}, u32[]{:S(2)}) collective-permute-start(bf16[16,128,128]{2,1,0:T(8,128)(2,1)S(1)} %merge.10.after_ref.mine_ref), channel_id=1, source_target_pairs={{8,0},{16,24},{9,1},{17,25},{10,2},{18,26},{11,3},{19,27},{12,4},{... | collective-permute-start | bytes 1572872 | tf_op jit(solution)/shard_map/ppermute | solution.py:580
  114.5 23.9 %collective-permute-start.20 = (bf16[16,128,128]{2,1,0:T(8,128)(2,1)S(1)}, bf16[16,128,128]{2,1,0:T(8,128)(2,1)S(1)}, u32[]{:S(2)}, u32[]{:S(2)}) collective-permute-start(bf16[16,128,128]{2,1,0:T(8,128)(2,1)S(1)} %copy-done.2), channel_id=1, source_target_pairs={{0,8},{24,16},{1,9},{25,17},{2,10},{26,18},{3,11},{27,19},{4,12},{... | collective-permute-start | bytes 1572872 | tf_op jit(solution)/shard_map/ppermute | solution.py:559
  121.8 17.6 %collective-permute-start.19 = (bf16[16,128,128]{2,1,0:T(8,128)(2,1)S(1)}, bf16[16,128,128]{2,1,0:T(8,128)(2,1)S(1)}, u32[]{:S(2)}, u32[]{:S(2)}) collective-permute-start(bf16[16,128,128]{2,1,0:T(8,128)(2,1)S(1)} %merge.11.after_ref.mine_ref), channel_id=1, source_target_pairs={{8,16},{16,8},{9,17},{17,9},{10,18},{18,10},{11,19},{19,11},{12,20... | collective-permute-start | bytes 1572872 | tf_op jit(solution)/shard_map/ppermute | solution.py:580
  123.7 17.2 %collective-permute-start.25 = (bf16[16,128,128]{2,1,0:T(8,128)(2,1)S(1)}, bf16[16,128,128]{2,1,0:T(8,128)(2,1)S(1)}, u32[]{:S(2)}, u32[]{:S(2)}) collective-permute-start(bf16[16,128,128]{2,1,0:T(8,128)(2,1)S(1)} %merge.12.after_ref.token_ref.mine_ref), channel_id=1, source_target_pairs={{8,0},{16,24},{9,1},{17,25},{10,2},{18,26},{11,3},{19,27},{12,4},{... | collective-permute-start | bytes 1572872 | tf_op jit(solution)/shard_map/ppermute | solution.py:580
  126.4 24.4 %collective-permute-start.26 = (bf16[16,128,128]{2,1,0:T(8,128)(2,1)S(1)}, bf16[16,128,128]{2,1,0:T(8,128)(2,1)S(1)}, u32[]{:S(2)}, u32[]{:S(2)}) collective-permute-start(bf16[16,128,128]{2,1,0:T(8,128)(2,1)S(1)} %pick.4.after_ref), channel_id=1, source_target_pairs={{0,6},{1,7},{2,4},{3,5},{4,2},{5,3},{6,0},{7,1},{8,14},{9,15},{10,... | collective-permute-start | bytes 1572872 | tf_op jit(solution)/shard_map/ppermute | solution.py:584
  138.5 14.0 %copy-start.1 = (bf16[128,256]{1,0:T(8,128)(2,1)S(1)}, bf16[128,256]{1,0:T(8,128)(2,1)}, u32[]{:S(2)}) copy-start(bf16[128,256]{1,0:T(8,128)(2,1)} %constant.19.clone.refs_2_) | copy-start | bytes 196612
  138.5 14.0 %copy-start.5 = (s32[1,64]{1,0:T(1,128)S(1)}, s32[1,64]{1,0:T(1,128)}, u32[]{:S(2)}) copy-start(s32[1,64]{1,0:T(1,128)} %refs_1_.7) | copy-start | bytes 772
  138.6 12.4 %collective-permute-start.24 = (bf16[16,128,128]{2,1,0:T(8,128)(2,1)S(1)}, bf16[16,128,128]{2,1,0:T(8,128)(2,1)S(1)}, u32[]{:S(2)}, u32[]{:S(2)}) collective-permute-start(bf16[16,128,128]{2,1,0:T(8,128)(2,1)S(1)} %merge.13.after_ref.mine_ref), channel_id=1, source_target_pairs={{8,16},{16,8},{9,17},{17,9},{10,18},{18,10},{11,19},{19,11},{12,20... | collective-permute-start | bytes 1572872 | tf_op jit(solution)/shard_map/ppermute | solution.py:580
  139.5 16.4 %collective-permute-start.23 = (bf16[16,128,128]{2,1,0:T(8,128)(2,1)S(1)}, bf16[16,128,128]{2,1,0:T(8,128)(2,1)S(1)}, u32[]{:S(2)}, u32[]{:S(2)}) collective-permute-start(bf16[16,128,128]{2,1,0:T(8,128)(2,1)S(1)} %merge.14.after_ref.token_ref.mine_ref), channel_id=1, source_target_pairs={{8,0},{16,24},{9,1},{17,25},{10,2},{18,26},{11,3},{19,27},{12,4},{... | collective-permute-start | bytes 1572872 | tf_op jit(solution)/shard_map/ppermute | solution.py:580
  141.0 15.5 %collective-permute-start.31 = (bf16[16,128,128]{2,1,0:T(8,128)(2,1)S(1)}, bf16[16,128,128]{2,1,0:T(8,128)(2,1)S(1)}, u32[]{:S(2)}, u32[]{:S(2)}) collective-permute-start(bf16[16,128,128]{2,1,0:T(8,128)(2,1)S(1)} %pick.5.after_ref), channel_id=1, source_target_pairs={{0,2},{1,3},{2,0},{3,1},{4,6},{5,7},{6,4},{7,5},{8,10},{9,11},{10,... | collective-permute-start | bytes 1572872 | tf_op jit(solution)/shard_map/ppermute | solution.py:584
  150.9 1.7 collective-permute-start.27
  151.1 16.2 %collective-permute-start.30 = (bf16[16,128,128]{2,1,0:T(8,128)(2,1)S(1)}, bf16[16,128,128]{2,1,0:T(8,128)(2,1)S(1)}, u32[]{:S(2)}, u32[]{:S(2)}) collective-permute-start(bf16[16,128,128]{2,1,0:T(8,128)(2,1)S(1)} %merge.15.after_ref.mine_ref), channel_id=1, source_target_pairs={{8,0},{16,24},{9,1},{17,25},{10,2},{18,26},{11,3},{19,27},{12,4},{... | collective-permute-start | bytes 1572872 | tf_op jit(solution)/shard_map/ppermute | solution.py:580
  156.1 14.5 %copy-start.12 = (bf16[32,128,128]{2,1,0:T(8,128)(2,1)S(1)}, bf16[32,128,128]{2,1,0:T(8,128)(2,1)}, u32[]{:S(2)}) copy-start(bf16[32,128,128]{2,1,0:T(8,128)(2,1)} %get-tuple-element.29) | copy-start | bytes 3145732
  156.1 14.4 %collective-permute-start.28 = (bf16[16,128,128]{2,1,0:T(8,128)(2,1)S(1)}, bf16[16,128,128]{2,1,0:T(8,128)(2,1)S(1)}, u32[]{:S(2)}, u32[]{:S(2)}) collective-permute-start(bf16[16,128,128]{2,1,0:T(8,128)(2,1)S(1)} %pick.6.after_ref), channel_id=1, source_target_pairs={{0,4},{1,5},{2,6},{3,7},{4,0},{5,1},{6,2},{7,3},{8,12},{9,13},{10,... | collective-permute-start | bytes 1572872 | tf_op jit(solution)/shard_map/ppermute | solution.py:584
  156.6 1.6 collective-permute-start.32
  167.4 4.7 %collective-permute-start.33 = (bf16[8,128,128]{2,1,0:T(8,128)(2,1)S(1)}, bf16[8,128,128]{2,1,0:T(8,128)(2,1)S(1)}, u32[]{:S(2)}, u32[]{:S(2)}) collective-permute-start(bf16[8,128,128]{2,1,0:T(8,128)(2,1)S(1)} %get-tuple-element.38), channel_id=1, source_target_pairs={{0,1},{1,0},{2,3},{3,2},{4,5},{5,4},{6,7},{7,6},{8,9},{9,8},{10,11... | collective-permute-start | bytes 786440 | tf_op jit(solution)/shard_map/ppermute | solution.py:584
  170.5 5.5 %collective-permute-start.29 = (bf16[8,128,128]{2,1,0:T(8,128)(2,1)S(1)}, bf16[8,128,128]{2,1,0:T(8,128)(2,1)S(1)}, u32[]{:S(2)}, u32[]{:S(2)}) collective-permute-start(bf16[8,128,128]{2,1,0:T(8,128)(2,1)S(1)} %slice.52), channel_id=1, source_target_pairs={{0,1},{1,0},{2,3},{3,2},{4,5},{5,4},{6,7},{7,6},{8,9},{9,8},{10,11... | collective-permute-start | bytes 786440 | tf_op jit(solution)/shard_map/ppermute | solution.py:584

commit v2 on v1

--- a/solution.py
+++ b/solution.py
@@ -247,7 +247,7 @@
 
 
 def adjoint_body(me_ref, rows_ref, cols_ref, count_ref, sens_ref, even_in_ref, odd_in_ref,
-                 after_ref, *refs):
+                 *refs):
     out_refs, image_ref = refs[:-9], refs[-9]
     block_ref, held_ref, acc_ref, half_ref, sems, got, put, whole = refs[-8:]
     peers = put.shape[0]
@@ -273,23 +273,24 @@
     for offset in reversed(range(peers)):
         part = acc_ref[pl.ds((me ^ offset) * each, each)]
         half_ref[offset] = part.astype(half_ref.dtype)
-        target = out_refs[offset // 2].at[pl.ds(offset % 2 * each, each)]
-        stores.append(pltpu.make_async_copy(half_ref.at[offset], target, put.at[offset]))
+        stores.append(
+            pltpu.make_async_copy(half_ref.at[offset], out_refs[offset], put.at[offset])
+        )
         stores[-1].start()
     wait_all(stores)
 
 
-def adjoint(me, rows, cols, count, sens, even, odd, after, blocks, peers):
+def adjoint(me, rows, cols, count, sens, even, odd, blocks, peers):
     slots = sens.shape[0]
     width = even.shape[2]
     piece = (blocks // peers, BLK, width)
     image = (RB_DEV, BLK, width)
     outs = pl.pallas_call(
         adjoint_body,
-        out_shape=[jax.ShapeDtypeStruct((2 * piece[0], *piece[1:]), jnp.bfloat16)] * (peers // 2)
+        out_shape=[jax.ShapeDtypeStruct(piece, jnp.bfloat16)] * peers
         + [jax.ShapeDtypeStruct(image, jnp.bfloat16)],
-        in_specs=[SMEM_SPEC] * 4 + [ANY_SPEC] * 4,
-        out_specs=[ANY_SPEC] * (peers // 2 + 1),
+        in_specs=[SMEM_SPEC] * 4 + [ANY_SPEC] * 3,
+        out_specs=[ANY_SPEC] * (peers + 1),
         scratch_shapes=[
             pltpu.VMEM(sens.shape, sens.dtype),
             pltpu.VMEM(image, jnp.bfloat16),
@@ -306,7 +307,7 @@
             transcendentals=0,
         ),
         name="adjoint",
-    )(me, rows, cols, count, sens, even, odd, after)
+    )(me, rows, cols, count, sens, even, odd)
     return outs[:-1], outs[-1]
 
 
@@ -384,8 +385,9 @@
 
 
 def edges_body(me_ref, offset_ref, model_ref, near_ref, weight_ref, base_ref, after_ref, *refs):
-    odd_refs, refs = refs[:-6], refs[-6:]
-    out_ref, window_ref, value_ref, ends_ref, got, put = refs
+    odd_refs, refs = refs[:-7], refs[-7:]
+    out_ref, token_ref, window_ref, value_ref, ends_ref, got, put = refs
+    token_ref[...] = jnp.zeros_like(token_ref)
     cells = model_ref.shape[0]
     each = odd_refs[-1].shape[0] - 1
     inner = 2 * BLK - RIM
@@ -430,10 +432,13 @@
     count = len(odd_pieces)
     return pl.pallas_call(
         edges_body,
-        out_shape=jax.ShapeDtypeStruct(base.shape, base.dtype),
+        out_shape=[
+            jax.ShapeDtypeStruct(base.shape, base.dtype),
+            jax.ShapeDtypeStruct((8, BLK), jnp.float32),
+        ],
         in_specs=[SMEM_SPEC, SMEM_SPEC, ANY_SPEC, VMEM_SPEC, VMEM_SPEC]
         + [ANY_SPEC] * (2 + count),
-        out_specs=ANY_SPEC,
+        out_specs=[ANY_SPEC, VMEM_SPEC],
         input_output_aliases={5: 0},
         scratch_shapes=[
             pltpu.VMEM((2, 2 * BLK, width), jnp.float32),
@@ -544,7 +549,7 @@
     )(take, got, mine, after, token)
 
 
-def line_sums(parts, axis, deliver):
+def line_sums(parts, axis, after, deliver):
     count = lax.axis_size(axis)
     half = count // 2
     me = lax.axis_index(axis)
@@ -557,7 +562,6 @@
         stages.append(([(left, left - 1), (right, right + 1)], True))
     state = list(parts)
     got = [lax.ppermute(part, axis, stages[0][0]) for part in parts]
-    after = parts[0]
     for time in range(len(parts) + len(stages) - 1):
         for s, (pairs, outwards) in enumerate(stages):
             k = time - s
@@ -618,42 +622,39 @@
         [image_share] + [swap(image_share, "cols", 2 * j) for j in far], axis=0
     )
     odd_image = swap(even_image, "cols", 1)
-    smooth = edges(
-        me, offset, model_dir, neighbors, face_weight, smooth, to_send, [partner, *[passed[j] for j in range(1, half)]]
-    )
-
     partial_cols, image = adjoint(
-        me, blk_row, blk_col, blk_count, sens, even_image, odd_image, smooth, blocks, peers
+        me, blk_row, blk_col, blk_count, sens, even_image, odd_image, blocks, peers
     )
     data_image = image.reshape(RB_DEV * BLK, width).astype(jnp.float32)
+    smooth, first = edges(
+        me, offset, model_dir, neighbors, face_weight, smooth, partial_cols[0],
+        [partner, *[passed[j] for j in range(1, half)]],
+    )
     normal = smooth.reshape(blocks, BLK, width)
-    order = [*far, 0]
-    waiting, tokens = [], []
-
-    def end_one(place):
+    order = [2 * j + odd for j in far for odd in (1, 0)] + [1, 0]
+    returned, waiting, tokens = {}, [], []
+
+    def end_one():
         nonlocal normal
-        even, odd_piece, j = waiting.pop(place)
-        normal, token = finish(me, send_order, even, odd_piece, normal, 2 * j)
+        j = waiting.pop(0)
+        even, odd = returned[2 * j], returned[2 * j + 1]
+        normal, token = finish(me, send_order, even, odd, normal, 2 * j)
         tokens.append(token)
 
     def deliver(k, take, got, mine, after):
-        if k >= 2:
-            end_one(0)
+        if k % 2 == 0 and k >= 4:
+            end_one()
         token = tokens[-1] if tokens else after
-        j = order[k]
-        if j:
-            [total] = pick(take, got, mine, after, token, 1)
-            even = swap(total, "cols", 2 * j)
-            other = even[per_peer:]
-        else:
-            even, other = pick(take, got, mine, after, token, 2)
-            total = even
-        waiting.append((even, swap(other, "cols", 1), j))
+        o = order[k]
+        [total] = pick(take, got, mine, after, token, 1)
+        returned[o] = swap(total, "cols", o) if o else total
+        if k % 2:
+            waiting.append(o // 2)
         return total
 
-    line_sums([partial_cols[j] for j in order], "rows", deliver)
+    line_sums([partial_cols[o] for o in order], "rows", first, deliver)
     while waiting:
-        end_one(-1)
+        end_one()
     return (data_image, normal.reshape(cell_count, width))
 
 

time: 181 us -> 182 us (level)
  starting transfers between devices: 61 us -> 81.5 us
  waiting for transfers between devices: 48.1 us -> 37.6 us
  Pallas kernels: 62 us -> 54.6 us
    ppermute x4 -> x8, starting transfers between devices: 13.8 us -> 41.8 us  [line_sums(): got = [lax.ppermute(part, axis, stages[0][0]) for part in parts]]
    ppermute x22, starting transfers between devices: 38 us -> 23.6 us  [swap(): lax.ppermute(piece, axis, [(c, c ^ offset) for c in range(lax.axis_size(a...]
    ppermute x4 -> x8, waiting for transfers between devices: 16.6 us -> 3.24 us  [line_sums(): got = [lax.ppermute(part, axis, stages[0][0]) for part in parts]]
    ppermute x8 -> x16, starting transfers between devices: 9.17 us -> 16.1 us  [line_sums(): got[k] = lax.ppermute(state[k], axis, stages[s + 1][0])]
    ppermute x8 -> x16, waiting for transfers between devices: 6.1 us -> 12.1 us  [line_sums(): got[k] = lax.ppermute(state[k], axis, stages[s + 1][0])]
    ppermute x22, waiting for transfers between devices: 25.5 us -> 22.3 us  [swap(): lax.ppermute(piece, axis, [(c, c ^ offset) for c in range(lax.axis_size(a...]
    pallas_call x1, Pallas kernels: 11 us -> 8.12 us  [forward(): pl.pallas_call(forward_body, out_shape=[jax.ShapeDtypeStruct(half, jnp.fl...]
    pallas_call x2, Pallas kernels: 14.7 us -> 12.2 us  [the longest x1 8.42 us: adjoint(): pl.pallas_call(adjoint_body, out_shape=[jax.ShapeDtypeStruct(piece, jnp.b...]
  transfers between devices with their start and end apart: 34 -> 46, of which waited for: 16 -> 17; matrix products, arithmetic and copies ran while one was open for 1% -> 1% of each run, Pallas kernels for 17% -> 16%
where the time goes in v2:
time: 182 us; the launch traced here: 181 us
  starting transfers between devices  81.5 us (45%)
  Pallas kernels  54.6 us (30%)
  waiting for transfers between devices  37.6 us (21%)
  other arithmetic  3.06 us (2%)
  local copies, waits for them, and re-layouts  2.36 us (1%)
  between operations  2.22 us (1%)
    ppermute x8, starting transfers between devices, line_sums(): got = [lax.ppermute(part, axis, stages[0][0]) for part in parts]  41.8 us
    ppermute x22, starting transfers between devices, swap(): lax.ppermute(piece, axis, [(c, c ^ offset) for c in range(lax.axis_size(a...  23.6 us
    ppermute x22, waiting for transfers between devices, swap(): lax.ppermute(piece, axis, [(c, c ^ offset) for c in range(lax.axis_size(a...  22.3 us
    ppermute x16, starting transfers between devices, line_sums(): got[k] = lax.ppermute(state[k], axis, stages[s + 1][0])  16.1 us
    pallas_call x4, Pallas kernels, finish(): pl.pallas_call(lambda *refs: finish_body(*refs, offset=offset), out_shape...  14.5 us
    pallas_call x1, Pallas kernels, smoothing(): pl.pallas_call(smooth_body, out_shape=jax.ShapeDtypeStruct((cells, width)...  13.3 us
    ppermute x16, waiting for transfers between devices, line_sums(): got[k] = lax.ppermute(state[k], axis, stages[s + 1][0])  12.1 us
    pallas_call x1, Pallas kernels, adjoint(): pl.pallas_call(adjoint_body, out_shape=[jax.ShapeDtypeStruct(piece, jnp.b...  8.42 us
  transfers between devices with their start and end apart: 46, of which 17 were waited for; matrix products, arithmetic and copies ran while one was open for 1% of the time, Pallas kernels for 16%

profile of v2, /device:TPU:0, one launch (start us, length us, event | category | flops | bytes accessed | tf_op | source)
XLA Modules:
  0.0 181.4 jit_solution(2868769064656730412)
XLA Ops:
  0.6 5.0 %analyze.1 = (bf16[8,128,128]{2,1,0:T(8,128)(2,1)}, bf16[8,128,128]{2,1,0:T(8,128)(2,1)}, bf16[8,128,128]{2,1,0:T(8,128)(2,1)}, bf16[8,128,128]{2,1,0:T(8,128)(2,1)}, bf16[36,128,128]{2,1,0:T(8,128)(2,1)}) custom-call(s32[1]{0:T(128)} %bitcast.me_ref.refs_0_, s32[1,64]{1,0:T(1,128)} %refs_1_.7, f32[64,128,128]{2,1,0:T(8,128)} %bitcast.14), custom_call_target="tpu_custom_call" | custom-call | flops 536870912 | bytes 6291456 | tf_op jit(solution)/shard_map/analyze/pallas_call | solution.py:145
  6.1 3.5 %collective-permute-start.1 = (bf16[8,128,128]{2,1,0:T(8,128)(2,1)}, bf16[8,128,128]{2,1,0:T(8,128)(2,1)S(1)}, u32[]{:S(2)}, u32[]{:S(2)}) collective-permute-start(bf16[8,128,128]{2,1,0:T(8,128)(2,1)} %get-tuple-element.28), channel_id=1, source_target_pairs={{0,6},{1,7},{2,4},{3,5},{4,2},{5,3},{6,0},{7,1},{8,14},{9,15},{10,... | collective-permute-start | bytes 786440 | tf_op jit(solution)/shard_map/ppermute | solution.py:588
  11.1 2.0 %collective-permute-start.6 = (bf16[9,128,128]{2,1,0:T(8,128)(2,1)S(1)}, bf16[9,128,128]{2,1,0:T(8,128)(2,1)S(1)}, u32[]{:S(2)}, u32[]{:S(2)}) collective-permute-start(bf16[9,128,128]{2,1,0:T(8,128)(2,1)S(1)} %get-tuple-element.52), channel_id=1, source_target_pairs={{0,4},{1,5},{2,6},{3,7},{4,0},{5,1},{6,2},{7,3},{8,12},{9,13},{10,... | collective-permute-start | bytes 884744 | tf_op jit(solution)/shard_map/ppermute | solution.py:588
  13.0 1.5 collective-permute-start.5
  14.5 2.5 %collective-permute-done.1.refs_2_ = bf16[8,128,128]{2,1,0:T(8,128)(2,1)S(1)} collective-permute-done((bf16[8,128,128]{2,1,0:T(8,128)(2,1)}, bf16[8,128,128]{2,1,0:T(8,128)(2,1)S(1)}, u32[]{:S(2)}, u32[]{:S(2)}) %collective-permute-start.1) | collective-permute-done | bytes 262176 | tf_op jit(solution)/shard_map/ppermute | solution.py:588
  17.1 2.8 %collective-permute-start.4 = (bf16[9,128,128]{2,1,0:T(8,128)(2,1)S(1)}, bf16[9,128,128]{2,1,0:T(8,128)(2,1)S(1)}, u32[]{:S(2)}, u32[]{:S(2)}) collective-permute-start(bf16[9,128,128]{2,1,0:T(8,128)(2,1)S(1)} %get-tuple-element.54), channel_id=1, source_target_pairs={{0,6},{1,7},{2,4},{3,5},{4,2},{5,3},{6,0},{7,1},{8,14},{9,15},{10,... | collective-permute-start | bytes 884744 | tf_op jit(solution)/shard_map/ppermute | solution.py:588
  19.9 13.3 %smoothing.1.refs_8_.base_ref = f32[8192,128]{1,0:T(8,128)} custom-call(s32[1]{0:T(128)} %bitcast.3.offset_ref, f32[8192,128]{1,0:T(8,128)} %model_ref.3, s32[4,8192]{1,0:T(4,128)} %near_ref.3, f32[4,8192]{1,0:T(4,128)} %weight_ref.3, bf16[36,128,128]{2,1,0:T(8,128)(2,1)} %copy-done.11), custom_call_target="tpu_custom_call" | custom-call | flops 3221225472 | bytes 16777216 | tf_op jit(solution)/shard_map/smoothing/pallas_call | solution.py:368
  33.3 1.7 collective-permute-done.4.refs_5_.refs_3_
  35.1 0.7 copy-done.15
  35.8 8.1 %forward.1 = (f32[16,128,128]{2,1,0:T(8,128)}, f32[16,128,128]{2,1,0:T(8,128)}) custom-call(s32[1]{0:T(128)} %bitcast.me_ref.refs_0_, s32[1,384]{1,0:T(1,128)} %rows_ref.3, s32[1,384]{1,0:T(1,128)} %cols_ref.3, s32[1,1]{1,0:T(1,128)S(6)} %copy.24.count_ref, bf16[384,128,128]{2,1,0:T(8,128)(2,1)} %bitcast.12, bf16[8,128,128]{2,1,0:T(8,128)(2,1)} %get-tuple-element.26.refs_0_, ...), custom_call_target="tpu_custom_call" | custom-call | flops 1610612736 | bytes 12582912 | tf_op jit(solution)/shard_map/forward/pallas_call | solution.py:227
  44.0 2.9 %collective-permute-done.7 = f32[16,128,128]{2,1,0:T(8,128)S(1)} collective-permute-done((f32[16,128,128]{2,1,0:T(8,128)}, f32[16,128,128]{2,1,0:T(8,128)S(1)}, u32[]{:S(2)}, u32[]{:S(2)}) %collective-permute-start.7) | collective-permute-done | bytes 1048608 | tf_op jit(solution)/shard_map/ppermute | solution.py:588
  46.8 1.4 fusion.1
  49.0 2.8 %collective-permute-start.9 = (bf16[4,128,128]{2,1,0:T(8,128)(2,1)S(1)}, bf16[4,128,128]{2,1,0:T(8,128)(2,1)S(1)}, u32[]{:S(2)}, u32[]{:S(2)}) collective-permute-start(bf16[4,128,128]{2,1,0:T(8,128)(2,1)S(1)} %get-tuple-element.57), channel_id=1, source_target_pairs={{0,2},{1,3},{2,0},{3,1},{4,6},{5,7},{6,4},{7,5},{8,10},{9,11},{10,... | collective-permute-start | bytes 393224 | tf_op jit(solution)/shard_map/ppermute | solution.py:588
  51.8 3.8 %collective-permute-done.8 = bf16[4,128,128]{2,1,0:T(8,128)(2,1)S(1)} collective-permute-done((bf16[4,128,128]{2,1,0:T(8,128)(2,1)S(1)}, bf16[4,128,128]{2,1,0:T(8,128)(2,1)S(1)}, u32[]{:S(2)}, u32[]{:S(2)}) %collective-permute-start.8) | collective-permute-done | bytes 131104 | tf_op jit(solution)/shard_map/ppermute | solution.py:588
  55.6 1.4 collective-permute-done.10
  57.1 1.2 collective-permute-start.13
  58.9 1.7 collective-permute-start.11
  60.7 2.1 %collective-permute-done.13 = bf16[4,128,128]{2,1,0:T(8,128)(2,1)S(1)} collective-permute-done((bf16[4,128,128]{2,1,0:T(8,128)(2,1)S(1)}, bf16[4,128,128]{2,1,0:T(8,128)(2,1)S(1)}, u32[]{:S(2)}, u32[]{:S(2)}) %collective-permute-start.13) | collective-permute-done | bytes 131104 | tf_op jit(solution)/shard_map/ppermute | solution.py:588
  62.8 1.4 collective-permute-done.12
  64.2 1.9 %collective-permute-done.11 = bf16[4,128,128]{2,1,0:T(8,128)(2,1)S(1)} collective-permute-done((bf16[4,128,128]{2,1,0:T(8,128)(2,1)S(1)}, bf16[4,128,128]{2,1,0:T(8,128)(2,1)S(1)}, u32[]{:S(2)}, u32[]{:S(2)}) %collective-permute-start.11) | collective-permute-done | bytes 131104 | tf_op jit(solution)/shard_map/ppermute | solution.py:588
  66.3 1.9 %collective-permute-done.14.odd_in_ref = bf16[16,128,128]{2,1,0:T(8,128)(2,1)S(1)} collective-permute-done((bf16[16,128,128]{2,1,0:T(8,128)(2,1)S(1)}, bf16[16,128,128]{2,1,0:T(8,128)(2,1)S(1)}, u32[]{:S(2)}, u32[]{:S(2)}) %collective-permute-start.14) | collective-permute-done | bytes 524320 | tf_op jit(solution)/shard_map/ppermute | solution.py:588
  68.2 0.8 copy-done.17
  69.0 8.4 %adjoint.1 = (bf16[8,128,128]{2,1,0:T(8,128)(2,1)}, bf16[8,128,128]{2,1,0:T(8,128)(2,1)}, bf16[8,128,128]{2,1,0:T(8,128)(2,1)}, bf16[8,128,128]{2,1,0:T(8,128)(2...) custom-call(s32[1]{0:T(128)} %bitcast.me_ref.refs_0_, ...), custom_call_target="tpu_custom_call" | custom-call | flops 1610612736 | bytes 12582912 | tf_op jit(solution)/shard_map/adjoint/pallas_call | solution.py:288
  77.4 1.3 collective-permute-start.18
  78.7 1.3 collective-permute-start.17
  80.1 3.7 %edges.1 = (f32[8192,128]{1,0:T(8,128)}, f32[8,128]{1,0:T(8,128)}) custom-call(s32[1]{0:T(128)} %bitcast.me_ref.refs_0_, s32[1]{0:T(128)} %bitcast.3.offset_ref, f32[8192,128]{1,0:T(8,128)} %model_ref.3, s32[4,8192]{1,0:T(4,128)} %near_ref.3, f32[4,8192]{1,0:T(4,128)} %weight_ref.3, ...), custom_call_target="tpu_custom_call", output_to_operand_aliasing={{0}: (5, {})} | custom-call | flops 100663296 | bytes 524288 | tf_op jit(solution)/shard_map/edges/pallas_call | solution.py:433
  83.8 1.8 %collective-permute-done.18.got_ref = bf16[8,128,128]{2,1,0:T(8,128)(2,1)S(1)} collective-permute-done((bf16[8,128,128]{2,1,0:T(8,128)(2,1)}, bf16[8,128,128]{2,1,0:T(8,128)(2,1)S(1)}, u32[]{:S(2)}, u32[]{:S(2)}) %collective-permute-start.18) | collective-permute-done | bytes 262176 | tf_op jit(solution)/shard_map/ppermute | solution.py:564
  85.7 0.7 copy-done.10
  86.4 0.7 collective-permute-start.21
  87.1 15.4 %collective-permute-start.20 = (bf16[8,128,128]{2,1,0:T(8,128)(2,1)S(1)}, bf16[8,128,128]{2,1,0:T(8,128)(2,1)S(1)}, u32[]{:S(2)}, u32[]{:S(2)}) collective-permute-start(bf16[8,128,128]{2,1,0:T(8,128)(2,1)S(1)} %copy-done.7), channel_id=1, source_target_pairs={{0,8},{24,16},{1,9},{25,17},{2,10},{26,18},{3,11},{27,19},{4,12},{... | collective-permute-start | bytes 786440 | tf_op jit(solution)/shard_map/ppermute | solution.py:564
  102.6 0.7 collective-permute-start.19
  103.4 1.4 collective-permute-start.25
  104.8 5.3 %collective-permute-start.24 = (bf16[8,128,128]{2,1,0:T(8,128)(2,1)S(1)}, bf16[8,128,128]{2,1,0:T(8,128)(2,1)S(1)}, u32[]{:S(2)}, u32[]{:S(2)}) collective-permute-start(bf16[8,128,128]{2,1,0:T(8,128)(2,1)S(1)} %copy-done.6), channel_id=1, source_target_pairs={{0,8},{24,16},{1,9},{25,17},{2,10},{26,18},{3,11},{27,19},{4,12},{... | collective-permute-start | bytes 786440 | tf_op jit(solution)/shard_map/ppermute | solution.py:564
  110.2 0.7 collective-permute-start.23
  111.0 1.3 collective-permute-start.22
  112.3 4.6 %collective-permute-start.16 = (bf16[8,128,128]{2,1,0:T(8,128)(2,1)S(1)}, bf16[8,128,128]{2,1,0:T(8,128)(2,1)S(1)}, u32[]{:S(2)}, u32[]{:S(2)}) collective-permute-start(bf16[8,128,128]{2,1,0:T(8,128)(2,1)S(1)} %copy-done.5), channel_id=1, source_target_pairs={{0,8},{24,16},{1,9},{25,17},{2,10},{26,18},{3,11},{27,19},{4,12},{... | collective-permute-start | bytes 786440 | tf_op jit(solution)/shard_map/ppermute | solution.py:564
  117.1 0.8 collective-permute-start.29
  118.0 4.8 %collective-permute-start.27 = (bf16[8,128,128]{2,1,0:T(8,128)(2,1)S(1)}, bf16[8,128,128]{2,1,0:T(8,128)(2,1)S(1)}, u32[]{:S(2)}, u32[]{:S(2)}) collective-permute-start(bf16[8,128,128]{2,1,0:T(8,128)(2,1)S(1)} %copy-done.4), channel_id=1, source_target_pairs={{0,8},{24,16},{1,9},{25,17},{2,10},{26,18},{3,11},{27,19},{4,12},{... | collective-permute-start | bytes 786440 | tf_op jit(solution)/shard_map/ppermute | solution.py:564
  122.8 1.3 collective-permute-start.28
  124.3 0.7 collective-permute-start.26
  125.0 6.9 %collective-permute-start.32 = (bf16[8,128,128]{2,1,0:T(8,128)(2,1)S(1)}, bf16[8,128,128]{2,1,0:T(8,128)(2,1)S(1)}, u32[]{:S(2)}, u32[]{:S(2)}) collective-permute-start(bf16[8,128,128]{2,1,0:T(8,128)(2,1)S(1)} %copy-done.3), channel_id=1, source_target_pairs={{0,8},{24,16},{1,9},{25,17},{2,10},{26,18},{3,11},{27,19},{4,12},{... | collective-permute-start | bytes 786440 | tf_op jit(solution)/shard_map/ppermute | solution.py:564
  132.1 1.3 collective-permute-start.33
  133.7 0.7 collective-permute-start.31
  134.5 1.4 collective-permute-done.32.got_ref
  135.8 1.3 collective-permute-start.30
  137.1 3.2 %collective-permute-done.33.got_ref = bf16[8,128,128]{2,1,0:T(8,128)(2,1)S(1)} collective-permute-done((bf16[8,128,128]{2,1,0:T(8,128)(2,1)S(1)}, bf16[8,128,128]{2,1,0:T(8,128)(2,1)S(1)}, u32[]{:S(2)}, u32[]{:S(2)}) %collective-permute-start.33) | collective-permute-done | bytes 262176 | tf_op jit(solution)/shard_map/ppermute | solution.py:584
  140.3 2.2 %collective-permute-start.15 = (bf16[8,128,128]{2,1,0:T(8,128)(2,1)S(1)}, bf16[8,128,128]{2,1,0:T(8,128)(2,1)S(1)}, u32[]{:S(2)}, u32[]{:S(2)}) collective-permute-start(bf16[8,128,128]{2,1,0:T(8,128)(2,1)S(1)} %copy-done), channel_id=1, source_target_pairs={{0,8},{24,16},{1,9},{25,17},{2,10},{26,18},{3,11},{27,19},{4,12},{... | collective-permute-start | bytes 786440 | tf_op jit(solution)/shard_map/ppermute | solution.py:564
  142.7 0.7 collective-permute-start.38
  143.7 3.3 %finish.4 = (f32[64,128,128]{2,1,0:T(8,128)}, f32[8,128]{1,0:T(8,128)S(1)}) custom-call(s32[1]{0:T(128)} %bitcast.me_ref.refs_0_, s32[1,64]{1,0:T(1,128)S(1)} %copy-done.9, bf16[128,256]{1,0:T(8,128)(2,1)S(1)} %copy-done.1, bf16[8,128,128]{2,1,0:T(8,128)(2,1)S(1)} %collective-permute-done.34.refs_3_, ...), custom_call_target="tpu_custom_call", output_to_operand_aliasing={{0}: (5, {})} | custom-call | flops 134217728 | bytes 2621440 | tf_op jit(solution)/shard_map/finish/pallas_call | solution.py:487
  147.1 1.3 collective-permute-start.37
  148.6 0.7 collective-permute-start.36
  149.3 0.8 collective-permute-start.42
  150.0 2.8 %collective-permute-start.41 = (bf16[8,128,128]{2,1,0:T(8,128)(2,1)S(1)}, bf16[8,128,128]{2,1,0:T(8,128)(2,1)S(1)}, u32[]{:S(2)}, u32[]{:S(2)}) collective-permute-start(bf16[8,128,128]{2,1,0:T(8,128)(2,1)S(1)} %pick.11.after_ref), channel_id=1, source_target_pairs={{0,2},{1,3},{2,0},{3,1},{4,6},{5,7},{6,4},{7,5},{8,10},{9,11},{10,... | collective-permute-start | bytes 786440 | tf_op jit(solution)/shard_map/ppermute | solution.py:588
  152.9 1.4 collective-permute-start.40
  154.4 5.0 %collective-permute-done.37.got_ref = bf16[8,128,128]{2,1,0:T(8,128)(2,1)S(1)} collective-permute-done((bf16[8,128,128]{2,1,0:T(8,128)(2,1)S(1)}, bf16[8,128,128]{2,1,0:T(8,128)(2,1)S(1)}, u32[]{:S(2)}, u32[]{:S(2)}) %collective-permute-start.37) | collective-permute-done | bytes 262176 | tf_op jit(solution)/shard_map/ppermute | solution.py:584
  159.5 1.5 collective-permute-start.44
  161.1 1.3 collective-permute-start.39
  162.4 1.2 collective-permute-done.41.refs_3_
  163.6 3.3 %finish.5 = (f32[64,128,128]{2,1,0:T(8,128)}, f32[8,128]{1,0:T(8,128)S(1)}) custom-call(s32[1]{0:T(128)} %bitcast.me_ref.refs_0_, s32[1,64]{1,0:T(1,128)S(1)} %copy-done.9, bf16[128,256]{1,0:T(8,128)(2,1)S(1)} %copy-done.1, bf16[8,128,128]{2,1,0:T(8,128)(2,1)S(1)} %collective-permute-done.41.refs_3_, ...), custom_call_target="tpu_custom_call", output_to_operand_aliasing={{0}: (5, {})} | custom-call | flops 134217728 | bytes 2621440 | tf_op jit(solution)/shard_map/finish/pallas_call | solution.py:487
  167.1 1.5 bitcast_convert_fusion
  168.6 3.8 %collective-permute-done.39.got_ref = bf16[8,128,128]{2,1,0:T(8,128)(2,1)S(1)} collective-permute-done((bf16[8,128,128]{2,1,0:T(8,128)(2,1)S(1)}, bf16[8,128,128]{2,1,0:T(8,128)(2,1)S(1)}, u32[]{:S(2)}, u32[]{:S(2)}) %collective-permute-start.39) | collective-permute-done | bytes 262176 | tf_op jit(solution)/shard_map/ppermute | solution.py:584
  172.5 1.1 collective-permute-done.44.refs_3_
  173.6 3.9 %finish.6 = (f32[64,128,128]{2,1,0:T(8,128)}, f32[8,128]{1,0:T(8,128)}) custom-call(s32[1]{0:T(128)} %bitcast.me_ref.refs_0_, s32[1,64]{1,0:T(1,128)S(1)} %copy-done.9, bf16[128,256]{1,0:T(8,128)(2,1)S(1)} %copy-done.1, bf16[8,128,128]{2,1,0:T(8,128)(2,1)S(1)} %collective-permute-done.44.refs_3_, ...), custom_call_target="tpu_custom_call", output_to_operand_aliasing={{0}: (5, {})} | custom-call | flops 134217728 | bytes 2621440 | tf_op jit(solution)/shard_map/finish/pallas_call | solution.py:487
  177.5 3.9 %finish.7 = (f32[64,128,128]{2,1,0:T(8,128)}, f32[8,128]{1,0:T(8,128)}) custom-call(s32[1]{0:T(128)} %bitcast.me_ref.refs_0_, s32[1,64]{1,0:T(1,128)S(1)} %copy-done.9, bf16[128,256]{1,0:T(8,128)(2,1)S(1)} %copy-done.1, bf16[8,128,128]{2,1,0:T(8,128)(2,1)S(1)} %pick.15.refs_3_, ...), custom_call_target="tpu_custom_call", output_to_operand_aliasing={{0}: (5, {})} | custom-call | flops 134217728 | bytes 2621440 | tf_op jit(solution)/shard_map/finish/pallas_call | solution.py:487
  (109 shorter events, 5.2 us)
Async XLA Ops:
  5.6 5.3 %collective-permute-start = (bf16[36,128,128]{2,1,0:T(8,128)(2,1)}, bf16[36,128,128]{2,1,0:T(8,128)(2,1)S(1)}, u32[]{:S(2)}, u32[]{:S(2)}) collective-permute-start(bf16[36,128,128]{2,1,0:T(8,128)(2,1)} %get-tuple-element.27), channel_id=1, source_target_pairs={{0,1},{1,0},{2,3},{3,2},{4,5},{5,4},{6,7},{7,6},{8,9},{9,8},{10,11... | collective-permute-start | bytes 3538952 | tf_op jit(solution)/shard_map/ppermute | solution.py:588
  6.1 10.9 %collective-permute-start.1 = (bf16[8,128,128]{2,1,0:T(8,128)(2,1)}, bf16[8,128,128]{2,1,0:T(8,128)(2,1)S(1)}, u32[]{:S(2)}, u32[]{:S(2)}) collective-permute-start(bf16[8,128,128]{2,1,0:T(8,128)(2,1)} %get-tuple-element.28), channel_id=1, source_target_pairs={{0,6},{1,7},{2,4},{3,5},{4,2},{5,3},{6,0},{7,1},{8,14},{9,15},{10,... | collective-permute-start | bytes 786440 | tf_op jit(solution)/shard_map/ppermute | solution.py:588
  9.6 23.6 %collective-permute-start.2 = (bf16[8,128,128]{2,1,0:T(8,128)(2,1)}, bf16[8,128,128]{2,1,0:T(8,128)(2,1)S(1)}, u32[]{:S(2)}, u32[]{:S(2)}) collective-permute-start(bf16[8,128,128]{2,1,0:T(8,128)(2,1)} %get-tuple-element.29), channel_id=1, source_target_pairs={{0,2},{1,3},{2,0},{3,1},{4,6},{5,7},{6,4},{7,5},{8,10},{9,11},{10,... | collective-permute-start | bytes 786440 | tf_op jit(solution)/shard_map/ppermute | solution.py:588
  10.2 23.1 %collective-permute-start.3 = (bf16[8,128,128]{2,1,0:T(8,128)(2,1)}, bf16[8,128,128]{2,1,0:T(8,128)(2,1)S(1)}, u32[]{:S(2)}, u32[]{:S(2)}) collective-permute-start(bf16[8,128,128]{2,1,0:T(8,128)(2,1)} %get-tuple-element.30), channel_id=1, source_target_pairs={{0,4},{1,5},{2,6},{3,7},{4,0},{5,1},{6,2},{7,3},{8,12},{9,13},{10,... | collective-permute-start | bytes 786440 | tf_op jit(solution)/shard_map/ppermute | solution.py:588
  11.0 8.9 %copy-start.11 = (bf16[36,128,128]{2,1,0:T(8,128)(2,1)}, bf16[36,128,128]{2,1,0:T(8,128)(2,1)S(1)}, u32[]{:S(2)}) copy-start(bf16[36,128,128]{2,1,0:T(8,128)(2,1)S(1)} %collective-permute-done.after_ref.refs_1_.refs_0_) | copy-start | bytes 3538948
  11.1 22.2 %collective-permute-start.6 = (bf16[9,128,128]{2,1,0:T(8,128)(2,1)S(1)}, bf16[9,128,128]{2,1,0:T(8,128)(2,1)S(1)}, u32[]{:S(2)}, u32[]{:S(2)}) collective-permute-start(bf16[9,128,128]{2,1,0:T(8,128)(2,1)S(1)} %get-tuple-element.52), channel_id=1, source_target_pairs={{0,4},{1,5},{2,6},{3,7},{4,0},{5,1},{6,2},{7,3},{8,12},{9,13},{10,... | collective-permute-start | bytes 884744 | tf_op jit(solution)/shard_map/ppermute | solution.py:588
  13.0 20.3 %collective-permute-start.5 = (bf16[9,128,128]{2,1,0:T(8,128)(2,1)S(1)}, bf16[9,128,128]{2,1,0:T(8,128)(2,1)S(1)}, u32[]{:S(2)}, u32[]{:S(2)}) collective-permute-start(bf16[9,128,128]{2,1,0:T(8,128)(2,1)S(1)} %get-tuple-element.53), channel_id=1, source_target_pairs={{0,2},{1,3},{2,0},{3,1},{4,6},{5,7},{6,4},{7,5},{8,10},{9,11},{10,... | collective-permute-start | bytes 884744 | tf_op jit(solution)/shard_map/ppermute | solution.py:588
  17.1 16.2 %copy-start.18 = (bf16[8,128,128]{2,1,0:T(8,128)(2,1)}, bf16[8,128,128]{2,1,0:T(8,128)(2,1)S(1)}, u32[]{:S(2)}) copy-start(bf16[8,128,128]{2,1,0:T(8,128)(2,1)S(1)} %collective-permute-done.1.refs_2_) | copy-start | bytes 786436
  17.1 18.0 %collective-permute-start.4 = (bf16[9,128,128]{2,1,0:T(8,128)(2,1)S(1)}, bf16[9,128,128]{2,1,0:T(8,128)(2,1)S(1)}, u32[]{:S(2)}, u32[]{:S(2)}) collective-permute-start(bf16[9,128,128]{2,1,0:T(8,128)(2,1)S(1)} %get-tuple-element.54), channel_id=1, source_target_pairs={{0,6},{1,7},{2,4},{3,5},{4,2},{5,3},{6,0},{7,1},{8,14},{9,15},{10,... | collective-permute-start | bytes 884744 | tf_op jit(solution)/shard_map/ppermute | solution.py:588
  33.2 1.8 copy-start.19
  33.3 1.8 copy-start.20
  33.3 1.8 copy-start.13
  33.3 1.8 copy-start.14
  43.9 2.9 %collective-permute-start.7 = (f32[16,128,128]{2,1,0:T(8,128)}, f32[16,128,128]{2,1,0:T(8,128)S(1)}, u32[]{:S(2)}, u32[]{:S(2)}) collective-permute-start(f32[16,128,128]{2,1,0:T(8,128)} %get-tuple-element.32), channel_id=1, source_target_pairs={{0,1},{1,0},{2,3},{3,2},{4,5},{5,4},{6,7},{7,6},{8,9},{9,8},{10,11... | collective-permute-start | bytes 3145736 | tf_op jit(solution)/shard_map/ppermute | solution.py:588
  48.3 7.3 %collective-permute-start.8 = (bf16[4,128,128]{2,1,0:T(8,128)(2,1)S(1)}, bf16[4,128,128]{2,1,0:T(8,128)(2,1)S(1)}, u32[]{:S(2)}, u32[]{:S(2)}) collective-permute-start(bf16[4,128,128]{2,1,0:T(8,128)(2,1)S(1)} %get-tuple-element.55), channel_id=1, source_target_pairs={{0,6},{1,7},{2,4},{3,5},{4,2},{5,3},{6,0},{7,1},{8,14},{9,15},{10,... | collective-permute-start | bytes 393224 | tf_op jit(solution)/shard_map/ppermute | solution.py:588
  48.8 8.2 %collective-permute-start.10 = (bf16[4,128,128]{2,1,0:T(8,128)(2,1)S(1)}, bf16[4,128,128]{2,1,0:T(8,128)(2,1)S(1)}, u32[]{:S(2)}, u32[]{:S(2)}) collective-permute-start(bf16[4,128,128]{2,1,0:T(8,128)(2,1)S(1)} %get-tuple-element.56), channel_id=1, source_target_pairs={{0,4},{1,5},{2,6},{3,7},{4,0},{5,1},{6,2},{7,3},{8,12},{9,13},{10,... | collective-permute-start | bytes 393224 | tf_op jit(solution)/shard_map/ppermute | solution.py:588
  49.0 8.0 %collective-permute-start.9 = (bf16[4,128,128]{2,1,0:T(8,128)(2,1)S(1)}, bf16[4,128,128]{2,1,0:T(8,128)(2,1)S(1)}, u32[]{:S(2)}, u32[]{:S(2)}) collective-permute-start(bf16[4,128,128]{2,1,0:T(8,128)(2,1)S(1)} %get-tuple-element.57), channel_id=1, source_target_pairs={{0,2},{1,3},{2,0},{3,1},{4,6},{5,7},{6,4},{7,5},{8,10},{9,11},{10,... | collective-permute-start | bytes 393224 | tf_op jit(solution)/shard_map/ppermute | solution.py:588
  57.1 5.6 %collective-permute-start.13 = (bf16[4,128,128]{2,1,0:T(8,128)(2,1)S(1)}, bf16[4,128,128]{2,1,0:T(8,128)(2,1)S(1)}, u32[]{:S(2)}, u32[]{:S(2)}) collective-permute-start(bf16[4,128,128]{2,1,0:T(8,128)(2,1)S(1)} %fusion), channel_id=1, source_target_pairs={{0,4},{1,5},{2,6},{3,7},{4,0},{5,1},{6,2},{7,3},{8,12},{9,13},{10,... | collective-permute-start | bytes 393224 | tf_op jit(solution)/shard_map/ppermute | solution.py:588
  58.3 5.8 %collective-permute-start.12 = (bf16[4,128,128]{2,1,0:T(8,128)(2,1)S(1)}, bf16[4,128,128]{2,1,0:T(8,128)(2,1)S(1)}, u32[]{:S(2)}, u32[]{:S(2)}) collective-permute-start(bf16[4,128,128]{2,1,0:T(8,128)(2,1)S(1)} %fusion), channel_id=1, source_target_pairs={{0,2},{1,3},{2,0},{3,1},{4,6},{5,7},{6,4},{7,5},{8,10},{9,11},{10,... | collective-permute-start | bytes 393224 | tf_op jit(solution)/shard_map/ppermute | solution.py:588
  58.9 7.2 %collective-permute-start.11 = (bf16[4,128,128]{2,1,0:T(8,128)(2,1)S(1)}, bf16[4,128,128]{2,1,0:T(8,128)(2,1)S(1)}, u32[]{:S(2)}, u32[]{:S(2)}) collective-permute-start(bf16[4,128,128]{2,1,0:T(8,128)(2,1)S(1)} %fusion), channel_id=1, source_target_pairs={{0,6},{1,7},{2,4},{3,5},{4,2},{5,3},{6,0},{7,1},{8,14},{9,15},{10,... | collective-permute-start | bytes 393224 | tf_op jit(solution)/shard_map/ppermute | solution.py:588
  66.2 2.0 %copy-start.12 = (bf16[16,128,128]{2,1,0:T(8,128)(2,1)}, bf16[16,128,128]{2,1,0:T(8,128)(2,1)S(1)}, u32[]{:S(2)}) copy-start(bf16[16,128,128]{2,1,0:T(8,128)(2,1)S(1)} %pad_maximum_fusion.even_in_ref) | copy-start | bytes 1572868
  66.2 2.0 %collective-permute-start.14 = (bf16[16,128,128]{2,1,0:T(8,128)(2,1)S(1)}, bf16[16,128,128]{2,1,0:T(8,128)(2,1)S(1)}, u32[]{:S(2)}, u32[]{:S(2)}) collective-permute-start(bf16[16,128,128]{2,1,0:T(8,128)(2,1)S(1)} %pad_maximum_fusion.even_in_ref), channel_id=1, source_target_pairs={{0,1},{1,0},{2,3},{3,2},{4,5},{5,4},{6,7},{7,6},{8,9},{9,8},{10,11... | collective-permute-start | bytes 1572872 | tf_op jit(solution)/shard_map/ppermute | solution.py:588
  77.4 8.3 %collective-permute-start.18 = (bf16[8,128,128]{2,1,0:T(8,128)(2,1)}, bf16[8,128,128]{2,1,0:T(8,128)(2,1)S(1)}, u32[]{:S(2)}, u32[]{:S(2)}) collective-permute-start(bf16[8,128,128]{2,1,0:T(8,128)(2,1)} %get-tuple-element.37.mine_ref), channel_id=1, source_target_pairs={{0,8},{24,16},{1,9},{25,17},{2,10},{26,18},{3,11},{27,19},{4,12},{... | collective-permute-start | bytes 786440 | tf_op jit(solution)/shard_map/ppermute | solution.py:564
  78.7 23.8 %collective-permute-start.17 = (bf16[8,128,128]{2,1,0:T(8,128)(2,1)}, bf16[8,128,128]{2,1,0:T(8,128)(2,1)S(1)}, u32[]{:S(2)}, u32[]{:S(2)}) collective-permute-start(bf16[8,128,128]{2,1,0:T(8,128)(2,1)} %get-tuple-element.36.mine_ref), channel_id=1, source_target_pairs={{0,8},{24,16},{1,9},{25,17},{2,10},{26,18},{3,11},{27,19},{4,12},{... | collective-permute-start | bytes 786440 | tf_op jit(solution)/shard_map/ppermute | solution.py:564
  80.0 5.7 %copy-start.2 = (bf16[8,128,128]{2,1,0:T(8,128)(2,1)S(1)}, bf16[8,128,128]{2,1,0:T(8,128)(2,1)}, u32[]{:S(2)}) copy-start(bf16[8,128,128]{2,1,0:T(8,128)(2,1)} %get-tuple-element.37.mine_ref) | copy-start | bytes 786436
  80.0 7.1 %copy-start.7 = (bf16[8,128,128]{2,1,0:T(8,128)(2,1)S(1)}, bf16[8,128,128]{2,1,0:T(8,128)(2,1)}, u32[]{:S(2)}) copy-start(bf16[8,128,128]{2,1,0:T(8,128)(2,1)} %get-tuple-element.39.mine_ref) | copy-start | bytes 786436
  80.0 22.5 %copy-start.8 = (bf16[8,128,128]{2,1,0:T(8,128)(2,1)S(1)}, bf16[8,128,128]{2,1,0:T(8,128)(2,1)}, u32[]{:S(2)}) copy-start(bf16[8,128,128]{2,1,0:T(8,128)(2,1)} %get-tuple-element.36.mine_ref) | copy-start | bytes 786436
  80.0 24.8 %copy-start.6 = (bf16[8,128,128]{2,1,0:T(8,128)(2,1)S(1)}, bf16[8,128,128]{2,1,0:T(8,128)(2,1)}, u32[]{:S(2)}) copy-start(bf16[8,128,128]{2,1,0:T(8,128)(2,1)} %get-tuple-element.40.mine_ref) | copy-start | bytes 786436
  83.8 28.5 %copy-start.5 = (bf16[8,128,128]{2,1,0:T(8,128)(2,1)S(1)}, bf16[8,128,128]{2,1,0:T(8,128)(2,1)}, u32[]{:S(2)}) copy-start(bf16[8,128,128]{2,1,0:T(8,128)(2,1)} %get-tuple-element.35.mine_ref) | copy-start | bytes 786436
  83.8 34.1 %copy-start.4 = (bf16[8,128,128]{2,1,0:T(8,128)(2,1)S(1)}, bf16[8,128,128]{2,1,0:T(8,128)(2,1)}, u32[]{:S(2)}) copy-start(bf16[8,128,128]{2,1,0:T(8,128)(2,1)} %get-tuple-element.41.mine_ref) | copy-start | bytes 786436
  86.4 16.9 %collective-permute-start.21 = (bf16[8,128,128]{2,1,0:T(8,128)(2,1)S(1)}, bf16[8,128,128]{2,1,0:T(8,128)(2,1)S(1)}, u32[]{:S(2)}, u32[]{:S(2)}) collective-permute-start(bf16[8,128,128]{2,1,0:T(8,128)(2,1)S(1)} %merge.16.after_ref.mine_ref), channel_id=1, source_target_pairs={{8,16},{16,8},{9,17},{17,9},{10,18},{18,10},{11,19},{19,11},{12,20... | collective-permute-start | bytes 786440 | tf_op jit(solution)/shard_map/ppermute | solution.py:584
  87.1 23.0 %collective-permute-start.20 = (bf16[8,128,128]{2,1,0:T(8,128)(2,1)S(1)}, bf16[8,128,128]{2,1,0:T(8,128)(2,1)S(1)}, u32[]{:S(2)}, u32[]{:S(2)}) collective-permute-start(bf16[8,128,128]{2,1,0:T(8,128)(2,1)S(1)} %copy-done.7), channel_id=1, source_target_pairs={{0,8},{24,16},{1,9},{25,17},{2,10},{26,18},{3,11},{27,19},{4,12},{... | collective-permute-start | bytes 786440 | tf_op jit(solution)/shard_map/ppermute | solution.py:564
  102.6 8.3 %collective-permute-start.19 = (bf16[8,128,128]{2,1,0:T(8,128)(2,1)S(1)}, bf16[8,128,128]{2,1,0:T(8,128)(2,1)S(1)}, u32[]{:S(2)}, u32[]{:S(2)}) collective-permute-start(bf16[8,128,128]{2,1,0:T(8,128)(2,1)S(1)} %merge.17.after_ref.mine_ref), channel_id=1, source_target_pairs={{8,16},{16,8},{9,17},{17,9},{10,18},{18,10},{11,19},{19,11},{12,20... | collective-permute-start | bytes 786440 | tf_op jit(solution)/shard_map/ppermute | solution.py:584
  103.4 21.6 %copy-start.3 = (bf16[8,128,128]{2,1,0:T(8,128)(2,1)S(1)}, bf16[8,128,128]{2,1,0:T(8,128)(2,1)}, u32[]{:S(2)}) copy-start(bf16[8,128,128]{2,1,0:T(8,128)(2,1)} %get-tuple-element.42.mine_ref) | copy-start | bytes 786436
  103.4 13.6 %collective-permute-start.25 = (bf16[8,128,128]{2,1,0:T(8,128)(2,1)S(1)}, bf16[8,128,128]{2,1,0:T(8,128)(2,1)S(1)}, u32[]{:S(2)}, u32[]{:S(2)}) collective-permute-start(bf16[8,128,128]{2,1,0:T(8,128)(2,1)S(1)} %merge.18.after_ref.mine_ref), channel_id=1, source_target_pairs={{8,0},{16,24},{9,1},{17,25},{10,2},{18,26},{11,3},{19,27},{12,4},{... | collective-permute-start | bytes 786440 | tf_op jit(solution)/shard_map/ppermute | solution.py:584
  104.8 12.2 %collective-permute-start.24 = (bf16[8,128,128]{2,1,0:T(8,128)(2,1)S(1)}, bf16[8,128,128]{2,1,0:T(8,128)(2,1)S(1)}, u32[]{:S(2)}, u32[]{:S(2)}) collective-permute-start(bf16[8,128,128]{2,1,0:T(8,128)(2,1)S(1)} %copy-done.6), channel_id=1, source_target_pairs={{0,8},{24,16},{1,9},{25,17},{2,10},{26,18},{3,11},{27,19},{4,12},{... | collective-permute-start | bytes 786440 | tf_op jit(solution)/shard_map/ppermute | solution.py:564
  110.2 12.5 %collective-permute-start.23 = (bf16[8,128,128]{2,1,0:T(8,128)(2,1)S(1)}, bf16[8,128,128]{2,1,0:T(8,128)(2,1)S(1)}, u32[]{:S(2)}, u32[]{:S(2)}) collective-permute-start(bf16[8,128,128]{2,1,0:T(8,128)(2,1)S(1)} %merge.19.after_ref.mine_ref), channel_id=1, source_target_pairs={{8,16},{16,8},{9,17},{17,9},{10,18},{18,10},{11,19},{19,11},{12,20... | collective-permute-start | bytes 786440 | tf_op jit(solution)/shard_map/ppermute | solution.py:584
  111.0 13.1 %collective-permute-start.22 = (bf16[8,128,128]{2,1,0:T(8,128)(2,1)S(1)}, bf16[8,128,128]{2,1,0:T(8,128)(2,1)S(1)}, u32[]{:S(2)}, u32[]{:S(2)}) collective-permute-start(bf16[8,128,128]{2,1,0:T(8,128)(2,1)S(1)} %merge.20.after_ref.token_ref.mine_ref), channel_id=1, source_target_pairs={{8,0},{16,24},{9,1},{17,25},{10,2},{18,26},{11,3},{19,27},{12,4},{... | collective-permute-start | bytes 786440 | tf_op jit(solution)/shard_map/ppermute | solution.py:584
  112.3 11.9 %collective-permute-start.16 = (bf16[8,128,128]{2,1,0:T(8,128)(2,1)S(1)}, bf16[8,128,128]{2,1,0:T(8,128)(2,1)S(1)}, u32[]{:S(2)}, u32[]{:S(2)}) collective-permute-start(bf16[8,128,128]{2,1,0:T(8,128)(2,1)S(1)} %copy-done.5), channel_id=1, source_target_pairs={{0,8},{24,16},{1,9},{25,17},{2,10},{26,18},{3,11},{27,19},{4,12},{... | collective-permute-start | bytes 786440 | tf_op jit(solution)/shard_map/ppermute | solution.py:564
  117.1 23.2 %copy-start = (bf16[8,128,128]{2,1,0:T(8,128)(2,1)S(1)}, bf16[8,128,128]{2,1,0:T(8,128)(2,1)}, u32[]{:S(2)}) copy-start(bf16[8,128,128]{2,1,0:T(8,128)(2,1)} %get-tuple-element.34.after_ref.mine_ref) | copy-start | bytes 786436
  117.1 14.8 %collective-permute-start.29 = (bf16[8,128,128]{2,1,0:T(8,128)(2,1)S(1)}, bf16[8,128,128]{2,1,0:T(8,128)(2,1)S(1)}, u32[]{:S(2)}, u32[]{:S(2)}) collective-permute-start(bf16[8,128,128]{2,1,0:T(8,128)(2,1)S(1)} %merge.21.after_ref.mine_ref), channel_id=1, source_target_pairs={{8,16},{16,8},{9,17},{17,9},{10,18},{18,10},{11,19},{19,11},{12,20... | collective-permute-start | bytes 786440 | tf_op jit(solution)/shard_map/ppermute | solution.py:584
  118.0 15.4 %collective-permute-start.27 = (bf16[8,128,128]{2,1,0:T(8,128)(2,1)S(1)}, bf16[8,128,128]{2,1,0:T(8,128)(2,1)S(1)}, u32[]{:S(2)}, u32[]{:S(2)}) collective-permute-start(bf16[8,128,128]{2,1,0:T(8,128)(2,1)S(1)} %copy-done.4), channel_id=1, source_target_pairs={{0,8},{24,16},{1,9},{25,17},{2,10},{26,18},{3,11},{27,19},{4,12},{... | collective-permute-start | bytes 786440 | tf_op jit(solution)/shard_map/ppermute | solution.py:564
  122.8 10.6 %collective-permute-start.28 = (bf16[8,128,128]{2,1,0:T(8,128)(2,1)S(1)}, bf16[8,128,128]{2,1,0:T(8,128)(2,1)S(1)}, u32[]{:S(2)}, u32[]{:S(2)}) collective-permute-start(bf16[8,128,128]{2,1,0:T(8,128)(2,1)S(1)} %merge.22.after_ref.token_ref.mine_ref), channel_id=1, source_target_pairs={{8,0},{16,24},{9,1},{17,25},{10,2},{18,26},{11,3},{19,27},{12,4},{... | collective-permute-start | bytes 786440 | tf_op jit(solution)/shard_map/ppermute | solution.py:584
  124.2 19.5 %copy-start.1 = (bf16[128,256]{1,0:T(8,128)(2,1)S(1)}, bf16[128,256]{1,0:T(8,128)(2,1)}, u32[]{:S(2)}) copy-start(bf16[128,256]{1,0:T(8,128)(2,1)} %constant.19.clone.refs_2_) | copy-start | bytes 196612
  124.2 19.5 %copy-start.9 = (s32[1,64]{1,0:T(1,128)S(1)}, s32[1,64]{1,0:T(1,128)}, u32[]{:S(2)}) copy-start(s32[1,64]{1,0:T(1,128)} %refs_1_.7) | copy-start | bytes 772
  124.3 9.4 %collective-permute-start.26 = (bf16[8,128,128]{2,1,0:T(8,128)(2,1)S(1)}, bf16[8,128,128]{2,1,0:T(8,128)(2,1)S(1)}, u32[]{:S(2)}, u32[]{:S(2)}) collective-permute-start(bf16[8,128,128]{2,1,0:T(8,128)(2,1)S(1)} %merge.23.after_ref.mine_ref), channel_id=1, source_target_pairs={{8,16},{16,8},{9,17},{17,9},{10,18},{18,10},{11,19},{19,11},{12,20... | collective-permute-start | bytes 786440 | tf_op jit(solution)/shard_map/ppermute | solution.py:584
  125.0 10.8 %collective-permute-start.32 = (bf16[8,128,128]{2,1,0:T(8,128)(2,1)S(1)}, bf16[8,128,128]{2,1,0:T(8,128)(2,1)S(1)}, u32[]{:S(2)}, u32[]{:S(2)}) collective-permute-start(bf16[8,128,128]{2,1,0:T(8,128)(2,1)S(1)} %copy-done.3), channel_id=1, source_target_pairs={{0,8},{24,16},{1,9},{25,17},{2,10},{26,18},{3,11},{27,19},{4,12},{... | collective-permute-start | bytes 786440 | tf_op jit(solution)/shard_map/ppermute | solution.py:564
  132.1 8.3 %collective-permute-start.33 = (bf16[8,128,128]{2,1,0:T(8,128)(2,1)S(1)}, bf16[8,128,128]{2,1,0:T(8,128)(2,1)S(1)}, u32[]{:S(2)}, u32[]{:S(2)}) collective-permute-start(bf16[8,128,128]{2,1,0:T(8,128)(2,1)S(1)} %merge.24.after_ref.token_ref.mine_ref), channel_id=1, source_target_pairs={{8,0},{16,24},{9,1},{17,25},{10,2},{18,26},{11,3},{19,27},{12,4},{... | collective-permute-start | bytes 786440 | tf_op jit(solution)/shard_map/ppermute | solution.py:584
  133.4 9.3 %collective-permute-start.35 = (bf16[8,128,128]{2,1,0:T(8,128)(2,1)S(1)}, bf16[8,128,128]{2,1,0:T(8,128)(2,1)S(1)}, u32[]{:S(2)}, u32[]{:S(2)}) collective-permute-start(bf16[8,128,128]{2,1,0:T(8,128)(2,1)S(1)} %pick.8.after_ref), channel_id=1, source_target_pairs={{0,7},{1,6},{2,5},{3,4},{4,3},{5,2},{6,1},{7,0},{8,15},{9,14},{10,... | collective-permute-start | bytes 786440 | tf_op jit(solution)/shard_map/ppermute | solution.py:588
  133.5 10.2 %collective-permute-start.34 = (bf16[8,128,128]{2,1,0:T(8,128)(2,1)S(1)}, bf16[8,128,128]{2,1,0:T(8,128)(2,1)S(1)}, u32[]{:S(2)}, u32[]{:S(2)}) collective-permute-start(bf16[8,128,128]{2,1,0:T(8,128)(2,1)S(1)} %pick.9.after_ref), channel_id=1, source_target_pairs={{0,6},{1,7},{2,4},{3,5},{4,2},{5,3},{6,0},{7,1},{8,14},{9,15},{10,... | collective-permute-start | bytes 786440 | tf_op jit(solution)/shard_map/ppermute | solution.py:588
  133.7 13.3 %collective-permute-start.31 = (bf16[8,128,128]{2,1,0:T(8,128)(2,1)S(1)}, bf16[8,128,128]{2,1,0:T(8,128)(2,1)S(1)}, u32[]{:S(2)}, u32[]{:S(2)}) collective-permute-start(bf16[8,128,128]{2,1,0:T(8,128)(2,1)S(1)} %merge.25.after_ref.mine_ref), channel_id=1, source_target_pairs={{8,16},{16,8},{9,17},{17,9},{10,18},{18,10},{11,19},{19,11},{12,20... | collective-permute-start | bytes 786440 | tf_op jit(solution)/shard_map/ppermute | solution.py:584
  135.8 12.6 %collective-permute-start.30 = (bf16[8,128,128]{2,1,0:T(8,128)(2,1)S(1)}, bf16[8,128,128]{2,1,0:T(8,128)(2,1)S(1)}, u32[]{:S(2)}, u32[]{:S(2)}) collective-permute-start(bf16[8,128,128]{2,1,0:T(8,128)(2,1)S(1)} %merge.26.after_ref.token_ref.mine_ref), channel_id=1, source_target_pairs={{8,0},{16,24},{9,1},{17,25},{10,2},{18,26},{11,3},{19,27},{12,4},{... | collective-permute-start | bytes 786440 | tf_op jit(solution)/shard_map/ppermute | solution.py:584
  140.3 8.2 %collective-permute-start.15 = (bf16[8,128,128]{2,1,0:T(8,128)(2,1)S(1)}, bf16[8,128,128]{2,1,0:T(8,128)(2,1)S(1)}, u32[]{:S(2)}, u32[]{:S(2)}) collective-permute-start(bf16[8,128,128]{2,1,0:T(8,128)(2,1)S(1)} %copy-done), channel_id=1, source_target_pairs={{0,8},{24,16},{1,9},{25,17},{2,10},{26,18},{3,11},{27,19},{4,12},{... | collective-permute-start | bytes 786440 | tf_op jit(solution)/shard_map/ppermute | solution.py:564
  142.7 10.2 %collective-permute-start.38 = (bf16[8,128,128]{2,1,0:T(8,128)(2,1)S(1)}, bf16[8,128,128]{2,1,0:T(8,128)(2,1)S(1)}, u32[]{:S(2)}, u32[]{:S(2)}) collective-permute-start(bf16[8,128,128]{2,1,0:T(8,128)(2,1)S(1)} %merge.27.after_ref.mine_ref), channel_id=1, source_target_pairs={{8,16},{16,8},{9,17},{17,9},{10,18},{18,10},{11,19},{19,11},{12,20... | collective-permute-start | bytes 786440 | tf_op jit(solution)/shard_map/ppermute | solution.py:584
  147.1 12.3 %collective-permute-start.37 = (bf16[8,128,128]{2,1,0:T(8,128)(2,1)S(1)}, bf16[8,128,128]{2,1,0:T(8,128)(2,1)S(1)}, u32[]{:S(2)}, u32[]{:S(2)}) collective-permute-start(bf16[8,128,128]{2,1,0:T(8,128)(2,1)S(1)} %merge.28.after_ref.mine_ref), channel_id=1, source_target_pairs={{8,0},{16,24},{9,1},{17,25},{10,2},{18,26},{11,3},{19,27},{12,4},{... | collective-permute-start | bytes 786440 | tf_op jit(solution)/shard_map/ppermute | solution.py:584
  148.6 10.9 %collective-permute-start.36 = (bf16[8,128,128]{2,1,0:T(8,128)(2,1)S(1)}, bf16[8,128,128]{2,1,0:T(8,128)(2,1)S(1)}, u32[]{:S(2)}, u32[]{:S(2)}) collective-permute-start(bf16[8,128,128]{2,1,0:T(8,128)(2,1)S(1)} %merge.29.after_ref.mine_ref), channel_id=1, source_target_pairs={{8,16},{16,8},{9,17},{17,9},{10,18},{18,10},{11,19},{19,11},{12,20... | collective-permute-start | bytes 786440 | tf_op jit(solution)/shard_map/ppermute | solution.py:584
  149.3 11.8 %collective-permute-start.42 = (bf16[8,128,128]{2,1,0:T(8,128)(2,1)S(1)}, bf16[8,128,128]{2,1,0:T(8,128)(2,1)S(1)}, u32[]{:S(2)}, u32[]{:S(2)}) collective-permute-start(bf16[8,128,128]{2,1,0:T(8,128)(2,1)S(1)} %pick.10.after_ref), channel_id=1, source_target_pairs={{0,3},{1,2},{2,1},{3,0},{4,7},{5,6},{6,5},{7,4},{8,11},{9,10},{10,... | collective-permute-start | bytes 786440 | tf_op jit(solution)/shard_map/ppermute | solution.py:588
  150.0 13.5 %collective-permute-start.41 = (bf16[8,128,128]{2,1,0:T(8,128)(2,1)S(1)}, bf16[8,128,128]{2,1,0:T(8,128)(2,1)S(1)}, u32[]{:S(2)}, u32[]{:S(2)}) collective-permute-start(bf16[8,128,128]{2,1,0:T(8,128)(2,1)S(1)} %pick.11.after_ref), channel_id=1, source_target_pairs={{0,2},{1,3},{2,0},{3,1},{4,6},{5,7},{6,4},{7,5},{8,10},{9,11},{10,... | collective-permute-start | bytes 786440 | tf_op jit(solution)/shard_map/ppermute | solution.py:588
  152.9 14.1 %copy-start.16 = (bf16[32,128,128]{2,1,0:T(8,128)(2,1)S(1)}, bf16[32,128,128]{2,1,0:T(8,128)(2,1)}, u32[]{:S(2)}) copy-start(bf16[32,128,128]{2,1,0:T(8,128)(2,1)} %get-tuple-element.33) | copy-start | bytes 3145732
  152.9 14.0 %collective-permute-start.40 = (bf16[8,128,128]{2,1,0:T(8,128)(2,1)S(1)}, bf16[8,128,128]{2,1,0:T(8,128)(2,1)S(1)}, u32[]{:S(2)}, u32[]{:S(2)}) collective-permute-start(bf16[8,128,128]{2,1,0:T(8,128)(2,1)S(1)} %merge.30.after_ref.mine_ref), channel_id=1, source_target_pairs={{8,0},{16,24},{9,1},{17,25},{10,2},{18,26},{11,3},{19,27},{12,4},{... | collective-permute-start | bytes 786440 | tf_op jit(solution)/shard_map/ppermute | solution.py:584
  159.4 13.1 %collective-permute-start.45 = (bf16[8,128,128]{2,1,0:T(8,128)(2,1)S(1)}, bf16[8,128,128]{2,1,0:T(8,128)(2,1)S(1)}, u32[]{:S(2)}, u32[]{:S(2)}) collective-permute-start(bf16[8,128,128]{2,1,0:T(8,128)(2,1)S(1)} %pick.12.after_ref), channel_id=1, source_target_pairs={{0,5},{1,4},{2,7},{3,6},{4,1},{5,0},{6,3},{7,2},{8,13},{9,12},{10,... | collective-permute-start | bytes 786440 | tf_op jit(solution)/shard_map/ppermute | solution.py:588
  159.5 14.1 %collective-permute-start.44 = (bf16[8,128,128]{2,1,0:T(8,128)(2,1)S(1)}, bf16[8,128,128]{2,1,0:T(8,128)(2,1)S(1)}, u32[]{:S(2)}, u32[]{:S(2)}) collective-permute-start(bf16[8,128,128]{2,1,0:T(8,128)(2,1)S(1)} %pick.13.after_ref), channel_id=1, source_target_pairs={{0,4},{1,5},{2,6},{3,7},{4,0},{5,1},{6,2},{7,3},{8,12},{9,13},{10,... | collective-permute-start | bytes 786440 | tf_op jit(solution)/shard_map/ppermute | solution.py:588
  161.1 11.3 %collective-permute-start.39 = (bf16[8,128,128]{2,1,0:T(8,128)(2,1)S(1)}, bf16[8,128,128]{2,1,0:T(8,128)(2,1)S(1)}, u32[]{:S(2)}, u32[]{:S(2)}) collective-permute-start(bf16[8,128,128]{2,1,0:T(8,128)(2,1)S(1)} %merge.31.after_ref.mine_ref), channel_id=1, source_target_pairs={{8,0},{16,24},{9,1},{17,25},{10,2},{18,26},{11,3},{19,27},{12,4},{... | collective-permute-start | bytes 786440 | tf_op jit(solution)/shard_map/ppermute | solution.py:584
  167.0 10.6 %collective-permute-start.43 = (bf16[8,128,128]{2,1,0:T(8,128)(2,1)S(1)}, bf16[8,128,128]{2,1,0:T(8,128)(2,1)S(1)}, u32[]{:S(2)}, u32[]{:S(2)}) collective-permute-start(bf16[8,128,128]{2,1,0:T(8,128)(2,1)S(1)} %pick.14.after_ref), channel_id=1, source_target_pairs={{0,1},{1,0},{2,3},{3,2},{4,5},{5,4},{6,7},{7,6},{8,9},{9,8},{10,11... | collective-permute-start | bytes 786440 | tf_op jit(solution)/shard_map/ppermute | solution.py:588
  (3 other events, 2.2 us)

commit v3 on v2

--- a/solution.py
+++ b/solution.py
@@ -273,9 +273,8 @@
     for offset in reversed(range(peers)):
         part = acc_ref[pl.ds((me ^ offset) * each, each)]
         half_ref[offset] = part.astype(half_ref.dtype)
-        stores.append(
-            pltpu.make_async_copy(half_ref.at[offset], out_refs[offset], put.at[offset])
-        )
+        target = out_refs[offset // 2].at[pl.ds(offset % 2 * each, each)]
+        stores.append(pltpu.make_async_copy(half_ref.at[offset], target, put.at[offset]))
         stores[-1].start()
     wait_all(stores)
 
@@ -287,10 +286,10 @@
     image = (RB_DEV, BLK, width)
     outs = pl.pallas_call(
         adjoint_body,
-        out_shape=[jax.ShapeDtypeStruct(piece, jnp.bfloat16)] * peers
+        out_shape=[jax.ShapeDtypeStruct((2 * piece[0], *piece[1:]), jnp.bfloat16)] * (peers // 2)
         + [jax.ShapeDtypeStruct(image, jnp.bfloat16)],
         in_specs=[SMEM_SPEC] * 4 + [ANY_SPEC] * 3,
-        out_specs=[ANY_SPEC] * (peers + 1),
+        out_specs=[ANY_SPEC] * (peers // 2 + 1),
         scratch_shapes=[
             pltpu.VMEM(sens.shape, sens.dtype),
             pltpu.VMEM(image, jnp.bfloat16),
@@ -547,6 +546,25 @@
         ),
         name="pick",
     )(take, got, mine, after, token)
+
+
+def second_half_body(whole_ref, after_ref, out_ref):
+    out_ref[...] = whole_ref[out_ref.shape[0] :]
+
+
+def second_half(whole, after):
+    shape = (whole.shape[0] // 2, *whole.shape[1:])
+    return pl.pallas_call(
+        second_half_body,
+        out_shape=jax.ShapeDtypeStruct(shape, whole.dtype),
+        in_specs=[VMEM_SPEC, ANY_SPEC],
+        out_specs=VMEM_SPEC,
+        compiler_params=pltpu.CompilerParams(vmem_limit_bytes=SMALL),
+        cost_estimate=pl.CostEstimate(
+            flops=0, bytes_accessed=2 * whole.size, transcendentals=0
+        ),
+        name="second_half",
+    )(whole, after)
 
 
 def line_sums(parts, axis, after, deliver):
@@ -631,30 +649,35 @@
         [partner, *[passed[j] for j in range(1, half)]],
     )
     normal = smooth.reshape(blocks, BLK, width)
-    order = [2 * j + odd for j in far for odd in (1, 0)] + [1, 0]
-    returned, waiting, tokens = {}, [], []
-
-    def end_one():
+    order = [*far, 0]
+    waiting, tokens = [], []
+
+    def end_one(place):
         nonlocal normal
-        j = waiting.pop(0)
-        even, odd = returned[2 * j], returned[2 * j + 1]
-        normal, token = finish(me, send_order, even, odd, normal, 2 * j)
+        even, other, j = waiting.pop(place)
+        if other is None:
+            other = swap(second_half(even, tokens[-1]), "cols", 1)
+        normal, token = finish(me, send_order, even, other, normal, 2 * j)
         tokens.append(token)
 
     def deliver(k, take, got, mine, after):
-        if k % 2 == 0 and k >= 4:
-            end_one()
+        if k >= 2:
+            end_one(0)
         token = tokens[-1] if tokens else after
-        o = order[k]
+        j = order[k]
+        if j == 0:
+            even, other = pick(take, got, mine, after, token, 2)
+            waiting.append((even, swap(other, "cols", 1), j))
+            return even
         [total] = pick(take, got, mine, after, token, 1)
-        returned[o] = swap(total, "cols", o) if o else total
-        if k % 2:
-            waiting.append(o // 2)
+        even = swap(total, "cols", 2 * j)
+        other = None if k == half - 2 else swap(even[per_peer:], "cols", 1)
+        waiting.append((even, other, j))
         return total
 
-    line_sums([partial_cols[o] for o in order], "rows", first, deliver)
+    line_sums([partial_cols[j] for j in order], "rows", first, deliver)
     while waiting:
-        end_one()
+        end_one(-1)
     return (data_image, normal.reshape(cell_count, width))
 
 

time: 182 us -> 179 us (0.984)
  starting transfers between devices: 81.5 us -> 48.5 us
  waiting for transfers between devices: 37.6 us -> 64.3 us
  Pallas kernels: 54.6 us -> 58.7 us
    ppermute x8 -> x4, starting transfers between devices: 41.8 us -> 18.6 us  [line_sums(): got = [lax.ppermute(part, axis, stages[0][0]) for part in parts]]
    ppermute x22, waiting for transfers between devices: 22.3 us -> 32 us  [swap(): lax.ppermute(piece, axis, [(c, c ^ offset) for c in range(lax.axis_size(a...]
    ppermute x8 -> x4, waiting for transfers between devices: 3.24 us -> 12.2 us  [line_sums(): got = [lax.ppermute(part, axis, stages[0][0]) for part in parts]]
    ppermute x16 -> x8, waiting for transfers between devices: 12.1 us -> 20.1 us  [line_sums(): got[k] = lax.ppermute(state[k], axis, stages[s + 1][0])]
    ppermute x16 -> x8, starting transfers between devices: 16.1 us -> 8.26 us  [line_sums(): got[k] = lax.ppermute(state[k], axis, stages[s + 1][0])]
    pallas_call x8 -> x4, Pallas kernels: 0.59 us -> 2.63 us  [pick(): pl.pallas_call(pick_body, out_shape=[jax.ShapeDtypeStruct(shape, mine.dty...]
    ppermute x22, starting transfers between devices: 23.6 us -> 21.7 us  [swap(): lax.ppermute(piece, axis, [(c, c ^ offset) for c in range(lax.axis_size(a...]
    pallas_call x1 -> x2, Pallas kernels: 8.42 us -> 9.8 us  [the longest x1 9.78 us: adjoint(): pl.pallas_call(adjoint_body, out_shape=[jax.ShapeDtypeStruct((2 * piece[0...]
  transfers between devices with their start and end apart: 46 -> 34, of which waited for: 17 -> 19; matrix products, arithmetic and copies ran while one was open for 1% -> 1% of each run, Pallas kernels for 16% -> 17%
where the time goes in v3:
time: 179 us
  waiting for transfers between devices  64.3 us (36%)
  Pallas kernels  58.7 us (33%)
  starting transfers between devices  48.5 us (27%)
  other arithmetic  3.06 us (2%)
  local copies, waits for them, and re-layouts  2.4 us (1%)
  between operations  2.05 us (1%)
    ppermute x22, waiting for transfers between devices, swap(): lax.ppermute(piece, axis, [(c, c ^ offset) for c in range(lax.axis_size(a...  32 us
    ppermute x22, starting transfers between devices, swap(): lax.ppermute(piece, axis, [(c, c ^ offset) for c in range(lax.axis_size(a...  21.7 us
    ppermute x8, waiting for transfers between devices, line_sums(): got[k] = lax.ppermute(state[k], axis, stages[s + 1][0])  20.1 us
    ppermute x4, starting transfers between devices, line_sums(): got = [lax.ppermute(part, axis, stages[0][0]) for part in parts]  18.6 us
    pallas_call x4, Pallas kernels, finish(): pl.pallas_call(lambda *refs: finish_body(*refs, offset=offset), out_shape...  13.9 us
    pallas_call x1, Pallas kernels, smoothing(): pl.pallas_call(smooth_body, out_shape=jax.ShapeDtypeStruct((cells, width)...  13.3 us
    ppermute x4, waiting for transfers between devices, line_sums(): got = [lax.ppermute(part, axis, stages[0][0]) for part in parts]  12.2 us
    pallas_call x1, Pallas kernels, adjoint(): pl.pallas_call(adjoint_body, out_shape=[jax.ShapeDtypeStruct((2 * piece[0...  9.78 us
  transfers between devices with their start and end apart: 34, of which 19 were waited for; matrix products, arithmetic and copies ran while one was open for 1% of the time, Pallas kernels for 17%

profile of v3, /device:TPU:0, one launch (start us, length us, event | category | flops | bytes accessed | tf_op | source)
XLA Modules:
  0.0 179.0 jit_solution(7197597005882125293)
XLA Ops:
  0.6 5.0 %analyze.1 = (bf16[8,128,128]{2,1,0:T(8,128)(2,1)}, bf16[8,128,128]{2,1,0:T(8,128)(2,1)}, bf16[8,128,128]{2,1,0:T(8,128)(2,1)}, bf16[8,128,128]{2,1,0:T(8,128)(2,1)}, bf16[36,128,128]{2,1,0:T(8,128)(2,1)}) custom-call(s32[1]{0:T(128)} %bitcast.me_ref.refs_0_, s32[1,64]{1,0:T(1,128)} %refs_1_.7, f32[64,128,128]{2,1,0:T(8,128)} %bitcast.14), custom_call_target="tpu_custom_call" | custom-call | flops 536870912 | bytes 6291456 | tf_op jit(solution)/shard_map/analyze/pallas_call | solution.py:145
  5.6 0.5 collective-permute-start
  6.2 3.5 %collective-permute-start.1 = (bf16[8,128,128]{2,1,0:T(8,128)(2,1)}, bf16[8,128,128]{2,1,0:T(8,128)(2,1)S(1)}, u32[]{:S(2)}, u32[]{:S(2)}) collective-permute-start(bf16[8,128,128]{2,1,0:T(8,128)(2,1)} %get-tuple-element.27), channel_id=1, source_target_pairs={{0,6},{1,7},{2,4},{3,5},{4,2},{5,3},{6,0},{7,1},{8,14},{9,15},{10,... | collective-permute-start | bytes 786440 | tf_op jit(solution)/shard_map/ppermute | solution.py:606
  9.7 0.5 collective-permute-start.2
  10.2 0.1 collective-permute-start.3
  11.1 2.0 %collective-permute-start.6 = (bf16[9,128,128]{2,1,0:T(8,128)(2,1)S(1)}, bf16[9,128,128]{2,1,0:T(8,128)(2,1)S(1)}, u32[]{:S(2)}, u32[]{:S(2)}) collective-permute-start(bf16[9,128,128]{2,1,0:T(8,128)(2,1)S(1)} %get-tuple-element.50), channel_id=1, source_target_pairs={{0,4},{1,5},{2,6},{3,7},{4,0},{5,1},{6,2},{7,3},{8,12},{9,13},{10,... | collective-permute-start | bytes 884744 | tf_op jit(solution)/shard_map/ppermute | solution.py:606
  13.0 1.5 collective-permute-start.5
  14.5 2.5 %collective-permute-done.1.refs_2_ = bf16[8,128,128]{2,1,0:T(8,128)(2,1)S(1)} collective-permute-done((bf16[8,128,128]{2,1,0:T(8,128)(2,1)}, bf16[8,128,128]{2,1,0:T(8,128)(2,1)S(1)}, u32[]{:S(2)}, u32[]{:S(2)}) %collective-permute-start.1) | collective-permute-done | bytes 262176 | tf_op jit(solution)/shard_map/ppermute | solution.py:606
  17.1 2.8 %collective-permute-start.4 = (bf16[9,128,128]{2,1,0:T(8,128)(2,1)S(1)}, bf16[9,128,128]{2,1,0:T(8,128)(2,1)S(1)}, u32[]{:S(2)}, u32[]{:S(2)}) collective-permute-start(bf16[9,128,128]{2,1,0:T(8,128)(2,1)S(1)} %get-tuple-element.52), channel_id=1, source_target_pairs={{0,6},{1,7},{2,4},{3,5},{4,2},{5,3},{6,0},{7,1},{8,14},{9,15},{10,... | collective-permute-start | bytes 884744 | tf_op jit(solution)/shard_map/ppermute | solution.py:606
  19.9 13.3 %smoothing.1.refs_8_.base_ref = f32[8192,128]{1,0:T(8,128)} custom-call(s32[1]{0:T(128)} %bitcast.3.offset_ref, f32[8192,128]{1,0:T(8,128)} %model_ref.3, s32[4,8192]{1,0:T(4,128)} %near_ref.3, f32[4,8192]{1,0:T(4,128)} %weight_ref.3, bf16[36,128,128]{2,1,0:T(8,128)(2,1)} %copy-done.7), custom_call_target="tpu_custom_call" | custom-call | flops 3221225472 | bytes 16777216 | tf_op jit(solution)/shard_map/smoothing/pallas_call | solution.py:367
  33.4 1.7 collective-permute-done.4.refs_5_.refs_3_
  35.1 0.7 copy-done.11
  35.8 9.4 %forward.1 = (f32[16,128,128]{2,1,0:T(8,128)}, f32[16,128,128]{2,1,0:T(8,128)}) custom-call(s32[1]{0:T(128)} %bitcast.me_ref.refs_0_, s32[1,384]{1,0:T(1,128)} %rows_ref.3, s32[1,384]{1,0:T(1,128)} %cols_ref.3, s32[1,1]{1,0:T(1,128)S(6)} %copy.24.count_ref, bf16[384,128,128]{2,1,0:T(8,128)(2,1)} %bitcast.12, bf16[8,128,128]{2,1,0:T(8,128)(2,1)} %get-tuple-element.25.refs_0_, ...), custom_call_target="tpu_custom_call" | custom-call | flops 1610612736 | bytes 12582912 | tf_op jit(solution)/shard_map/forward/pallas_call | solution.py:227
  45.3 2.9 %collective-permute-done.7 = f32[16,128,128]{2,1,0:T(8,128)S(1)} collective-permute-done((f32[16,128,128]{2,1,0:T(8,128)}, f32[16,128,128]{2,1,0:T(8,128)S(1)}, u32[]{:S(2)}, u32[]{:S(2)}) %collective-permute-start.7) | collective-permute-done | bytes 1048608 | tf_op jit(solution)/shard_map/ppermute | solution.py:606
  48.2 1.4 fusion.1
  49.6 4.9 %collective-permute-start.8 = (bf16[4,128,128]{2,1,0:T(8,128)(2,1)S(1)}, bf16[4,128,128]{2,1,0:T(8,128)(2,1)S(1)}, u32[]{:S(2)}, u32[]{:S(2)}) collective-permute-start(bf16[4,128,128]{2,1,0:T(8,128)(2,1)S(1)} %get-tuple-element.53), channel_id=1, source_target_pairs={{0,6},{1,7},{2,4},{3,5},{4,2},{5,3},{6,0},{7,1},{8,14},{9,15},{10,... | collective-permute-start | bytes 393224 | tf_op jit(solution)/shard_map/ppermute | solution.py:606
  54.5 0.6 collective-permute-start.9
  55.1 3.3 %collective-permute-done.8 = bf16[4,128,128]{2,1,0:T(8,128)(2,1)S(1)} collective-permute-done((bf16[4,128,128]{2,1,0:T(8,128)(2,1)S(1)}, bf16[4,128,128]{2,1,0:T(8,128)(2,1)S(1)}, u32[]{:S(2)}, u32[]{:S(2)}) %collective-permute-start.8) | collective-permute-done | bytes 131104 | tf_op jit(solution)/shard_map/ppermute | solution.py:606
  58.4 2.7 %collective-permute-done.10 = bf16[4,128,128]{2,1,0:T(8,128)(2,1)S(1)} collective-permute-done((bf16[4,128,128]{2,1,0:T(8,128)(2,1)S(1)}, bf16[4,128,128]{2,1,0:T(8,128)(2,1)S(1)}, u32[]{:S(2)}, u32[]{:S(2)}) %collective-permute-start.10) | collective-permute-done | bytes 131104 | tf_op jit(solution)/shard_map/ppermute | solution.py:606
  61.2 0.6 collective-permute-start.13
  61.8 1.8 %collective-permute-start.12 = (bf16[4,128,128]{2,1,0:T(8,128)(2,1)S(1)}, bf16[4,128,128]{2,1,0:T(8,128)(2,1)S(1)}, u32[]{:S(2)}, u32[]{:S(2)}) collective-permute-start(bf16[4,128,128]{2,1,0:T(8,128)(2,1)S(1)} %fusion), channel_id=1, source_target_pairs={{0,2},{1,3},{2,0},{3,1},{4,6},{5,7},{6,4},{7,5},{8,10},{9,11},{10,... | collective-permute-start | bytes 393224 | tf_op jit(solution)/shard_map/ppermute | solution.py:606
  63.6 1.1 collective-permute-start.11
  64.7 2.0 %collective-permute-done.13 = bf16[4,128,128]{2,1,0:T(8,128)(2,1)S(1)} collective-permute-done((bf16[4,128,128]{2,1,0:T(8,128)(2,1)S(1)}, bf16[4,128,128]{2,1,0:T(8,128)(2,1)S(1)}, u32[]{:S(2)}, u32[]{:S(2)}) %collective-permute-start.13) | collective-permute-done | bytes 131104 | tf_op jit(solution)/shard_map/ppermute | solution.py:606
  66.7 1.0 collective-permute-done.12
  67.8 2.9 %collective-permute-done.11 = bf16[4,128,128]{2,1,0:T(8,128)(2,1)S(1)} collective-permute-done((bf16[4,128,128]{2,1,0:T(8,128)(2,1)S(1)}, bf16[4,128,128]{2,1,0:T(8,128)(2,1)S(1)}, u32[]{:S(2)}, u32[]{:S(2)}) %collective-permute-start.11) | collective-permute-done | bytes 131104 | tf_op jit(solution)/shard_map/ppermute | solution.py:606
  70.8 1.9 %collective-permute-done.14.odd_in_ref = bf16[16,128,128]{2,1,0:T(8,128)(2,1)S(1)} collective-permute-done((bf16[16,128,128]{2,1,0:T(8,128)(2,1)S(1)}, bf16[16,128,128]{2,1,0:T(8,128)(2,1)S(1)}, u32[]{:S(2)}, u32[]{:S(2)}) %collective-permute-start.14) | collective-permute-done | bytes 524320 | tf_op jit(solution)/shard_map/ppermute | solution.py:606
  72.7 0.8 copy-done.13
  73.5 9.8 %adjoint.1 = (bf16[16,128,128]{2,1,0:T(8,128)(2,1)}, bf16[16,128,128]{2,1,0:T(8,128)(2,1)}, bf16[16,128,128]{2,1,0:T(8,128)(2,1)}, bf16[16,128,128]{2,1,0:T(8,128)(2,1)}, bf16[32,128,128]{2,1,0:T(8,128)(2,1)}) custom-call(s32[1]{0:T(128)} %bitcast.me_ref.refs_0_, s32[1,384]{1,0:T(1,128)} %rows_ref.3, s32[1,384]{1,0:T(1,128)} %cols_ref.3, ...), custom_call_target="tpu_custom_call" | custom-call | flops 1610612736 | bytes 12582912 | tf_op jit(solution)/shard_map/adjoint/pallas_call | solution.py:287
  83.3 1.3 collective-permute-start.16
  84.7 1.3 collective-permute-start.18
  86.0 3.8 %edges.1 = (f32[8192,128]{1,0:T(8,128)}, f32[8,128]{1,0:T(8,128)}) custom-call(s32[1]{0:T(128)} %bitcast.me_ref.refs_0_, s32[1]{0:T(128)} %bitcast.3.offset_ref, f32[8192,128]{1,0:T(8,128)} %model_ref.3, s32[4,8192]{1,0:T(4,128)} %near_ref.3, f32[4,8192]{1,0:T(4,128)} %weight_ref.3, ...), custom_call_target="tpu_custom_call", output_to_operand_aliasing={{0}: (5, {})} | custom-call | flops 100663296 | bytes 524288 | tf_op jit(solution)/shard_map/edges/pallas_call | solution.py:432
  89.8 7.4 %collective-permute-done.16.got_ref = bf16[16,128,128]{2,1,0:T(8,128)(2,1)S(1)} collective-permute-done((bf16[16,128,128]{2,1,0:T(8,128)(2,1)}, bf16[16,128,128]{2,1,0:T(8,128)(2,1)S(1)}, u32[]{:S(2)}, u32[]{:S(2)}) %collective-permute-start.16) | collective-permute-done | bytes 524320 | tf_op jit(solution)/shard_map/ppermute | solution.py:582
  97.2 0.7 copy-done.6
  98.0 0.7 collective-permute-start.17
  98.7 5.5 %collective-permute-start.15 = (bf16[16,128,128]{2,1,0:T(8,128)(2,1)S(1)}, bf16[16,128,128]{2,1,0:T(8,128)(2,1)S(1)}, u32[]{:S(2)}, u32[]{:S(2)}) collective-permute-start(bf16[16,128,128]{2,1,0:T(8,128)(2,1)S(1)} %copy-done.3), channel_id=1, source_target_pairs={{0,8},{24,16},{1,9},{25,17},{2,10},{26,18},{3,11},{27,19},{4,12},{... | collective-permute-start | bytes 1572872 | tf_op jit(solution)/shard_map/ppermute | solution.py:582
  104.2 4.2 %collective-permute-done.18.got_ref = bf16[16,128,128]{2,1,0:T(8,128)(2,1)S(1)} collective-permute-done((bf16[16,128,128]{2,1,0:T(8,128)(2,1)}, bf16[16,128,128]{2,1,0:T(8,128)(2,1)S(1)}, u32[]{:S(2)}, u32[]{:S(2)}) %collective-permute-start.18) | collective-permute-done | bytes 524320 | tf_op jit(solution)/shard_map/ppermute | solution.py:582
  108.5 0.7 collective-permute-start.22
  109.2 0.1 merge.10.after_ref.mine_ref
  109.4 1.3 collective-permute-start.21
  110.7 10.4 %collective-permute-start.20 = (bf16[16,128,128]{2,1,0:T(8,128)(2,1)S(1)}, bf16[16,128,128]{2,1,0:T(8,128)(2,1)S(1)}, u32[]{:S(2)}, u32[]{:S(2)}) collective-permute-start(bf16[16,128,128]{2,1,0:T(8,128)(2,1)S(1)} %copy-done), channel_id=1, source_target_pairs={{0,8},{24,16},{1,9},{25,17},{2,10},{26,18},{3,11},{27,19},{4,12},{... | collective-permute-start | bytes 1572872 | tf_op jit(solution)/shard_map/ppermute | solution.py:582
  121.3 0.7 collective-permute-start.19
  122.1 1.3 collective-permute-start.25
  123.4 6.5 %collective-permute-done.21.got_ref = bf16[16,128,128]{2,1,0:T(8,128)(2,1)} collective-permute-done((bf16[16,128,128]{2,1,0:T(8,128)(2,1)S(1)}, bf16[16,128,128]{2,1,0:T(8,128)(2,1)}, u32[]{:S(2)}, u32[]{:S(2)}) %collective-permute-start.21) | collective-permute-done | bytes 524320 | tf_op jit(solution)/shard_map/ppermute | solution.py:602
  129.9 1.2 pick.4.after_ref
  131.2 0.6 collective-permute-done.20.got_ref
  132.0 0.8 collective-permute-start.24
  132.9 8.2 %collective-permute-done.25.got_ref = bf16[16,128,128]{2,1,0:T(8,128)(2,1)} collective-permute-done((bf16[16,128,128]{2,1,0:T(8,128)(2,1)S(1)}, bf16[16,128,128]{2,1,0:T(8,128)(2,1)}, u32[]{:S(2)}, u32[]{:S(2)}) %collective-permute-start.25) | collective-permute-done | bytes 524320 | tf_op jit(solution)/shard_map/ppermute | solution.py:602
  141.2 1.2 pick.5.after_ref
  142.4 1.3 collective-permute-start.23
  143.7 3.2 %collective-permute-done.26.refs_3_ = bf16[16,128,128]{2,1,0:T(8,128)(2,1)S(1)} collective-permute-done((bf16[16,128,128]{2,1,0:T(8,128)(2,1)S(1)}, bf16[16,128,128]{2,1,0:T(8,128)(2,1)S(1)}, u32[]{:S(2)}, u32[]{:S(2)}) %collective-permute-start.26) | collective-permute-done | bytes 524320 | tf_op jit(solution)/shard_map/ppermute | solution.py:606
  147.2 1.5 collective-permute-start.29
  148.7 6.4 %collective-permute-done.30.refs_3_ = bf16[16,128,128]{2,1,0:T(8,128)(2,1)S(1)} collective-permute-done((bf16[16,128,128]{2,1,0:T(8,128)(2,1)S(1)}, bf16[16,128,128]{2,1,0:T(8,128)(2,1)S(1)}, u32[]{:S(2)}, u32[]{:S(2)}) %collective-permute-start.30) | collective-permute-done | bytes 524320 | tf_op jit(solution)/shard_map/ppermute | solution.py:606
  155.2 3.3 %finish.4 = (f32[64,128,128]{2,1,0:T(8,128)}, f32[8,128]{1,0:T(8,128)S(1)}) custom-call(s32[1]{0:T(128)} %bitcast.me_ref.refs_0_, s32[1,64]{1,0:T(1,128)S(1)} %copy-done.5, bf16[128,256]{1,0:T(8,128)(2,1)S(1)} %copy-done.1, bf16[16,128,128]{2,1,0:T(8,128)(2,1)S(1)} %collective-permute-done.26.refs_3_, ...), custom_call_target="tpu_custom_call", output_to_operand_aliasing={{0}: (5, {})} | custom-call | flops 134217728 | bytes 2621440 | tf_op jit(solution)/shard_map/finish/pallas_call | solution.py:486
  158.5 0.7 collective-permute-done.23.got_ref
  159.2 0.1 pick.6.after_ref
  159.3 0.9 collective-permute-start.28
  160.2 3.3 %finish.5 = (f32[64,128,128]{2,1,0:T(8,128)}, f32[8,128]{1,0:T(8,128)S(1)}) custom-call(s32[1]{0:T(128)} %bitcast.me_ref.refs_0_, s32[1,64]{1,0:T(1,128)S(1)} %copy-done.5, bf16[128,256]{1,0:T(8,128)(2,1)S(1)} %copy-done.1, bf16[16,128,128]{2,1,0:T(8,128)(2,1)S(1)} %collective-permute-done.30.refs_3_, ...), custom_call_target="tpu_custom_call", output_to_operand_aliasing={{0}: (5, {})} | custom-call | flops 134217728 | bytes 2621440 | tf_op jit(solution)/shard_map/finish/pallas_call | solution.py:486
  163.5 4.6 %collective-permute-done.29.got_ref = bf16[16,128,128]{2,1,0:T(8,128)(2,1)S(1)} collective-permute-done((bf16[16,128,128]{2,1,0:T(8,128)(2,1)S(1)}, bf16[16,128,128]{2,1,0:T(8,128)(2,1)S(1)}, u32[]{:S(2)}, u32[]{:S(2)}) %collective-permute-start.29) | collective-permute-done | bytes 524320 | tf_op jit(solution)/shard_map/ppermute | solution.py:602
  168.2 0.1 pick.7
  168.4 1.5 collective-permute-done.32.refs_4_
  169.9 3.3 %finish.6 = (f32[64,128,128]{2,1,0:T(8,128)}, f32[8,128]{1,0:T(8,128)S(1)}) custom-call(s32[1]{0:T(128)} %bitcast.me_ref.refs_0_, s32[1,64]{1,0:T(1,128)S(1)} %copy-done.5, bf16[128,256]{1,0:T(8,128)(2,1)S(1)} %copy-done.1, bf16[8,128,128]{2,1,0:T(8,128)(2,1)S(1)} %get-tuple-element.42.refs_3_, ...), custom_call_target="tpu_custom_call", output_to_operand_aliasing={{0}: (5, {})} | custom-call | flops 134217728 | bytes 2621440 | tf_op jit(solution)/shard_map/finish/pallas_call | solution.py:486
  173.2 0.2 collective-permute-start.33
  173.4 1.5 bitcast_convert_fusion
  175.0 3.9 %finish.7 = (f32[64,128,128]{2,1,0:T(8,128)}, f32[8,128]{1,0:T(8,128)}) custom-call(s32[1]{0:T(128)} %bitcast.me_ref.refs_0_, s32[1,64]{1,0:T(1,128)S(1)} %copy-done.5, bf16[128,256]{1,0:T(8,128)(2,1)S(1)} %copy-done.1, bf16[16,128,128]{2,1,0:T(8,128)(2,1)S(1)} %collective-permute-done.28.whole_ref.refs_3_, ...), custom_call_target="tpu_custom_call", output_to_operand_aliasing={{0}: (5, {})} | custom-call | flops 134217728 | bytes 2621440 | tf_op jit(solution)/shard_map/finish/pallas_call | solution.py:486
  (68 shorter events, 1.8 us)
Async XLA Ops:
  5.6 5.4 %collective-permute-start = (bf16[36,128,128]{2,1,0:T(8,128)(2,1)}, bf16[36,128,128]{2,1,0:T(8,128)(2,1)S(1)}, u32[]{:S(2)}, u32[]{:S(2)}) collective-permute-start(bf16[36,128,128]{2,1,0:T(8,128)(2,1)} %get-tuple-element.26), channel_id=1, source_target_pairs={{0,1},{1,0},{2,3},{3,2},{4,5},{5,4},{6,7},{7,6},{8,9},{9,8},{10,11... | collective-permute-start | bytes 3538952 | tf_op jit(solution)/shard_map/ppermute | solution.py:606
  6.2 10.9 %collective-permute-start.1 = (bf16[8,128,128]{2,1,0:T(8,128)(2,1)}, bf16[8,128,128]{2,1,0:T(8,128)(2,1)S(1)}, u32[]{:S(2)}, u32[]{:S(2)}) collective-permute-start(bf16[8,128,128]{2,1,0:T(8,128)(2,1)} %get-tuple-element.27), channel_id=1, source_target_pairs={{0,6},{1,7},{2,4},{3,5},{4,2},{5,3},{6,0},{7,1},{8,14},{9,15},{10,... | collective-permute-start | bytes 786440 | tf_op jit(solution)/shard_map/ppermute | solution.py:606
  9.7 23.6 %collective-permute-start.2 = (bf16[8,128,128]{2,1,0:T(8,128)(2,1)}, bf16[8,128,128]{2,1,0:T(8,128)(2,1)S(1)}, u32[]{:S(2)}, u32[]{:S(2)}) collective-permute-start(bf16[8,128,128]{2,1,0:T(8,128)(2,1)} %get-tuple-element.28), channel_id=1, source_target_pairs={{0,2},{1,3},{2,0},{3,1},{4,6},{5,7},{6,4},{7,5},{8,10},{9,11},{10,... | collective-permute-start | bytes 786440 | tf_op jit(solution)/shard_map/ppermute | solution.py:606
  10.2 23.1 %collective-permute-start.3 = (bf16[8,128,128]{2,1,0:T(8,128)(2,1)}, bf16[8,128,128]{2,1,0:T(8,128)(2,1)S(1)}, u32[]{:S(2)}, u32[]{:S(2)}) collective-permute-start(bf16[8,128,128]{2,1,0:T(8,128)(2,1)} %get-tuple-element.29), channel_id=1, source_target_pairs={{0,4},{1,5},{2,6},{3,7},{4,0},{5,1},{6,2},{7,3},{8,12},{9,13},{10,... | collective-permute-start | bytes 786440 | tf_op jit(solution)/shard_map/ppermute | solution.py:606
  11.0 8.9 %copy-start.7 = (bf16[36,128,128]{2,1,0:T(8,128)(2,1)}, bf16[36,128,128]{2,1,0:T(8,128)(2,1)S(1)}, u32[]{:S(2)}) copy-start(bf16[36,128,128]{2,1,0:T(8,128)(2,1)S(1)} %collective-permute-done.after_ref.refs_1_.refs_0_) | copy-start | bytes 3538948
  11.1 22.2 %collective-permute-start.6 = (bf16[9,128,128]{2,1,0:T(8,128)(2,1)S(1)}, bf16[9,128,128]{2,1,0:T(8,128)(2,1)S(1)}, u32[]{:S(2)}, u32[]{:S(2)}) collective-permute-start(bf16[9,128,128]{2,1,0:T(8,128)(2,1)S(1)} %get-tuple-element.50), channel_id=1, source_target_pairs={{0,4},{1,5},{2,6},{3,7},{4,0},{5,1},{6,2},{7,3},{8,12},{9,13},{10,... | collective-permute-start | bytes 884744 | tf_op jit(solution)/shard_map/ppermute | solution.py:606
  13.0 20.3 %collective-permute-start.5 = (bf16[9,128,128]{2,1,0:T(8,128)(2,1)S(1)}, bf16[9,128,128]{2,1,0:T(8,128)(2,1)S(1)}, u32[]{:S(2)}, u32[]{:S(2)}) collective-permute-start(bf16[9,128,128]{2,1,0:T(8,128)(2,1)S(1)} %get-tuple-element.51), channel_id=1, source_target_pairs={{0,2},{1,3},{2,0},{3,1},{4,6},{5,7},{6,4},{7,5},{8,10},{9,11},{10,... | collective-permute-start | bytes 884744 | tf_op jit(solution)/shard_map/ppermute | solution.py:606
  17.1 16.2 %copy-start.14 = (bf16[8,128,128]{2,1,0:T(8,128)(2,1)}, bf16[8,128,128]{2,1,0:T(8,128)(2,1)S(1)}, u32[]{:S(2)}) copy-start(bf16[8,128,128]{2,1,0:T(8,128)(2,1)S(1)} %collective-permute-done.1.refs_2_) | copy-start | bytes 786436
  17.1 18.0 %collective-permute-start.4 = (bf16[9,128,128]{2,1,0:T(8,128)(2,1)S(1)}, bf16[9,128,128]{2,1,0:T(8,128)(2,1)S(1)}, u32[]{:S(2)}, u32[]{:S(2)}) collective-permute-start(bf16[9,128,128]{2,1,0:T(8,128)(2,1)S(1)} %get-tuple-element.52), channel_id=1, source_target_pairs={{0,6},{1,7},{2,4},{3,5},{4,2},{5,3},{6,0},{7,1},{8,14},{9,15},{10,... | collective-permute-start | bytes 884744 | tf_op jit(solution)/shard_map/ppermute | solution.py:606
  33.3 1.8 %copy-start.15 = (bf16[8,128,128]{2,1,0:T(8,128)(2,1)}, bf16[8,128,128]{2,1,0:T(8,128)(2,1)S(1)}, u32[]{:S(2)}) copy-start(bf16[8,128,128]{2,1,0:T(8,128)(2,1)S(1)} %collective-permute-done.2.refs_3_) | copy-start | bytes 786436
  33.3 1.8 %copy-start.16 = (bf16[8,128,128]{2,1,0:T(8,128)(2,1)}, bf16[8,128,128]{2,1,0:T(8,128)(2,1)S(1)}, u32[]{:S(2)}) copy-start(bf16[8,128,128]{2,1,0:T(8,128)(2,1)S(1)} %collective-permute-done.3.refs_4_) | copy-start | bytes 786436
  33.3 1.8 copy-start.9
  33.3 1.8 copy-start.10
  35.1 0.7 copy-start.11
  45.2 2.9 %collective-permute-start.7 = (f32[16,128,128]{2,1,0:T(8,128)}, f32[16,128,128]{2,1,0:T(8,128)S(1)}, u32[]{:S(2)}, u32[]{:S(2)}) collective-permute-start(f32[16,128,128]{2,1,0:T(8,128)} %get-tuple-element.31), channel_id=1, source_target_pairs={{0,1},{1,0},{2,3},{3,2},{4,5},{5,4},{6,7},{7,6},{8,9},{9,8},{10,11... | collective-permute-start | bytes 3145736 | tf_op jit(solution)/shard_map/ppermute | solution.py:606
  49.6 8.8 %collective-permute-start.8 = (bf16[4,128,128]{2,1,0:T(8,128)(2,1)S(1)}, bf16[4,128,128]{2,1,0:T(8,128)(2,1)S(1)}, u32[]{:S(2)}, u32[]{:S(2)}) collective-permute-start(bf16[4,128,128]{2,1,0:T(8,128)(2,1)S(1)} %get-tuple-element.53), channel_id=1, source_target_pairs={{0,6},{1,7},{2,4},{3,5},{4,2},{5,3},{6,0},{7,1},{8,14},{9,15},{10,... | collective-permute-start | bytes 393224 | tf_op jit(solution)/shard_map/ppermute | solution.py:606
  54.5 6.6 %collective-permute-start.10 = (bf16[4,128,128]{2,1,0:T(8,128)(2,1)S(1)}, bf16[4,128,128]{2,1,0:T(8,128)(2,1)S(1)}, u32[]{:S(2)}, u32[]{:S(2)}) collective-permute-start(bf16[4,128,128]{2,1,0:T(8,128)(2,1)S(1)} %get-tuple-element.54), channel_id=1, source_target_pairs={{0,4},{1,5},{2,6},{3,7},{4,0},{5,1},{6,2},{7,3},{8,12},{9,13},{10,... | collective-permute-start | bytes 393224 | tf_op jit(solution)/shard_map/ppermute | solution.py:606
  54.5 6.6 %collective-permute-start.9 = (bf16[4,128,128]{2,1,0:T(8,128)(2,1)S(1)}, bf16[4,128,128]{2,1,0:T(8,128)(2,1)S(1)}, u32[]{:S(2)}, u32[]{:S(2)}) collective-permute-start(bf16[4,128,128]{2,1,0:T(8,128)(2,1)S(1)} %get-tuple-element.55), channel_id=1, source_target_pairs={{0,2},{1,3},{2,0},{3,1},{4,6},{5,7},{6,4},{7,5},{8,10},{9,11},{10,... | collective-permute-start | bytes 393224 | tf_op jit(solution)/shard_map/ppermute | solution.py:606
  61.2 5.6 %collective-permute-start.13 = (bf16[4,128,128]{2,1,0:T(8,128)(2,1)S(1)}, bf16[4,128,128]{2,1,0:T(8,128)(2,1)S(1)}, u32[]{:S(2)}, u32[]{:S(2)}) collective-permute-start(bf16[4,128,128]{2,1,0:T(8,128)(2,1)S(1)} %fusion), channel_id=1, source_target_pairs={{0,4},{1,5},{2,6},{3,7},{4,0},{5,1},{6,2},{7,3},{8,12},{9,13},{10,... | collective-permute-start | bytes 393224 | tf_op jit(solution)/shard_map/ppermute | solution.py:606
  61.8 6.0 %collective-permute-start.12 = (bf16[4,128,128]{2,1,0:T(8,128)(2,1)S(1)}, bf16[4,128,128]{2,1,0:T(8,128)(2,1)S(1)}, u32[]{:S(2)}, u32[]{:S(2)}) collective-permute-start(bf16[4,128,128]{2,1,0:T(8,128)(2,1)S(1)} %fusion), channel_id=1, source_target_pairs={{0,2},{1,3},{2,0},{3,1},{4,6},{5,7},{6,4},{7,5},{8,10},{9,11},{10,... | collective-permute-start | bytes 393224 | tf_op jit(solution)/shard_map/ppermute | solution.py:606
  63.6 7.0 %collective-permute-start.11 = (bf16[4,128,128]{2,1,0:T(8,128)(2,1)S(1)}, bf16[4,128,128]{2,1,0:T(8,128)(2,1)S(1)}, u32[]{:S(2)}, u32[]{:S(2)}) collective-permute-start(bf16[4,128,128]{2,1,0:T(8,128)(2,1)S(1)} %fusion), channel_id=1, source_target_pairs={{0,6},{1,7},{2,4},{3,5},{4,2},{5,3},{6,0},{7,1},{8,14},{9,15},{10,... | collective-permute-start | bytes 393224 | tf_op jit(solution)/shard_map/ppermute | solution.py:606
  70.7 2.0 %copy-start.8 = (bf16[16,128,128]{2,1,0:T(8,128)(2,1)}, bf16[16,128,128]{2,1,0:T(8,128)(2,1)S(1)}, u32[]{:S(2)}) copy-start(bf16[16,128,128]{2,1,0:T(8,128)(2,1)S(1)} %pad_maximum_fusion.even_in_ref) | copy-start | bytes 1572868
  70.7 2.0 %collective-permute-start.14 = (bf16[16,128,128]{2,1,0:T(8,128)(2,1)S(1)}, bf16[16,128,128]{2,1,0:T(8,128)(2,1)S(1)}, u32[]{:S(2)}, u32[]{:S(2)}) collective-permute-start(bf16[16,128,128]{2,1,0:T(8,128)(2,1)S(1)} %pad_maximum_fusion.even_in_ref), channel_id=1, source_target_pairs={{0,1},{1,0},{2,3},{3,2},{4,5},{5,4},{6,7},{7,6},{8,9},{9,8},{10,11... | collective-permute-start | bytes 1572872 | tf_op jit(solution)/shard_map/ppermute | solution.py:606
  72.7 0.8 copy-start.13
  83.3 13.8 %collective-permute-start.16 = (bf16[16,128,128]{2,1,0:T(8,128)(2,1)}, bf16[16,128,128]{2,1,0:T(8,128)(2,1)S(1)}, u32[]{:S(2)}, u32[]{:S(2)}) collective-permute-start(bf16[16,128,128]{2,1,0:T(8,128)(2,1)} %get-tuple-element.34.mine_ref), channel_id=1, source_target_pairs={{0,8},{24,16},{1,9},{25,17},{2,10},{26,18},{3,11},{27,19},{4,12},{... | collective-permute-start | bytes 1572872 | tf_op jit(solution)/shard_map/ppermute | solution.py:582
  84.7 23.8 %collective-permute-start.18 = (bf16[16,128,128]{2,1,0:T(8,128)(2,1)}, bf16[16,128,128]{2,1,0:T(8,128)(2,1)S(1)}, u32[]{:S(2)}, u32[]{:S(2)}) collective-permute-start(bf16[16,128,128]{2,1,0:T(8,128)(2,1)} %get-tuple-element.37.mine_ref), channel_id=1, source_target_pairs={{0,8},{24,16},{1,9},{25,17},{2,10},{26,18},{3,11},{27,19},{4,12},{... | collective-permute-start | bytes 1572872 | tf_op jit(solution)/shard_map/ppermute | solution.py:582
  86.0 11.2 %copy-start.2 = (bf16[16,128,128]{2,1,0:T(8,128)(2,1)S(1)}, bf16[16,128,128]{2,1,0:T(8,128)(2,1)}, u32[]{:S(2)}) copy-start(bf16[16,128,128]{2,1,0:T(8,128)(2,1)} %get-tuple-element.34.mine_ref) | copy-start | bytes 1572868
  86.0 12.7 %copy-start.3 = (bf16[16,128,128]{2,1,0:T(8,128)(2,1)S(1)}, bf16[16,128,128]{2,1,0:T(8,128)(2,1)}, u32[]{:S(2)}) copy-start(bf16[16,128,128]{2,1,0:T(8,128)(2,1)} %get-tuple-element.33.mine_ref) | copy-start | bytes 1572868
  86.0 22.4 %copy-start.4 = (bf16[16,128,128]{2,1,0:T(8,128)(2,1)S(1)}, bf16[16,128,128]{2,1,0:T(8,128)(2,1)}, u32[]{:S(2)}) copy-start(bf16[16,128,128]{2,1,0:T(8,128)(2,1)} %get-tuple-element.37.mine_ref) | copy-start | bytes 1572868
  89.8 20.9 %copy-start = (bf16[16,128,128]{2,1,0:T(8,128)(2,1)S(1)}, bf16[16,128,128]{2,1,0:T(8,128)(2,1)}, u32[]{:S(2)}) copy-start(bf16[16,128,128]{2,1,0:T(8,128)(2,1)} %get-tuple-element.35.after_ref.mine_ref) | copy-start | bytes 1572868
  97.2 0.7 copy-start.6
  98.0 11.3 %collective-permute-start.17 = (bf16[16,128,128]{2,1,0:T(8,128)(2,1)S(1)}, bf16[16,128,128]{2,1,0:T(8,128)(2,1)S(1)}, u32[]{:S(2)}, u32[]{:S(2)}) collective-permute-start(bf16[16,128,128]{2,1,0:T(8,128)(2,1)S(1)} %merge.8.after_ref.mine_ref), channel_id=1, source_target_pairs={{8,16},{16,8},{9,17},{17,9},{10,18},{18,10},{11,19},{19,11},{12,20... | collective-permute-start | bytes 1572872 | tf_op jit(solution)/shard_map/ppermute | solution.py:602
  98.7 22.4 %collective-permute-start.15 = (bf16[16,128,128]{2,1,0:T(8,128)(2,1)S(1)}, bf16[16,128,128]{2,1,0:T(8,128)(2,1)S(1)}, u32[]{:S(2)}, u32[]{:S(2)}) collective-permute-start(bf16[16,128,128]{2,1,0:T(8,128)(2,1)S(1)} %copy-done.3), channel_id=1, source_target_pairs={{0,8},{24,16},{1,9},{25,17},{2,10},{26,18},{3,11},{27,19},{4,12},{... | collective-permute-start | bytes 1572872 | tf_op jit(solution)/shard_map/ppermute | solution.py:582
  108.5 13.4 %collective-permute-start.22 = (bf16[16,128,128]{2,1,0:T(8,128)(2,1)S(1)}, bf16[16,128,128]{2,1,0:T(8,128)(2,1)S(1)}, u32[]{:S(2)}, u32[]{:S(2)}) collective-permute-start(bf16[16,128,128]{2,1,0:T(8,128)(2,1)S(1)} %merge.9.after_ref.mine_ref), channel_id=1, source_target_pairs={{8,16},{16,8},{9,17},{17,9},{10,18},{18,10},{11,19},{19,11},{12,20... | collective-permute-start | bytes 1572872 | tf_op jit(solution)/shard_map/ppermute | solution.py:602
  109.4 20.6 %collective-permute-start.21 = (bf16[16,128,128]{2,1,0:T(8,128)(2,1)S(1)}, bf16[16,128,128]{2,1,0:T(8,128)(2,1)}, u32[]{:S(2)}, u32[]{:S(2)}) collective-permute-start(bf16[16,128,128]{2,1,0:T(8,128)(2,1)S(1)} %merge.10.after_ref.mine_ref), channel_id=1, source_target_pairs={{8,0},{16,24},{9,1},{17,25},{10,2},{18,26},{11,3},{19,27},{12,4},{... | collective-permute-start | bytes 1572872 | tf_op jit(solution)/shard_map/ppermute | solution.py:602
  110.7 21.1 %collective-permute-start.20 = (bf16[16,128,128]{2,1,0:T(8,128)(2,1)S(1)}, bf16[16,128,128]{2,1,0:T(8,128)(2,1)S(1)}, u32[]{:S(2)}, u32[]{:S(2)}) collective-permute-start(bf16[16,128,128]{2,1,0:T(8,128)(2,1)S(1)} %copy-done), channel_id=1, source_target_pairs={{0,8},{24,16},{1,9},{25,17},{2,10},{26,18},{3,11},{27,19},{4,12},{... | collective-permute-start | bytes 1572872 | tf_op jit(solution)/shard_map/ppermute | solution.py:582
  121.3 11.5 %collective-permute-start.19 = (bf16[16,128,128]{2,1,0:T(8,128)(2,1)S(1)}, bf16[16,128,128]{2,1,0:T(8,128)(2,1)S(1)}, u32[]{:S(2)}, u32[]{:S(2)}) collective-permute-start(bf16[16,128,128]{2,1,0:T(8,128)(2,1)S(1)} %merge.11.after_ref.mine_ref), channel_id=1, source_target_pairs={{8,16},{16,8},{9,17},{17,9},{10,18},{18,10},{11,19},{19,11},{12,20... | collective-permute-start | bytes 1572872 | tf_op jit(solution)/shard_map/ppermute | solution.py:602
  122.1 19.1 %collective-permute-start.25 = (bf16[16,128,128]{2,1,0:T(8,128)(2,1)S(1)}, bf16[16,128,128]{2,1,0:T(8,128)(2,1)}, u32[]{:S(2)}, u32[]{:S(2)}) collective-permute-start(bf16[16,128,128]{2,1,0:T(8,128)(2,1)S(1)} %merge.12.after_ref.token_ref.mine_ref), channel_id=1, source_target_pairs={{8,0},{16,24},{9,1},{17,25},{10,2},{18,26},{11,3},{19,27},{12,4},{... | collective-permute-start | bytes 1572872 | tf_op jit(solution)/shard_map/ppermute | solution.py:602
  131.1 15.8 %collective-permute-start.26 = (bf16[16,128,128]{2,1,0:T(8,128)(2,1)S(1)}, bf16[16,128,128]{2,1,0:T(8,128)(2,1)S(1)}, u32[]{:S(2)}, u32[]{:S(2)}) collective-permute-start(bf16[16,128,128]{2,1,0:T(8,128)(2,1)S(1)} %pick.4.after_ref), channel_id=1, source_target_pairs={{0,6},{1,7},{2,4},{3,5},{4,2},{5,3},{6,0},{7,1},{8,14},{9,15},{10,... | collective-permute-start | bytes 1572872 | tf_op jit(solution)/shard_map/ppermute | solution.py:606
  131.9 23.2 %copy-start.1 = (bf16[128,256]{1,0:T(8,128)(2,1)S(1)}, bf16[128,256]{1,0:T(8,128)(2,1)}, u32[]{:S(2)}) copy-start(bf16[128,256]{1,0:T(8,128)(2,1)} %constant.19.clone.refs_2_) | copy-start | bytes 196612
  132.0 23.2 %copy-start.5 = (s32[1,64]{1,0:T(1,128)S(1)}, s32[1,64]{1,0:T(1,128)}, u32[]{:S(2)}) copy-start(s32[1,64]{1,0:T(1,128)} %refs_1_.7) | copy-start | bytes 772
  132.0 15.1 %collective-permute-start.24 = (bf16[16,128,128]{2,1,0:T(8,128)(2,1)S(1)}, bf16[16,128,128]{2,1,0:T(8,128)(2,1)S(1)}, u32[]{:S(2)}, u32[]{:S(2)}) collective-permute-start(bf16[16,128,128]{2,1,0:T(8,128)(2,1)S(1)} %merge.13.after_ref.mine_ref), channel_id=1, source_target_pairs={{8,16},{16,8},{9,17},{17,9},{10,18},{18,10},{11,19},{19,11},{12,20... | collective-permute-start | bytes 1572872 | tf_op jit(solution)/shard_map/ppermute | solution.py:602
  142.4 12.7 %collective-permute-start.30 = (bf16[16,128,128]{2,1,0:T(8,128)(2,1)S(1)}, bf16[16,128,128]{2,1,0:T(8,128)(2,1)S(1)}, u32[]{:S(2)}, u32[]{:S(2)}) collective-permute-start(bf16[16,128,128]{2,1,0:T(8,128)(2,1)S(1)} %pick.5.after_ref), channel_id=1, source_target_pairs={{0,2},{1,3},{2,0},{3,1},{4,6},{5,7},{6,4},{7,5},{8,10},{9,11},{10,... | collective-permute-start | bytes 1572872 | tf_op jit(solution)/shard_map/ppermute | solution.py:606
  142.4 16.8 %collective-permute-start.23 = (bf16[16,128,128]{2,1,0:T(8,128)(2,1)S(1)}, bf16[16,128,128]{2,1,0:T(8,128)(2,1)S(1)}, u32[]{:S(2)}, u32[]{:S(2)}) collective-permute-start(bf16[16,128,128]{2,1,0:T(8,128)(2,1)S(1)} %merge.14.after_ref.token_ref.mine_ref), channel_id=1, source_target_pairs={{8,0},{16,24},{9,1},{17,25},{10,2},{18,26},{11,3},{19,27},{12,4},{... | collective-permute-start | bytes 1572872 | tf_op jit(solution)/shard_map/ppermute | solution.py:602
  147.0 8.2 %collective-permute-start.27 = (bf16[8,128,128]{2,1,0:T(8,128)(2,1)S(1)}, bf16[8,128,128]{2,1,0:T(8,128)(2,1)S(1)}, u32[]{:S(2)}, u32[]{:S(2)}) collective-permute-start(bf16[8,128,128]{2,1,0:T(8,128)(2,1)S(1)} %slice.47), channel_id=1, source_target_pairs={{0,1},{1,0},{2,3},{3,2},{4,5},{5,4},{6,7},{7,6},{8,9},{9,8},{10,11... | collective-permute-start | bytes 786440 | tf_op jit(solution)/shard_map/ppermute | solution.py:606
  147.2 21.0 %collective-permute-start.29 = (bf16[16,128,128]{2,1,0:T(8,128)(2,1)S(1)}, bf16[16,128,128]{2,1,0:T(8,128)(2,1)S(1)}, u32[]{:S(2)}, u32[]{:S(2)}) collective-permute-start(bf16[16,128,128]{2,1,0:T(8,128)(2,1)S(1)} %merge.15.after_ref.mine_ref), channel_id=1, source_target_pairs={{8,0},{16,24},{9,1},{17,25},{10,2},{18,26},{11,3},{19,27},{12,4},{... | collective-permute-start | bytes 1572872 | tf_op jit(solution)/shard_map/ppermute | solution.py:602
  155.0 5.1 %collective-permute-start.31 = (bf16[8,128,128]{2,1,0:T(8,128)(2,1)S(1)}, bf16[8,128,128]{2,1,0:T(8,128)(2,1)S(1)}, u32[]{:S(2)}, u32[]{:S(2)}) collective-permute-start(bf16[8,128,128]{2,1,0:T(8,128)(2,1)S(1)} %slice.48), channel_id=1, source_target_pairs={{0,1},{1,0},{2,3},{3,2},{4,5},{5,4},{6,7},{7,6},{8,9},{9,8},{10,11... | collective-permute-start | bytes 786440 | tf_op jit(solution)/shard_map/ppermute | solution.py:606
  159.3 13.9 %collective-permute-start.28 = (bf16[16,128,128]{2,1,0:T(8,128)(2,1)S(1)}, bf16[16,128,128]{2,1,0:T(8,128)(2,1)S(1)}, u32[]{:S(2)}, u32[]{:S(2)}) collective-permute-start(bf16[16,128,128]{2,1,0:T(8,128)(2,1)S(1)} %pick.6.after_ref), channel_id=1, source_target_pairs={{0,4},{1,5},{2,6},{3,7},{4,0},{5,1},{6,2},{7,3},{8,12},{9,13},{10,... | collective-permute-start | bytes 1572872 | tf_op jit(solution)/shard_map/ppermute | solution.py:606
  163.5 9.9 %copy-start.12 = (bf16[32,128,128]{2,1,0:T(8,128)(2,1)S(1)}, bf16[32,128,128]{2,1,0:T(8,128)(2,1)}, u32[]{:S(2)}) copy-start(bf16[32,128,128]{2,1,0:T(8,128)(2,1)} %get-tuple-element.32) | copy-start | bytes 3145732
  168.3 1.6 collective-permute-start.32
  173.2 1.7 collective-permute-start.33

commit v4 on v3

--- a/solution.py
+++ b/solution.py
@@ -247,7 +247,7 @@
 
 
 def adjoint_body(me_ref, rows_ref, cols_ref, count_ref, sens_ref, even_in_ref, odd_in_ref,
-                 *refs):
+                 after_ref, *refs):
     out_refs, image_ref = refs[:-9], refs[-9]
     block_ref, held_ref, acc_ref, half_ref, sems, got, put, whole = refs[-8:]
     peers = put.shape[0]
@@ -279,7 +279,7 @@
     wait_all(stores)
 
 
-def adjoint(me, rows, cols, count, sens, even, odd, blocks, peers):
+def adjoint(me, rows, cols, count, sens, even, odd, after, blocks, peers):
     slots = sens.shape[0]
     width = even.shape[2]
     piece = (blocks // peers, BLK, width)
@@ -288,7 +288,7 @@
         adjoint_body,
         out_shape=[jax.ShapeDtypeStruct((2 * piece[0], *piece[1:]), jnp.bfloat16)] * (peers // 2)
         + [jax.ShapeDtypeStruct(image, jnp.bfloat16)],
-        in_specs=[SMEM_SPEC] * 4 + [ANY_SPEC] * 3,
+        in_specs=[SMEM_SPEC] * 4 + [ANY_SPEC] * 4,
         out_specs=[ANY_SPEC] * (peers // 2 + 1),
         scratch_shapes=[
             pltpu.VMEM(sens.shape, sens.dtype),
@@ -306,7 +306,7 @@
             transcendentals=0,
         ),
         name="adjoint",
-    )(me, rows, cols, count, sens, even, odd)
+    )(me, rows, cols, count, sens, even, odd, after)
     return outs[:-1], outs[-1]
 
 
@@ -384,9 +384,8 @@
 
 
 def edges_body(me_ref, offset_ref, model_ref, near_ref, weight_ref, base_ref, after_ref, *refs):
-    odd_refs, refs = refs[:-7], refs[-7:]
-    out_ref, token_ref, window_ref, value_ref, ends_ref, got, put = refs
-    token_ref[...] = jnp.zeros_like(token_ref)
+    odd_refs, refs = refs[:-6], refs[-6:]
+    out_ref, window_ref, value_ref, ends_ref, got, put = refs
     cells = model_ref.shape[0]
     each = odd_refs[-1].shape[0] - 1
     inner = 2 * BLK - RIM
@@ -431,13 +430,10 @@
     count = len(odd_pieces)
     return pl.pallas_call(
         edges_body,
-        out_shape=[
-            jax.ShapeDtypeStruct(base.shape, base.dtype),
-            jax.ShapeDtypeStruct((8, BLK), jnp.float32),
-        ],
+        out_shape=jax.ShapeDtypeStruct(base.shape, base.dtype),
         in_specs=[SMEM_SPEC, SMEM_SPEC, ANY_SPEC, VMEM_SPEC, VMEM_SPEC]
         + [ANY_SPEC] * (2 + count),
-        out_specs=[ANY_SPEC, VMEM_SPEC],
+        out_specs=ANY_SPEC,
         input_output_aliases={5: 0},
         scratch_shapes=[
             pltpu.VMEM((2, 2 * BLK, width), jnp.float32),
@@ -567,7 +563,7 @@
     )(whole, after)
 
 
-def line_sums(parts, axis, after, deliver):
+def line_sums(parts, axis, deliver):
     count = lax.axis_size(axis)
     half = count // 2
     me = lax.axis_index(axis)
@@ -580,6 +576,7 @@
         stages.append(([(left, left - 1), (right, right + 1)], True))
     state = list(parts)
     got = [lax.ppermute(part, axis, stages[0][0]) for part in parts]
+    after = parts[0]
     for time in range(len(parts) + len(stages) - 1):
         for s, (pairs, outwards) in enumerate(stages):
             k = time - s
@@ -640,14 +637,14 @@
         [image_share] + [swap(image_share, "cols", 2 * j) for j in far], axis=0
     )
     odd_image = swap(even_image, "cols", 1)
+    smooth = edges(
+        me, offset, model_dir, neighbors, face_weight, smooth, to_send, [partner, *[passed[j] for j in range(1, half)]]
+    )
+
     partial_cols, image = adjoint(
-        me, blk_row, blk_col, blk_count, sens, even_image, odd_image, blocks, peers
+        me, blk_row, blk_col, blk_count, sens, even_image, odd_image, smooth, blocks, peers
     )
     data_image = image.reshape(RB_DEV * BLK, width).astype(jnp.float32)
-    smooth, first = edges(
-        me, offset, model_dir, neighbors, face_weight, smooth, partial_cols[0],
-        [partner, *[passed[j] for j in range(1, half)]],
-    )
     normal = smooth.reshape(blocks, BLK, width)
     order = [*far, 0]
     waiting, tokens = [], []
@@ -675,7 +672,7 @@
         waiting.append((even, other, j))
         return total
 
-    line_sums([partial_cols[j] for j in order], "rows", first, deliver)
+    line_sums([partial_cols[j] for j in order], "rows", deliver)
     while waiting:
         end_one(-1)
     return (data_image, normal.reshape(cell_count, width))

time: 179 us -> 184 us (1.028)
  the two profiles are of different devices: /device:TPU:0 before, /device:TPU:9 now
where the time goes in v4:
time: 184 us; the launch traced here: 182 us
  waiting for transfers between devices  61 us (33%)
  Pallas kernels  56.1 us (30%)
  starting transfers between devices  56.1 us (30%)
  local copies, waits for them, and re-layouts  3.76 us (2%)
  other arithmetic  3.06 us (2%)
  between operations  1.95 us (1%)
    ppermute x22, waiting for transfers between devices, swap(): lax.ppermute(piece, axis, [(c, c ^ offset) for c in range(lax.axis_size(a...  34.1 us
    ppermute x22, starting transfers between devices, swap(): lax.ppermute(piece, axis, [(c, c ^ offset) for c in range(lax.axis_size(a...  29.6 us
    ppermute x4, waiting for transfers between devices, line_sums(): got = [lax.ppermute(part, axis, stages[0][0]) for part in parts]  24.6 us
    ppermute x8, starting transfers between devices, line_sums(): got[k] = lax.ppermute(state[k], axis, stages[s + 1][0])  21.3 us
    pallas_call x4, Pallas kernels, finish(): pl.pallas_call(lambda *refs: finish_body(*refs, offset=offset), out_shape...  13.9 us
    pallas_call x1, Pallas kernels, smoothing(): pl.pallas_call(smooth_body, out_shape=jax.ShapeDtypeStruct((cells, width)...  13.3 us
    pallas_call x1, Pallas kernels, adjoint(): pl.pallas_call(adjoint_body, out_shape=[jax.ShapeDtypeStruct((2 * piece[0...  8.76 us
    pallas_call x1, Pallas kernels, forward(): pl.pallas_call(forward_body, out_shape=[jax.ShapeDtypeStruct(half, jnp.fl...  8.45 us
  transfers between devices with their start and end apart: 34, of which 19 were waited for; matrix products, arithmetic and copies ran while one was open for 1% of the time, Pallas kernels for 16%

profile of v4, /device:TPU:9, one launch (start us, length us, event | category | flops | bytes accessed | tf_op | source)
XLA Modules:
  0.0 182.0 jit_solution(629195323382431811)
XLA Ops:
  0.6 5.0 %analyze.1 = (bf16[8,128,128]{2,1,0:T(8,128)(2,1)}, bf16[8,128,128]{2,1,0:T(8,128)(2,1)}, bf16[8,128,128]{2,1,0:T(8,128)(2,1)}, bf16[8,128,128]{2,1,0:T(8,128)(2,1)}, bf16[36,128,128]{2,1,0:T(8,128)(2,1)}) custom-call(s32[1]{0:T(128)} %bitcast.me_ref.refs_0_, s32[1,64]{1,0:T(1,128)} %refs_1_.7, f32[64,128,128]{2,1,0:T(8,128)} %bitcast.15), custom_call_target="tpu_custom_call" | custom-call | flops 536870912 | bytes 6291456 | tf_op jit(solution)/shard_map/analyze/pallas_call | solution.py:145
  5.6 0.7 collective-permute-start
  6.4 2.2 %collective-permute-start.1 = (bf16[8,128,128]{2,1,0:T(8,128)(2,1)}, bf16[8,128,128]{2,1,0:T(8,128)(2,1)S(1)}, u32[]{:S(2)}, u32[]{:S(2)}) collective-permute-start(bf16[8,128,128]{2,1,0:T(8,128)(2,1)} %get-tuple-element.25), channel_id=1, source_target_pairs={{0,6},{1,7},{2,4},{3,5},{4,2},{5,3},{6,0},{7,1},{8,14},{9,15},{10,... | collective-permute-start | bytes 786440 | tf_op jit(solution)/shard_map/ppermute | solution.py:603
  8.5 0.2 collective-permute-start.2
  8.8 0.2 collective-permute-start.3
  9.8 2.2 %collective-permute-start.4 = (bf16[9,128,128]{2,1,0:T(8,128)(2,1)S(1)}, bf16[9,128,128]{2,1,0:T(8,128)(2,1)S(1)}, u32[]{:S(2)}, u32[]{:S(2)}) collective-permute-start(bf16[9,128,128]{2,1,0:T(8,128)(2,1)S(1)} %get-tuple-element.48), channel_id=1, source_target_pairs={{0,6},{1,7},{2,4},{3,5},{4,2},{5,3},{6,0},{7,1},{8,14},{9,15},{10,... | collective-permute-start | bytes 884744 | tf_op jit(solution)/shard_map/ppermute | solution.py:603
  12.0 0.2 collective-permute-start.5
  12.3 3.1 %collective-permute-done.1.refs_2_ = bf16[8,128,128]{2,1,0:T(8,128)(2,1)S(1)} collective-permute-done((bf16[8,128,128]{2,1,0:T(8,128)(2,1)}, bf16[8,128,128]{2,1,0:T(8,128)(2,1)S(1)}, u32[]{:S(2)}, u32[]{:S(2)}) %collective-permute-start.1) | collective-permute-done | bytes 262176 | tf_op jit(solution)/shard_map/ppermute | solution.py:603
  15.4 1.2 collective-permute-start.6
  16.6 13.3 %smoothing.1.refs_8_.base_ref = f32[8192,128]{1,0:T(8,128)} custom-call(s32[1]{0:T(128)} %bitcast.3.offset_ref, f32[8192,128]{1,0:T(8,128)} %model_ref.3, s32[4,8192]{1,0:T(4,128)} %near_ref.3, f32[4,8192]{1,0:T(4,128)} %weight_ref.3, bf16[36,128,128]{2,1,0:T(8,128)(2,1)} %copy-done.6), custom_call_target="tpu_custom_call" | custom-call | flops 3221225472 | bytes 16777216 | tf_op jit(solution)/shard_map/smoothing/pallas_call | solution.py:367
  30.0 3.7 %collective-permute-done.5.refs_6_.refs_1_ = bf16[9,128,128]{2,1,0:T(8,128)(2,1)S(1)} collective-permute-done((bf16[9,128,128]{2,1,0:T(8,128)(2,1)S(1)}, bf16[9,128,128]{2,1,0:T(8,128)(2,1)S(1)}, u32[]{:S(2)}, u32[]{:S(2)}) %collective-permute-start.5) | collective-permute-done | bytes 294944 | tf_op jit(solution)/shard_map/ppermute | solution.py:603
  34.0 0.5 copy-done.10
  34.7 8.5 %forward.1 = (f32[16,128,128]{2,1,0:T(8,128)}, f32[16,128,128]{2,1,0:T(8,128)}) custom-call(s32[1]{0:T(128)} %bitcast.me_ref.refs_0_, s32[1,384]{1,0:T(1,128)} %rows_ref.3, s32[1,384]{1,0:T(1,128)} %cols_ref.3, s32[1,1]{1,0:T(1,128)S(6)} %copy.24.count_ref, bf16[384,128,128]{2,1,0:T(8,128)(2,1)} %bitcast.13, bf16[8,128,128]{2,1,0:T(8,128)(2,1)} %get-tuple-element.23.refs_0_, ...), custom_call_target="tpu_custom_call" | custom-call | flops 1610612736 | bytes 12582912 | tf_op jit(solution)/shard_map/forward/pallas_call | solution.py:227
  43.2 2.9 %collective-permute-done.7 = f32[16,128,128]{2,1,0:T(8,128)S(1)} collective-permute-done((f32[16,128,128]{2,1,0:T(8,128)}, f32[16,128,128]{2,1,0:T(8,128)S(1)}, u32[]{:S(2)}, u32[]{:S(2)}) %collective-permute-start.7) | collective-permute-done | bytes 1048608 | tf_op jit(solution)/shard_map/ppermute | solution.py:603
  46.1 1.4 fusion.1
  47.5 1.7 collective-permute-start.10
  49.3 1.0 collective-permute-start.8
  50.5 3.7 %collective-permute-done.10 = bf16[4,128,128]{2,1,0:T(8,128)(2,1)S(1)} collective-permute-done((bf16[4,128,128]{2,1,0:T(8,128)(2,1)S(1)}, bf16[4,128,128]{2,1,0:T(8,128)(2,1)S(1)}, u32[]{:S(2)}, u32[]{:S(2)}) %collective-permute-start.10) | collective-permute-done | bytes 131104 | tf_op jit(solution)/shard_map/ppermute | solution.py:603
  54.3 0.4 collective-permute-done.8
  54.6 2.0 %collective-permute-done.9 = bf16[4,128,128]{2,1,0:T(8,128)(2,1)S(1)} collective-permute-done((bf16[4,128,128]{2,1,0:T(8,128)(2,1)S(1)}, bf16[4,128,128]{2,1,0:T(8,128)(2,1)S(1)}, u32[]{:S(2)}, u32[]{:S(2)}) %collective-permute-start.9) | collective-permute-done | bytes 131104 | tf_op jit(solution)/shard_map/ppermute | solution.py:603
  56.7 2.1 %collective-permute-start.11 = (bf16[4,128,128]{2,1,0:T(8,128)(2,1)S(1)}, bf16[4,128,128]{2,1,0:T(8,128)(2,1)S(1)}, u32[]{:S(2)}, u32[]{:S(2)}) collective-permute-start(bf16[4,128,128]{2,1,0:T(8,128)(2,1)S(1)} %fusion), channel_id=1, source_target_pairs={{0,6},{1,7},{2,4},{3,5},{4,2},{5,3},{6,0},{7,1},{8,14},{9,15},{10,... | collective-permute-start | bytes 393224 | tf_op jit(solution)/shard_map/ppermute | solution.py:603
  59.1 0.4 collective-permute-start.13
  59.4 2.1 %collective-permute-done.11 = bf16[4,128,128]{2,1,0:T(8,128)(2,1)S(1)} collective-permute-done((bf16[4,128,128]{2,1,0:T(8,128)(2,1)S(1)}, bf16[4,128,128]{2,1,0:T(8,128)(2,1)S(1)}, u32[]{:S(2)}, u32[]{:S(2)}) %collective-permute-start.11) | collective-permute-done | bytes 131104 | tf_op jit(solution)/shard_map/ppermute | solution.py:603
  61.5 2.4 %collective-permute-done.12 = bf16[4,128,128]{2,1,0:T(8,128)(2,1)S(1)} collective-permute-done((bf16[4,128,128]{2,1,0:T(8,128)(2,1)S(1)}, bf16[4,128,128]{2,1,0:T(8,128)(2,1)S(1)}, u32[]{:S(2)}, u32[]{:S(2)}) %collective-permute-start.12) | collective-permute-done | bytes 131104 | tf_op jit(solution)/shard_map/ppermute | solution.py:603
  63.9 0.3 collective-permute-done.13
  64.3 2.2 %collective-permute-start.14 = (bf16[16,128,128]{2,1,0:T(8,128)(2,1)S(1)}, bf16[16,128,128]{2,1,0:T(8,128)(2,1)S(1)}, u32[]{:S(2)}, u32[]{:S(2)}) collective-permute-start(bf16[16,128,128]{2,1,0:T(8,128)(2,1)S(1)} %pad_maximum_fusion.even_in_ref), channel_id=1, source_target_pairs={{0,1},{1,0},{2,3},{3,2},{4,5},{5,4},{6,7},{7,6},{8,9},{9,8},{10,11... | collective-permute-start | bytes 1572872 | tf_op jit(solution)/shard_map/ppermute | solution.py:603
  66.5 3.1 %edges.1.after_ref = f32[8192,128]{1,0:T(8,128)} custom-call(s32[1]{0:T(128)} %bitcast.me_ref.refs_0_, s32[1]{0:T(128)} %bitcast.3.offset_ref, f32[8192,128]{1,0:T(8,128)} %model_ref.3, s32[4,8192]{1,0:T(4,128)} %near_ref.3, f32[4,8192]{1,0:T(4,128)} %weight_ref.3, f32[8192,128]{1,0:T(8,128)} %smoothing.1.refs_8_.base_ref, ...), custom_call_target="tpu_custom_call", output_to_operand_aliasing={{}: (5, {})} | custom-call | flops 100663296 | bytes 524288 | tf_op jit(solution)/shard_map/edges/pallas_call | solution.py:431
  69.6 0.8 copy-done.13
  70.4 8.8 %adjoint.1 = (bf16[16,128,128]{2,1,0:T(8,128)(2,1)}, bf16[16,128,128]{2,1,0:T(8,128)(2,1)}, bf16[16,128,128]{2,1,0:T(8,128)(2,1)}, bf16[16,128,128]{2,1,0:T(8,128)(2,1)}, bf16[32,128,128]{2,1,0:T(8,128)(2,1)}) custom-call(s32[1]{0:T(128)} %bitcast.me_ref.refs_0_, s32[1,384]{1,0:T(1,128)} %rows_ref.3, s32[1,384]{1,0:T(1,128)} %cols_ref.3, ...), custom_call_target="tpu_custom_call" | custom-call | flops 1610612736 | bytes 12582912 | tf_op jit(solution)/shard_map/adjoint/pallas_call | solution.py:287
  79.2 1.3 collective-permute-start.16
  80.5 1.3 collective-permute-start.18
  81.8 13.7 %collective-permute-done.16.got_ref = bf16[16,128,128]{2,1,0:T(8,128)(2,1)S(1)} collective-permute-done((bf16[16,128,128]{2,1,0:T(8,128)(2,1)}, bf16[16,128,128]{2,1,0:T(8,128)(2,1)S(1)}, u32[]{:S(2)}, u32[]{:S(2)}) %collective-permute-start.16) | collective-permute-done | bytes 524320 | tf_op jit(solution)/shard_map/ppermute | solution.py:578
  95.5 1.0 copy-done
  96.7 2.1 %collective-permute-start.17 = (bf16[16,128,128]{2,1,0:T(8,128)(2,1)S(1)}, bf16[16,128,128]{2,1,0:T(8,128)(2,1)S(1)}, u32[]{:S(2)}, u32[]{:S(2)}) collective-permute-start(bf16[16,128,128]{2,1,0:T(8,128)(2,1)S(1)} %merge.8.after_ref.mine_ref), channel_id=1, source_target_pairs={{8,16},{16,8},{9,17},{17,9},{10,18},{18,10},{11,19},{19,11},{12,20... | collective-permute-start | bytes 1572872 | tf_op jit(solution)/shard_map/ppermute | solution.py:599
  98.8 1.3 collective-permute-start.15
  100.1 6.7 %collective-permute-done.18.got_ref = bf16[16,128,128]{2,1,0:T(8,128)(2,1)S(1)} collective-permute-done((bf16[16,128,128]{2,1,0:T(8,128)(2,1)}, bf16[16,128,128]{2,1,0:T(8,128)(2,1)S(1)}, u32[]{:S(2)}, u32[]{:S(2)}) %collective-permute-start.18) | collective-permute-done | bytes 524320 | tf_op jit(solution)/shard_map/ppermute | solution.py:578
  106.8 1.0 copy-done.4
  107.9 1.9 %collective-permute-start.22 = (bf16[16,128,128]{2,1,0:T(8,128)(2,1)S(1)}, bf16[16,128,128]{2,1,0:T(8,128)(2,1)S(1)}, u32[]{:S(2)}, u32[]{:S(2)}) collective-permute-start(bf16[16,128,128]{2,1,0:T(8,128)(2,1)S(1)} %merge.9.after_ref.mine_ref), channel_id=1, source_target_pairs={{8,16},{16,8},{9,17},{17,9},{10,18},{18,10},{11,19},{19,11},{12,20... | collective-permute-start | bytes 1572872 | tf_op jit(solution)/shard_map/ppermute | solution.py:599
  110.0 2.1 %collective-permute-start.21 = (bf16[16,128,128]{2,1,0:T(8,128)(2,1)S(1)}, bf16[16,128,128]{2,1,0:T(8,128)(2,1)}, u32[]{:S(2)}, u32[]{:S(2)}) collective-permute-start(bf16[16,128,128]{2,1,0:T(8,128)(2,1)S(1)} %merge.10.after_ref.mine_ref), channel_id=1, source_target_pairs={{8,0},{16,24},{9,1},{17,25},{10,2},{18,26},{11,3},{19,27},{12,4},{... | collective-permute-start | bytes 1572872 | tf_op jit(solution)/shard_map/ppermute | solution.py:599
  112.1 1.3 collective-permute-start.20
  113.4 2.4 %collective-permute-done.15.got_ref = bf16[16,128,128]{2,1,0:T(8,128)(2,1)S(1)} collective-permute-done((bf16[16,128,128]{2,1,0:T(8,128)(2,1)}, bf16[16,128,128]{2,1,0:T(8,128)(2,1)S(1)}, u32[]{:S(2)}, u32[]{:S(2)}) %collective-permute-start.15) | collective-permute-done | bytes 524320 | tf_op jit(solution)/shard_map/ppermute | solution.py:578
  115.9 4.0 %collective-permute-start.19 = (bf16[16,128,128]{2,1,0:T(8,128)(2,1)S(1)}, bf16[16,128,128]{2,1,0:T(8,128)(2,1)S(1)}, u32[]{:S(2)}, u32[]{:S(2)}) collective-permute-start(bf16[16,128,128]{2,1,0:T(8,128)(2,1)S(1)} %merge.11.after_ref.mine_ref), channel_id=1, source_target_pairs={{8,16},{16,8},{9,17},{17,9},{10,18},{18,10},{11,19},{19,11},{12,20... | collective-permute-start | bytes 1572872 | tf_op jit(solution)/shard_map/ppermute | solution.py:599
  120.1 2.1 %collective-permute-start.25 = (bf16[16,128,128]{2,1,0:T(8,128)(2,1)S(1)}, bf16[16,128,128]{2,1,0:T(8,128)(2,1)}, u32[]{:S(2)}, u32[]{:S(2)}) collective-permute-start(bf16[16,128,128]{2,1,0:T(8,128)(2,1)S(1)} %merge.12.after_ref.token_ref.mine_ref), channel_id=1, source_target_pairs={{8,0},{16,24},{9,1},{17,25},{10,2},{18,26},{11,3},{19,27},{12,4},{... | collective-permute-start | bytes 1572872 | tf_op jit(solution)/shard_map/ppermute | solution.py:599
  122.2 1.2 pick.4.after_ref
  123.4 1.8 collective-permute-done.20.got_ref
  125.3 6.3 %collective-permute-start.24 = (bf16[16,128,128]{2,1,0:T(8,128)(2,1)S(1)}, bf16[16,128,128]{2,1,0:T(8,128)(2,1)S(1)}, u32[]{:S(2)}, u32[]{:S(2)}) collective-permute-start(bf16[16,128,128]{2,1,0:T(8,128)(2,1)S(1)} %merge.13.after_ref.mine_ref), channel_id=1, source_target_pairs={{8,16},{16,8},{9,17},{17,9},{10,18},{18,10},{11,19},{19,11},{12,20... | collective-permute-start | bytes 1572872 | tf_op jit(solution)/shard_map/ppermute | solution.py:599
  131.7 0.3 collective-permute-done.19.got_ref
  132.2 1.2 pick.5.after_ref
  133.4 7.5 %collective-permute-start.30 = (bf16[16,128,128]{2,1,0:T(8,128)(2,1)S(1)}, bf16[16,128,128]{2,1,0:T(8,128)(2,1)S(1)}, u32[]{:S(2)}, u32[]{:S(2)}) collective-permute-start(bf16[16,128,128]{2,1,0:T(8,128)(2,1)S(1)} %pick.5.after_ref), channel_id=1, source_target_pairs={{0,2},{1,3},{2,0},{3,1},{4,6},{5,7},{6,4},{7,5},{8,10},{9,11},{10,... | collective-permute-start | bytes 1572872 | tf_op jit(solution)/shard_map/ppermute | solution.py:603
  140.9 1.3 collective-permute-start.23
  142.2 2.0 %collective-permute-done.24.got_ref = bf16[16,128,128]{2,1,0:T(8,128)(2,1)S(1)} collective-permute-done((bf16[16,128,128]{2,1,0:T(8,128)(2,1)S(1)}, bf16[16,128,128]{2,1,0:T(8,128)(2,1)S(1)}, u32[]{:S(2)}, u32[]{:S(2)}) %collective-permute-start.24) | collective-permute-done | bytes 524320 | tf_op jit(solution)/shard_map/ppermute | solution.py:599
  144.3 1.5 collective-permute-start.29
  145.9 4.8 %collective-permute-start.27 = (bf16[8,128,128]{2,1,0:T(8,128)(2,1)S(1)}, bf16[8,128,128]{2,1,0:T(8,128)(2,1)S(1)}, u32[]{:S(2)}, u32[]{:S(2)}) collective-permute-start(bf16[8,128,128]{2,1,0:T(8,128)(2,1)S(1)} %slice.47), channel_id=1, source_target_pairs={{0,1},{1,0},{2,3},{3,2},{4,5},{5,4},{6,7},{7,6},{8,9},{9,8},{10,11... | collective-permute-start | bytes 786440 | tf_op jit(solution)/shard_map/ppermute | solution.py:603
  150.7 7.6 %collective-permute-done.30.refs_3_ = bf16[16,128,128]{2,1,0:T(8,128)(2,1)S(1)} collective-permute-done((bf16[16,128,128]{2,1,0:T(8,128)(2,1)S(1)}, bf16[16,128,128]{2,1,0:T(8,128)(2,1)S(1)}, u32[]{:S(2)}, u32[]{:S(2)}) %collective-permute-start.30) | collective-permute-done | bytes 524320 | tf_op jit(solution)/shard_map/ppermute | solution.py:603
  158.4 3.3 %finish.4 = (f32[64,128,128]{2,1,0:T(8,128)}, f32[8,128]{1,0:T(8,128)S(1)}) custom-call(s32[1]{0:T(128)} %bitcast.me_ref.refs_0_, s32[1,64]{1,0:T(1,128)S(1)} %copy-done.5, bf16[128,256]{1,0:T(8,128)(2,1)S(1)} %copy-done.1, bf16[16,128,128]{2,1,0:T(8,128)(2,1)S(1)} %collective-permute-done.26.refs_3_, ...), custom_call_target="tpu_custom_call", output_to_operand_aliasing={{0}: (5, {})} | custom-call | flops 134217728 | bytes 2621440 | tf_op jit(solution)/shard_map/finish/pallas_call | solution.py:482
  161.9 0.3 collective-permute-start.28
  162.1 3.3 %finish.5 = (f32[64,128,128]{2,1,0:T(8,128)}, f32[8,128]{1,0:T(8,128)S(1)}) custom-call(s32[1]{0:T(128)} %bitcast.me_ref.refs_0_, s32[1,64]{1,0:T(1,128)S(1)} %copy-done.5, bf16[128,256]{1,0:T(8,128)(2,1)S(1)} %copy-done.1, bf16[16,128,128]{2,1,0:T(8,128)(2,1)S(1)} %collective-permute-done.30.refs_3_, ...), custom_call_target="tpu_custom_call", output_to_operand_aliasing={{0}: (5, {})} | custom-call | flops 134217728 | bytes 2621440 | tf_op jit(solution)/shard_map/finish/pallas_call | solution.py:482
  165.7 0.4 collective-permute-start.32
  166.0 1.2 collective-permute-done.32.refs_4_
  167.3 3.3 %finish.6 = (f32[64,128,128]{2,1,0:T(8,128)}, f32[8,128]{1,0:T(8,128)S(1)}) custom-call(s32[1]{0:T(128)} %bitcast.me_ref.refs_0_, s32[1,64]{1,0:T(1,128)S(1)} %copy-done.5, bf16[128,256]{1,0:T(8,128)(2,1)S(1)} %copy-done.1, bf16[8,128,128]{2,1,0:T(8,128)(2,1)S(1)} %get-tuple-element.38.refs_3_, ...), custom_call_target="tpu_custom_call", output_to_operand_aliasing={{0}: (5, {})} | custom-call | flops 134217728 | bytes 2621440 | tf_op jit(solution)/shard_map/finish/pallas_call | solution.py:482
  170.6 4.4 %collective-permute-done.28.whole_ref.refs_3_ = bf16[16,128,128]{2,1,0:T(8,128)(2,1)S(1)} collective-permute-done((bf16[16,128,128]{2,1,0:T(8,128)(2,1)S(1)}, bf16[16,128,128]{2,1,0:T(8,128)(2,1)S(1)}, u32[]{:S(2)}, u32[]{:S(2)}) %collective-permute-start.28) | collective-permute-done | bytes 524320 | tf_op jit(solution)/shard_map/ppermute | solution.py:603
  175.0 1.4 collective-permute-start.33
  176.4 1.5 bitcast_convert_fusion
  177.9 3.9 %finish.7 = (f32[64,128,128]{2,1,0:T(8,128)}, f32[8,128]{1,0:T(8,128)}) custom-call(s32[1]{0:T(128)} %bitcast.me_ref.refs_0_, s32[1,64]{1,0:T(1,128)S(1)} %copy-done.5, bf16[128,256]{1,0:T(8,128)(2,1)S(1)} %copy-done.1, bf16[16,128,128]{2,1,0:T(8,128)(2,1)S(1)} %collective-permute-done.28.whole_ref.refs_3_, ...), custom_call_target="tpu_custom_call", output_to_operand_aliasing={{0}: (5, {})} | custom-call | flops 134217728 | bytes 2621440 | tf_op jit(solution)/shard_map/finish/pallas_call | solution.py:482
  (68 shorter events, 2.7 us)
Async XLA Ops:
  5.6 4.1 %collective-permute-start = (bf16[36,128,128]{2,1,0:T(8,128)(2,1)}, bf16[36,128,128]{2,1,0:T(8,128)(2,1)S(1)}, u32[]{:S(2)}, u32[]{:S(2)}) collective-permute-start(bf16[36,128,128]{2,1,0:T(8,128)(2,1)} %get-tuple-element.24), channel_id=1, source_target_pairs={{0,1},{1,0},{2,3},{3,2},{4,5},{5,4},{6,7},{7,6},{8,9},{9,8},{10,11... | collective-permute-start | bytes 3538952 | tf_op jit(solution)/shard_map/ppermute | solution.py:603
  6.4 9.0 %collective-permute-start.1 = (bf16[8,128,128]{2,1,0:T(8,128)(2,1)}, bf16[8,128,128]{2,1,0:T(8,128)(2,1)S(1)}, u32[]{:S(2)}, u32[]{:S(2)}) collective-permute-start(bf16[8,128,128]{2,1,0:T(8,128)(2,1)} %get-tuple-element.25), channel_id=1, source_target_pairs={{0,6},{1,7},{2,4},{3,5},{4,2},{5,3},{6,0},{7,1},{8,14},{9,15},{10,... | collective-permute-start | bytes 786440 | tf_op jit(solution)/shard_map/ppermute | solution.py:603
  8.5 21.4 %collective-permute-start.2 = (bf16[8,128,128]{2,1,0:T(8,128)(2,1)}, bf16[8,128,128]{2,1,0:T(8,128)(2,1)S(1)}, u32[]{:S(2)}, u32[]{:S(2)}) collective-permute-start(bf16[8,128,128]{2,1,0:T(8,128)(2,1)} %get-tuple-element.26), channel_id=1, source_target_pairs={{0,2},{1,3},{2,0},{3,1},{4,6},{5,7},{6,4},{7,5},{8,10},{9,11},{10,... | collective-permute-start | bytes 786440 | tf_op jit(solution)/shard_map/ppermute | solution.py:603
  8.8 21.2 %collective-permute-start.3 = (bf16[8,128,128]{2,1,0:T(8,128)(2,1)}, bf16[8,128,128]{2,1,0:T(8,128)(2,1)S(1)}, u32[]{:S(2)}, u32[]{:S(2)}) collective-permute-start(bf16[8,128,128]{2,1,0:T(8,128)(2,1)} %get-tuple-element.27), channel_id=1, source_target_pairs={{0,4},{1,5},{2,6},{3,7},{4,0},{5,1},{6,2},{7,3},{8,12},{9,13},{10,... | collective-permute-start | bytes 786440 | tf_op jit(solution)/shard_map/ppermute | solution.py:603
  9.7 7.0 %copy-start.6 = (bf16[36,128,128]{2,1,0:T(8,128)(2,1)}, bf16[36,128,128]{2,1,0:T(8,128)(2,1)S(1)}, u32[]{:S(2)}) copy-start(bf16[36,128,128]{2,1,0:T(8,128)(2,1)S(1)} %collective-permute-done.after_ref.refs_1_.refs_0_) | copy-start | bytes 3538948
  9.8 20.2 %collective-permute-start.4 = (bf16[9,128,128]{2,1,0:T(8,128)(2,1)S(1)}, bf16[9,128,128]{2,1,0:T(8,128)(2,1)S(1)}, u32[]{:S(2)}, u32[]{:S(2)}) collective-permute-start(bf16[9,128,128]{2,1,0:T(8,128)(2,1)S(1)} %get-tuple-element.48), channel_id=1, source_target_pairs={{0,6},{1,7},{2,4},{3,5},{4,2},{5,3},{6,0},{7,1},{8,14},{9,15},{10,... | collective-permute-start | bytes 884744 | tf_op jit(solution)/shard_map/ppermute | solution.py:603
  12.0 21.8 %collective-permute-start.5 = (bf16[9,128,128]{2,1,0:T(8,128)(2,1)S(1)}, bf16[9,128,128]{2,1,0:T(8,128)(2,1)S(1)}, u32[]{:S(2)}, u32[]{:S(2)}) collective-permute-start(bf16[9,128,128]{2,1,0:T(8,128)(2,1)S(1)} %get-tuple-element.47), channel_id=1, source_target_pairs={{0,2},{1,3},{2,0},{3,1},{4,6},{5,7},{6,4},{7,5},{8,10},{9,11},{10,... | collective-permute-start | bytes 884744 | tf_op jit(solution)/shard_map/ppermute | solution.py:603
  15.4 14.6 %copy-start.14 = (bf16[8,128,128]{2,1,0:T(8,128)(2,1)}, bf16[8,128,128]{2,1,0:T(8,128)(2,1)S(1)}, u32[]{:S(2)}) copy-start(bf16[8,128,128]{2,1,0:T(8,128)(2,1)S(1)} %collective-permute-done.1.refs_2_) | copy-start | bytes 786436
  15.4 18.6 %collective-permute-start.6 = (bf16[9,128,128]{2,1,0:T(8,128)(2,1)S(1)}, bf16[9,128,128]{2,1,0:T(8,128)(2,1)S(1)}, u32[]{:S(2)}, u32[]{:S(2)}) collective-permute-start(bf16[9,128,128]{2,1,0:T(8,128)(2,1)S(1)} %get-tuple-element.46), channel_id=1, source_target_pairs={{0,4},{1,5},{2,6},{3,7},{4,0},{5,1},{6,2},{7,3},{8,12},{9,13},{10,... | collective-permute-start | bytes 884744 | tf_op jit(solution)/shard_map/ppermute | solution.py:603
  30.0 4.0 %copy-start.15 = (bf16[8,128,128]{2,1,0:T(8,128)(2,1)}, bf16[8,128,128]{2,1,0:T(8,128)(2,1)S(1)}, u32[]{:S(2)}) copy-start(bf16[8,128,128]{2,1,0:T(8,128)(2,1)S(1)} %collective-permute-done.2.refs_3_) | copy-start | bytes 786436
  30.0 4.0 %copy-start.16 = (bf16[8,128,128]{2,1,0:T(8,128)(2,1)}, bf16[8,128,128]{2,1,0:T(8,128)(2,1)S(1)}, u32[]{:S(2)}) copy-start(bf16[8,128,128]{2,1,0:T(8,128)(2,1)S(1)} %collective-permute-done.3.refs_4_) | copy-start | bytes 786436
  30.0 4.0 %copy-start.9 = (bf16[9,128,128]{2,1,0:T(8,128)(2,1)}, bf16[9,128,128]{2,1,0:T(8,128)(2,1)S(1)}, u32[]{:S(2)}) copy-start(bf16[9,128,128]{2,1,0:T(8,128)(2,1)S(1)} %collective-permute-done.4.refs_5_.refs_3_) | copy-start | bytes 884740
  33.8 0.7 copy-start.10
  34.0 0.7 copy-start.11
  43.1 2.9 %collective-permute-start.7 = (f32[16,128,128]{2,1,0:T(8,128)}, f32[16,128,128]{2,1,0:T(8,128)S(1)}, u32[]{:S(2)}, u32[]{:S(2)}) collective-permute-start(f32[16,128,128]{2,1,0:T(8,128)} %get-tuple-element.29), channel_id=1, source_target_pairs={{0,1},{1,0},{2,3},{3,2},{4,5},{5,4},{6,7},{7,6},{8,9},{9,8},{10,11... | collective-permute-start | bytes 3145736 | tf_op jit(solution)/shard_map/ppermute | solution.py:603
  47.5 19.1 %copy-start.7 = (bf16[16,128,128]{2,1,0:T(8,128)(2,1)}, bf16[16,128,128]{2,1,0:T(8,128)(2,1)S(1)}, u32[]{:S(2)}) copy-start(bf16[16,128,128]{2,1,0:T(8,128)(2,1)S(1)} %get-tuple-element.44) | copy-start | bytes 1572868
  47.5 6.7 %collective-permute-start.10 = (bf16[4,128,128]{2,1,0:T(8,128)(2,1)S(1)}, bf16[4,128,128]{2,1,0:T(8,128)(2,1)S(1)}, u32[]{:S(2)}, u32[]{:S(2)}) collective-permute-start(bf16[4,128,128]{2,1,0:T(8,128)(2,1)S(1)} %get-tuple-element.50), channel_id=1, source_target_pairs={{0,4},{1,5},{2,6},{3,7},{4,0},{5,1},{6,2},{7,3},{8,12},{9,13},{10,... | collective-permute-start | bytes 393224 | tf_op jit(solution)/shard_map/ppermute | solution.py:603
  49.3 5.4 %collective-permute-start.8 = (bf16[4,128,128]{2,1,0:T(8,128)(2,1)S(1)}, bf16[4,128,128]{2,1,0:T(8,128)(2,1)S(1)}, u32[]{:S(2)}, u32[]{:S(2)}) collective-permute-start(bf16[4,128,128]{2,1,0:T(8,128)(2,1)S(1)} %get-tuple-element.49), channel_id=1, source_target_pairs={{0,6},{1,7},{2,4},{3,5},{4,2},{5,3},{6,0},{7,1},{8,14},{9,15},{10,... | collective-permute-start | bytes 393224 | tf_op jit(solution)/shard_map/ppermute | solution.py:603
  50.3 6.3 %collective-permute-start.9 = (bf16[4,128,128]{2,1,0:T(8,128)(2,1)S(1)}, bf16[4,128,128]{2,1,0:T(8,128)(2,1)S(1)}, u32[]{:S(2)}, u32[]{:S(2)}) collective-permute-start(bf16[4,128,128]{2,1,0:T(8,128)(2,1)S(1)} %get-tuple-element.51), channel_id=1, source_target_pairs={{0,2},{1,3},{2,0},{3,1},{4,6},{5,7},{6,4},{7,5},{8,10},{9,11},{10,... | collective-permute-start | bytes 393224 | tf_op jit(solution)/shard_map/ppermute | solution.py:603
  56.7 4.8 %collective-permute-start.11 = (bf16[4,128,128]{2,1,0:T(8,128)(2,1)S(1)}, bf16[4,128,128]{2,1,0:T(8,128)(2,1)S(1)}, u32[]{:S(2)}, u32[]{:S(2)}) collective-permute-start(bf16[4,128,128]{2,1,0:T(8,128)(2,1)S(1)} %fusion), channel_id=1, source_target_pairs={{0,6},{1,7},{2,4},{3,5},{4,2},{5,3},{6,0},{7,1},{8,14},{9,15},{10,... | collective-permute-start | bytes 393224 | tf_op jit(solution)/shard_map/ppermute | solution.py:603
  58.8 5.1 %collective-permute-start.12 = (bf16[4,128,128]{2,1,0:T(8,128)(2,1)S(1)}, bf16[4,128,128]{2,1,0:T(8,128)(2,1)S(1)}, u32[]{:S(2)}, u32[]{:S(2)}) collective-permute-start(bf16[4,128,128]{2,1,0:T(8,128)(2,1)S(1)} %fusion), channel_id=1, source_target_pairs={{0,2},{1,3},{2,0},{3,1},{4,6},{5,7},{6,4},{7,5},{8,10},{9,11},{10,... | collective-permute-start | bytes 393224 | tf_op jit(solution)/shard_map/ppermute | solution.py:603
  59.1 5.2 %collective-permute-start.13 = (bf16[4,128,128]{2,1,0:T(8,128)(2,1)S(1)}, bf16[4,128,128]{2,1,0:T(8,128)(2,1)S(1)}, u32[]{:S(2)}, u32[]{:S(2)}) collective-permute-start(bf16[4,128,128]{2,1,0:T(8,128)(2,1)S(1)} %fusion), channel_id=1, source_target_pairs={{0,4},{1,5},{2,6},{3,7},{4,0},{5,1},{6,2},{7,3},{8,12},{9,13},{10,... | collective-permute-start | bytes 393224 | tf_op jit(solution)/shard_map/ppermute | solution.py:603
  64.3 5.3 %copy-start.8 = (bf16[16,128,128]{2,1,0:T(8,128)(2,1)}, bf16[16,128,128]{2,1,0:T(8,128)(2,1)S(1)}, u32[]{:S(2)}) copy-start(bf16[16,128,128]{2,1,0:T(8,128)(2,1)S(1)} %pad_maximum_fusion.even_in_ref) | copy-start | bytes 1572868
  64.3 5.3 %collective-permute-start.14 = (bf16[16,128,128]{2,1,0:T(8,128)(2,1)S(1)}, bf16[16,128,128]{2,1,0:T(8,128)(2,1)S(1)}, u32[]{:S(2)}, u32[]{:S(2)}) collective-permute-start(bf16[16,128,128]{2,1,0:T(8,128)(2,1)S(1)} %pad_maximum_fusion.even_in_ref), channel_id=1, source_target_pairs={{0,1},{1,0},{2,3},{3,2},{4,5},{5,4},{6,7},{7,6},{8,9},{9,8},{10,11... | collective-permute-start | bytes 1572872 | tf_op jit(solution)/shard_map/ppermute | solution.py:603
  69.6 0.8 copy-start.13
  79.2 16.3 %collective-permute-start.16 = (bf16[16,128,128]{2,1,0:T(8,128)(2,1)}, bf16[16,128,128]{2,1,0:T(8,128)(2,1)S(1)}, u32[]{:S(2)}, u32[]{:S(2)}) collective-permute-start(bf16[16,128,128]{2,1,0:T(8,128)(2,1)} %get-tuple-element.32.mine_ref.after_ref), channel_id=1, source_target_pairs={{0,8},{24,16},{1,9},{25,17},{2,10},{26,18},{3,11},{27,19},{4,12},{... | collective-permute-start | bytes 1572872 | tf_op jit(solution)/shard_map/ppermute | solution.py:578
  80.5 26.3 %collective-permute-start.18 = (bf16[16,128,128]{2,1,0:T(8,128)(2,1)}, bf16[16,128,128]{2,1,0:T(8,128)(2,1)S(1)}, u32[]{:S(2)}, u32[]{:S(2)}) collective-permute-start(bf16[16,128,128]{2,1,0:T(8,128)(2,1)} %get-tuple-element.33.mine_ref), channel_id=1, source_target_pairs={{0,8},{24,16},{1,9},{25,17},{2,10},{26,18},{3,11},{27,19},{4,12},{... | collective-permute-start | bytes 1572872 | tf_op jit(solution)/shard_map/ppermute | solution.py:578
  95.5 1.0 copy-start
  96.6 15.5 %copy-start.2 = (bf16[16,128,128]{2,1,0:T(8,128)(2,1)S(1)}, bf16[16,128,128]{2,1,0:T(8,128)(2,1)}, u32[]{:S(2)}) copy-start(bf16[16,128,128]{2,1,0:T(8,128)(2,1)} %get-tuple-element.34.mine_ref) | copy-start | bytes 1572868
  96.6 19.3 %copy-start.3 = (bf16[16,128,128]{2,1,0:T(8,128)(2,1)S(1)}, bf16[16,128,128]{2,1,0:T(8,128)(2,1)}, u32[]{:S(2)}) copy-start(bf16[16,128,128]{2,1,0:T(8,128)(2,1)} %get-tuple-element.31.mine_ref) | copy-start | bytes 1572868
  96.7 13.2 %collective-permute-start.17 = (bf16[16,128,128]{2,1,0:T(8,128)(2,1)S(1)}, bf16[16,128,128]{2,1,0:T(8,128)(2,1)S(1)}, u32[]{:S(2)}, u32[]{:S(2)}) collective-permute-start(bf16[16,128,128]{2,1,0:T(8,128)(2,1)S(1)} %merge.8.after_ref.mine_ref), channel_id=1, source_target_pairs={{8,16},{16,8},{9,17},{17,9},{10,18},{18,10},{11,19},{19,11},{12,20... | collective-permute-start | bytes 1572872 | tf_op jit(solution)/shard_map/ppermute | solution.py:599
  98.8 17.1 %collective-permute-start.15 = (bf16[16,128,128]{2,1,0:T(8,128)(2,1)}, bf16[16,128,128]{2,1,0:T(8,128)(2,1)S(1)}, u32[]{:S(2)}, u32[]{:S(2)}) collective-permute-start(bf16[16,128,128]{2,1,0:T(8,128)(2,1)} %get-tuple-element.31.mine_ref), channel_id=1, source_target_pairs={{0,8},{24,16},{1,9},{25,17},{2,10},{26,18},{3,11},{27,19},{4,12},{... | collective-permute-start | bytes 1572872 | tf_op jit(solution)/shard_map/ppermute | solution.py:578
  106.8 1.0 copy-start.4
  107.9 12.0 %collective-permute-start.22 = (bf16[16,128,128]{2,1,0:T(8,128)(2,1)S(1)}, bf16[16,128,128]{2,1,0:T(8,128)(2,1)S(1)}, u32[]{:S(2)}, u32[]{:S(2)}) collective-permute-start(bf16[16,128,128]{2,1,0:T(8,128)(2,1)S(1)} %merge.9.after_ref.mine_ref), channel_id=1, source_target_pairs={{8,16},{16,8},{9,17},{17,9},{10,18},{18,10},{11,19},{19,11},{12,20... | collective-permute-start | bytes 1572872 | tf_op jit(solution)/shard_map/ppermute | solution.py:599
  110.0 12.2 %collective-permute-start.21 = (bf16[16,128,128]{2,1,0:T(8,128)(2,1)S(1)}, bf16[16,128,128]{2,1,0:T(8,128)(2,1)}, u32[]{:S(2)}, u32[]{:S(2)}) collective-permute-start(bf16[16,128,128]{2,1,0:T(8,128)(2,1)S(1)} %merge.10.after_ref.mine_ref), channel_id=1, source_target_pairs={{8,0},{16,24},{9,1},{17,25},{10,2},{18,26},{11,3},{19,27},{12,4},{... | collective-permute-start | bytes 1572872 | tf_op jit(solution)/shard_map/ppermute | solution.py:599
  112.1 13.0 %collective-permute-start.20 = (bf16[16,128,128]{2,1,0:T(8,128)(2,1)S(1)}, bf16[16,128,128]{2,1,0:T(8,128)(2,1)S(1)}, u32[]{:S(2)}, u32[]{:S(2)}) collective-permute-start(bf16[16,128,128]{2,1,0:T(8,128)(2,1)S(1)} %copy-done.2), channel_id=1, source_target_pairs={{0,8},{24,16},{1,9},{25,17},{2,10},{26,18},{3,11},{27,19},{4,12},{... | collective-permute-start | bytes 1572872 | tf_op jit(solution)/shard_map/ppermute | solution.py:578
  115.9 16.1 %collective-permute-start.19 = (bf16[16,128,128]{2,1,0:T(8,128)(2,1)S(1)}, bf16[16,128,128]{2,1,0:T(8,128)(2,1)S(1)}, u32[]{:S(2)}, u32[]{:S(2)}) collective-permute-start(bf16[16,128,128]{2,1,0:T(8,128)(2,1)S(1)} %merge.11.after_ref.mine_ref), channel_id=1, source_target_pairs={{8,16},{16,8},{9,17},{17,9},{10,18},{18,10},{11,19},{19,11},{12,20... | collective-permute-start | bytes 1572872 | tf_op jit(solution)/shard_map/ppermute | solution.py:599
  120.1 12.1 %collective-permute-start.25 = (bf16[16,128,128]{2,1,0:T(8,128)(2,1)S(1)}, bf16[16,128,128]{2,1,0:T(8,128)(2,1)}, u32[]{:S(2)}, u32[]{:S(2)}) collective-permute-start(bf16[16,128,128]{2,1,0:T(8,128)(2,1)S(1)} %merge.12.after_ref.token_ref.mine_ref), channel_id=1, source_target_pairs={{8,0},{16,24},{9,1},{17,25},{10,2},{18,26},{11,3},{19,27},{12,4},{... | collective-permute-start | bytes 1572872 | tf_op jit(solution)/shard_map/ppermute | solution.py:599
  125.3 33.1 %copy-start.1 = (bf16[128,256]{1,0:T(8,128)(2,1)S(1)}, bf16[128,256]{1,0:T(8,128)(2,1)}, u32[]{:S(2)}) copy-start(bf16[128,256]{1,0:T(8,128)(2,1)} %constant.19.clone.refs_2_) | copy-start | bytes 196612
  125.3 33.1 %copy-start.5 = (s32[1,64]{1,0:T(1,128)S(1)}, s32[1,64]{1,0:T(1,128)}, u32[]{:S(2)}) copy-start(s32[1,64]{1,0:T(1,128)} %refs_1_.7) | copy-start | bytes 772
  125.3 18.9 %collective-permute-start.24 = (bf16[16,128,128]{2,1,0:T(8,128)(2,1)S(1)}, bf16[16,128,128]{2,1,0:T(8,128)(2,1)S(1)}, u32[]{:S(2)}, u32[]{:S(2)}) collective-permute-start(bf16[16,128,128]{2,1,0:T(8,128)(2,1)S(1)} %merge.13.after_ref.mine_ref), channel_id=1, source_target_pairs={{8,16},{16,8},{9,17},{17,9},{10,18},{18,10},{11,19},{19,11},{12,20... | collective-permute-start | bytes 1572872 | tf_op jit(solution)/shard_map/ppermute | solution.py:599
  131.7 14.2 %collective-permute-start.26 = (bf16[16,128,128]{2,1,0:T(8,128)(2,1)S(1)}, bf16[16,128,128]{2,1,0:T(8,128)(2,1)S(1)}, u32[]{:S(2)}, u32[]{:S(2)}) collective-permute-start(bf16[16,128,128]{2,1,0:T(8,128)(2,1)S(1)} %pick.4.after_ref), channel_id=1, source_target_pairs={{0,6},{1,7},{2,4},{3,5},{4,2},{5,3},{6,0},{7,1},{8,14},{9,15},{10,... | collective-permute-start | bytes 1572872 | tf_op jit(solution)/shard_map/ppermute | solution.py:603
  133.4 24.9 %collective-permute-start.30 = (bf16[16,128,128]{2,1,0:T(8,128)(2,1)S(1)}, bf16[16,128,128]{2,1,0:T(8,128)(2,1)S(1)}, u32[]{:S(2)}, u32[]{:S(2)}) collective-permute-start(bf16[16,128,128]{2,1,0:T(8,128)(2,1)S(1)} %pick.5.after_ref), channel_id=1, source_target_pairs={{0,2},{1,3},{2,0},{3,1},{4,6},{5,7},{6,4},{7,5},{8,10},{9,11},{10,... | collective-permute-start | bytes 1572872 | tf_op jit(solution)/shard_map/ppermute | solution.py:603
  140.9 20.8 %collective-permute-start.23 = (bf16[16,128,128]{2,1,0:T(8,128)(2,1)S(1)}, bf16[16,128,128]{2,1,0:T(8,128)(2,1)S(1)}, u32[]{:S(2)}, u32[]{:S(2)}) collective-permute-start(bf16[16,128,128]{2,1,0:T(8,128)(2,1)S(1)} %merge.14.after_ref.token_ref.mine_ref), channel_id=1, source_target_pairs={{8,0},{16,24},{9,1},{17,25},{10,2},{18,26},{11,3},{19,27},{12,4},{... | collective-permute-start | bytes 1572872 | tf_op jit(solution)/shard_map/ppermute | solution.py:599
  144.3 21.2 %collective-permute-start.29 = (bf16[16,128,128]{2,1,0:T(8,128)(2,1)S(1)}, bf16[16,128,128]{2,1,0:T(8,128)(2,1)S(1)}, u32[]{:S(2)}, u32[]{:S(2)}) collective-permute-start(bf16[16,128,128]{2,1,0:T(8,128)(2,1)S(1)} %merge.15.after_ref.mine_ref), channel_id=1, source_target_pairs={{8,0},{16,24},{9,1},{17,25},{10,2},{18,26},{11,3},{19,27},{12,4},{... | collective-permute-start | bytes 1572872 | tf_op jit(solution)/shard_map/ppermute | solution.py:599
  145.9 12.5 %collective-permute-start.27 = (bf16[8,128,128]{2,1,0:T(8,128)(2,1)S(1)}, bf16[8,128,128]{2,1,0:T(8,128)(2,1)S(1)}, u32[]{:S(2)}, u32[]{:S(2)}) collective-permute-start(bf16[8,128,128]{2,1,0:T(8,128)(2,1)S(1)} %slice.47), channel_id=1, source_target_pairs={{0,1},{1,0},{2,3},{3,2},{4,5},{5,4},{6,7},{7,6},{8,9},{9,8},{10,11... | collective-permute-start | bytes 786440 | tf_op jit(solution)/shard_map/ppermute | solution.py:603
  158.3 3.9 %collective-permute-start.31 = (bf16[8,128,128]{2,1,0:T(8,128)(2,1)S(1)}, bf16[8,128,128]{2,1,0:T(8,128)(2,1)S(1)}, u32[]{:S(2)}, u32[]{:S(2)}) collective-permute-start(bf16[8,128,128]{2,1,0:T(8,128)(2,1)S(1)} %slice.48), channel_id=1, source_target_pairs={{0,1},{1,0},{2,3},{3,2},{4,5},{5,4},{6,7},{7,6},{8,9},{9,8},{10,11... | collective-permute-start | bytes 786440 | tf_op jit(solution)/shard_map/ppermute | solution.py:603
  161.9 13.1 %collective-permute-start.28 = (bf16[16,128,128]{2,1,0:T(8,128)(2,1)S(1)}, bf16[16,128,128]{2,1,0:T(8,128)(2,1)S(1)}, u32[]{:S(2)}, u32[]{:S(2)}) collective-permute-start(bf16[16,128,128]{2,1,0:T(8,128)(2,1)S(1)} %pick.6.after_ref), channel_id=1, source_target_pairs={{0,4},{1,5},{2,6},{3,7},{4,0},{5,1},{6,2},{7,3},{8,12},{9,13},{10,... | collective-permute-start | bytes 1572872 | tf_op jit(solution)/shard_map/ppermute | solution.py:603
  165.5 10.9 %copy-start.12 = (bf16[32,128,128]{2,1,0:T(8,128)(2,1)S(1)}, bf16[32,128,128]{2,1,0:T(8,128)(2,1)}, u32[]{:S(2)}) copy-start(bf16[32,128,128]{2,1,0:T(8,128)(2,1)} %get-tuple-element.30) | copy-start | bytes 3145732
  165.7 1.6 collective-permute-start.32
  175.0 2.9 %collective-permute-start.33 = (bf16[8,128,128]{2,1,0:T(8,128)(2,1)S(1)}, bf16[8,128,128]{2,1,0:T(8,128)(2,1)S(1)}, u32[]{:S(2)}, u32[]{:S(2)}) collective-permute-start(bf16[8,128,128]{2,1,0:T(8,128)(2,1)S(1)} %second_half.1), channel_id=1, source_target_pairs={{0,1},{1,0},{2,3},{3,2},{4,5},{5,4},{6,7},{7,6},{8,9},{9,8},{10,11... | collective-permute-start | bytes 786440 | tf_op jit(solution)/shard_map/ppermute | solution.py:603
